TPU v7x, 512 devices: a whole 4x8x8 slice. The times are simulated.
512 devices in a mesh: seq: 32 (over y, z_hi, core), row: 4 (over x), col: 4 (over z_lo).
Axes of the slice: x: 4, y: 8, z: 8 (z_hi: 2, z_lo: 4; z = z_hi * 4 + z_lo), core: 2. Of those that a mesh axis runs over, the one named last changes fastest.
Arguments:
- query_rows: bfloat16 [5120, 48, 128], P('seq', ('row', 'col')), may hold values from -6 to 6
- key_rows: bfloat16 [5120, 48, 128], P('seq', ('row', 'col')), may hold values from -6 to 6
- value_rows: bfloat16 [5120, 48, 128], P('seq', ('row', 'col')), may hold values from -6 to 6
- out_weight: bfloat16 [48, 128, 6144], P('row', 'seq', 'col'), may hold values from -0.3125 to 0.3125
- out_bias: float32 [6144], P('col'), may hold values from -3 to 3
Outputs:
- output: bfloat16 [5120, 6144], P(('seq', 'row'), 'col')
All inputs are finite; a program needn't handle non-finite values.
Results may differ from a plain program's by a relative error of at most 0.015.
Values may be sent and summed in bfloat16 or wider, within the bound.
No kernel may reach another device: no remote copies, remote signals or barrier semaphores. Data moves between devices by JAX's collectives and lax.ppermute only.
A program may use at most 64 MiB of HBM per device.

v0:
```python
import jax
import jax.numpy as jnp
from jax import lax
from jax.sharding import PartitionSpec as P


def attend(running, queries, query_pos, key_block, value_block, key_pos, score_scale):
    allowed = key_pos[None, :] <= query_pos[:, None]
    scores = (
        jnp.einsum("qhd,khd->qhk", queries, key_block, preferred_element_type=jnp.float32)
        * score_scale
    )
    scores = jnp.where(allowed[:, None, :], scores, -1e30)
    old_max, old_total, old_sum = running
    new_max = jnp.maximum(old_max, jnp.max(scores, axis=2))
    attn_weights = jnp.where(allowed[:, None, :], jnp.exp(scores - new_max[:, :, None]), 0.0)
    new_total = jnp.sum(attn_weights, axis=2)
    new_sum = jnp.einsum(
        "qhk,khd->qhd",
        attn_weights.astype(jnp.bfloat16),
        value_block,
        preferred_element_type=jnp.float32,
    )
    return (new_max, new_total, new_sum)


def on_device(query_rows, key_rows, value_rows, out_weight, out_bias):
    local_rows, head_count, head_size = query_rows.shape
    score_scale = head_size ** (-0.5)
    seq_index = lax.axis_index("seq")

    def place(source, local):
        return source * local_rows + local

    query_pos = place(seq_index, jnp.arange(local_rows))
    initial = (
        jnp.full((local_rows, head_count), -1e30, jnp.float32),
        jnp.zeros((local_rows, head_count), jnp.float32),
        jnp.zeros((local_rows, head_count, head_size), jnp.float32),
    )
    key_block = lax.all_gather(key_rows, "seq", axis=0, tiled=True)
    value_block = lax.all_gather(value_rows, "seq", axis=0, tiled=True)
    gathered = jnp.arange(key_block.shape[0])
    key_pos = place(gathered // local_rows, gathered % local_rows)
    running = attend(initial, query_rows, query_pos, key_block, value_block, key_pos, score_scale)
    row_total = running[1]
    row_sum = running[2]
    attended = (row_sum / row_total[:, :, None]).astype(jnp.bfloat16)
    row_block = lax.all_gather(attended, "col", axis=1, tiled=True)
    projected = jnp.einsum(
        "qhd,hdo->qo",
        row_block,
        lax.all_gather(out_weight, "seq", axis=1, tiled=True),
        preferred_element_type=jnp.float32,
    )
    summed = lax.psum_scatter(
        projected.astype(jnp.bfloat16), "row", scatter_dimension=0, tiled=True
    ).astype(jnp.float32)
    return (summed + out_bias[None, :]).astype(jnp.bfloat16)


def solution(mesh):
    in_specs = (
        P("seq", ("row", "col"), None),
        P("seq", ("row", "col"), None),
        P("seq", ("row", "col"), None),
        P("row", "seq", "col"),
        P("col"),
    )
    out_specs = P(("seq", "row"), "col")
    return jax.shard_map(
        on_device, mesh=mesh, in_specs=in_specs, out_specs=out_specs, check_vma=False
    )
```

profile of v0, /device:TPU:1, one launch (start us, length us, event | category | flops | bytes accessed | tf_op | source)
XLA Modules:
  0.0 379.4 jit_solution(10510141556917201237)
XLA Ops:
  6.5 0.0 copy-start
  6.5 0.0 all-gather.4.cloned.1.call-start
  6.5 0.7 all-gather.4.cloned.1.call-update
  7.3 0.0 all-gather.6.cloned.1.call-start
  7.3 0.7 all-gather.6.cloned.1.call-update
  8.0 0.0 all-gather.8.cloned.1.call-start
  8.1 1.6 copy.6
  9.7 0.0 all-gather.8.cloned.1.call-update
  9.7 0.0 reduce-scatter.2.cloned.1.call-start
  9.8 0.5 broadcast_compare_fusion
  10.3 112.0 %all-gather.4.cloned.1.call-done = bf16[5120,3,128]{2,0,1:T(8,128)(2,1)} async-done(((bf16[160,3,128]{2,0,1:T(8,128)(2,1)}), bf16[5120,3,128]{2,0,1:T(8,128)(2,1)}) %all-gather.4.cloned.1.call-update) | async-done | bytes 3932176 | tf_op jit(solution)/shard_map/all_gather | solution.py:41
  122.3 0.0 copy-done
  122.3 4.2 %fusion = (f32[160,3]{0,1:T(4,128)S(1)}, f32[3,5120,160]{1,2,0:T(8,128)S(1)}) fusion(pred[160,5120]{1,0:T(8,128)(4,1)S(1)} %broadcast_compare_fusion, bf16[5120,3,128]{2,0,1:T(8,128)(2,1)} %all-gather.4.cloned.1.call-done, bf16[160,3,128]{2,0,1:T(8,128)(2,1)S(1)} %copy-done), kind=kOutput, calls=%fused_computation.2 | convolution fusion | flops 636517888 | bytes 14706560 | tf_op jit(solution)/shard_map/qhd,khd->qhk/dot_general | solution.py:10
  126.5 0.0 copy-start.1
  126.5 3.8 copy-done.1
  130.3 3.1 fusion.1
  133.4 0.0 copy-start.2
  133.4 91.3 %all-gather.6.cloned.1.call-done = bf16[5120,3,128]{2,0,1:T(8,128)(2,1)} async-done(((bf16[160,3,128]{2,0,1:T(8,128)(2,1)}), bf16[5120,3,128]{2,0,1:T(8,128)(2,1)}) %all-gather.6.cloned.1.call-update) | async-done | bytes 3932176 | tf_op jit(solution)/shard_map/all_gather | solution.py:42
  224.7 7.8 %fusion.20 = bf16[160,3,128]{2,0,1:T(8,128)(2,1)S(1)} fusion(bf16[5120,3,128]{2,0,1:T(8,128)(2,1)} %all-gather.6.cloned.1.call-done, f32[3,5120,160]{1,2,0:T(8,128)} %copy-done.1, f32[160,3]{0,1:T(4,128)S(1)} %broadcast_maximum_fusion, pred[160,5120]{1,0:T(8,128)(4,1)S(1)} %broadcast_compare_fusion, f32[160,3]{0,1:T(4,128)S(1)} %fusion.1), kind=kOutput, calls=%fused_computation.14 | convolution fusion | flops 641556480 | bytes 14708480 | tf_op jit(solution)/shard_map/qhk,khd->qhd/dot_general | solution.py:18
  232.5 15.7 %all_gather.14 = bf16[160,12,128]{2,0,1:T(8,128)(2,1)S(1)} all-gather(bf16[160,3,128]{2,0,1:T(8,128)(2,1)S(1)} %fusion.20), channel_id=1, replica_groups=mesh['seq'=32,'row'=4,'col'=4] {'col'}, dimensions={1}, use_global_device_ids=true | all-gather | bytes 614400 | tf_op jit(solution)/shard_map/all_gather | solution.py:49
  248.2 95.6 %all-gather.8.cloned.1.call-done = bf16[12,128,1536]{2,0,1:T(8,128)(2,1)} async-done(((bf16[12,4,1536]{2,0,1:T(8,128)(2,1)}), bf16[12,128,1536]{2,0,1:T(8,128)(2,1)}) %all-gather.8.cloned.1.call-update) | async-done | bytes 4718608 | tf_op jit(solution)/shard_map/all_gather | solution.py:53
  343.8 8.9 %fusion.11 = bf16[160,1536]{1,0:T(8,128)(2,1)} fusion(bf16[160,12,128]{2,0,1:T(8,128)(2,1)S(1)} %all_gather.14, bf16[12,128,1536]{2,0,1:T(8,128)(2,1)} %all-gather.8.cloned.1.call-done), kind=kOutput, calls=%fused_computation.10 | convolution fusion | flops 755220480 | bytes 5701632 | tf_op jit(solution)/shard_map/qhd,hdo->qo/dot_general | solution.py:50
  352.7 0.0 reduce-scatter.2.cloned.1.call-update
  352.8 18.5 %reduce-scatter.2.cloned.1.call-done = bf16[40,1536]{1,0:T(8,128)(2,1)} async-done(((bf16[160,1536]{1,0:T(8,128)(2,1)}), bf16[40,1536]{1,0:T(8,128)(2,1)}) %reduce-scatter.2.cloned.1.call-update) | async-done | bytes 122896 | tf_op jit(solution)/shard_map/reduce_scatter | solution.py:56
  371.3 0.0 copy-done.2
  371.3 1.6 add_convert_fusion
  (3 shorter events, 0.0 us)
Async XLA Ops:
  6.5 115.8 %copy-start = (bf16[160,3,128]{2,0,1:T(8,128)(2,1)S(1)}, bf16[160,3,128]{2,0,1:T(8,128)(2,1)}, u32[]{:S(2)}) copy-start(bf16[160,3,128]{2,0,1:T(8,128)(2,1)} %param.5) | copy-start | bytes 368644
  6.5 115.7 %all-gather.4.cloned.1.call-start = ((), (), s32[]{:S(2)}) async-start(), calls=%async_computation.1 | async-start | bytes 4055040 | tf_op jit(solution)/shard_map/all_gather | solution.py:41
  7.3 217.5 %all-gather.6.cloned.1.call-start = ((), (), s32[]{:S(2)}) async-start(), calls=%async_computation.2 | async-start | bytes 4055040 | tf_op jit(solution)/shard_map/all_gather | solution.py:42
  8.0 335.8 %all-gather.8.cloned.1.call-start = ((), (), s32[]{:S(2)}) async-start(), calls=%async_computation.3 | async-start | bytes 6488064 | tf_op jit(solution)/shard_map/all_gather | solution.py:53
  9.7 361.6 %reduce-scatter.2.cloned.1.call-start = ((), (), s32[]{:S(2)}) async-start(), calls=%async_computation.4 | async-start | bytes 614400 | tf_op jit(solution)/shard_map/reduce_scatter | solution.py:56
  126.5 3.8 copy-start.1
  133.4 237.9 %copy-start.2 = (f32[1536]{0:T(1024)S(1)}, f32[1536]{0:T(1024)}, u32[]{:S(2)}) copy-start(f32[1536]{0:T(1024)} %param.9) | copy-start | bytes 18436
Sparse Core Ops, SparseCore 0:
  10.8 111.4 all-gather.3
  125.7 98.9 all-gather.5
  228.0 115.7 all-gather.7
  352.9 18.3 reduce-scatter.1
where the time goes:
time: 380 us; the launch traced here: 379 us
  waiting for transfers between devices  319 us (84%)
  matrix products  20.9 us (6%)
  blocking collectives  15.7 us (4%)
  between operations  13.2 us (3%)
  local copies, waits for them, and re-layouts  5.38 us (1%)
  other arithmetic  5.2 us (1%)
    all_gather x1, waiting for transfers between devices, on_device(): key_block = lax.all_gather(key_rows, 'seq', axis=0, tiled=True)  112 us
    all_gather x1, waiting for transfers between devices, on_device(): lax.all_gather(out_weight, 'seq', axis=1, tiled=True)  95.6 us
    all_gather x1, waiting for transfers between devices, on_device(): value_block = lax.all_gather(value_rows, 'seq', axis=0, tiled=True)  91.3 us
    reduce_scatter x1, waiting for transfers between devices, on_device(): lax.psum_scatter(projected.astype(jnp.bfloat16), 'row', scatter_dimension...  18.5 us
    all_gather x1, blocking collectives, on_device(): row_block = lax.all_gather(attended, 'col', axis=1, tiled=True)  15.7 us
    dot_general x1, matrix products, on_device(): jnp.einsum('qhd,hdo->qo', row_block, lax.all_gather(out_weight, 'seq', ax...  8.88 us
    dot_general x1, matrix products, attend(): jnp.einsum('qhk,khd->qhd', attn_weights.astype(jnp.bfloat16), value_block...  7.77 us
  transfers between devices with their start and end apart: 4, of which 4 were waited for; matrix products, arithmetic and copies ran while one was open for 5% of the time, Pallas kernels for 0%

commit v1 on v0

v1 whole, which is shorter than its diff:
```python
import functools
import math

import jax
import jax.numpy as jnp
from jax import lax
from jax.experimental import pallas as pl
from jax.experimental.pallas import tpu as pltpu
from jax.sharding import Mesh
from jax.sharding import PartitionSpec as P

LOW = -1e30
VMEM = pl.BlockSpec(memory_space=pltpu.VMEM)
SMEM = pl.BlockSpec(memory_space=pltpu.SMEM)
PARAMS = pltpu.CompilerParams(vmem_limit_bytes=48 * 1024 * 1024)


def split3(x):
    high = x.astype(jnp.bfloat16).astype(jnp.float32)
    rest = x - high
    mid = rest.astype(jnp.bfloat16).astype(jnp.float32)
    return high, mid, rest - mid


def put_logs(logs, rows):
    lane = lax.broadcasted_iota(jnp.int32, (rows, 128), 1)
    plane = jnp.zeros((rows, 128), jnp.float32)
    for head, value in enumerate(logs):
        for part, piece in enumerate(split3(value)):
            plane = jnp.where(lane == 3 * head + part, piece, plane)
    return plane.astype(jnp.bfloat16)


def get_log(plane, head):
    wide = plane.astype(jnp.float32)
    at = 3 * head
    return wide[:, at : at + 1] + wide[:, at + 1 : at + 2] + wide[:, at + 2 : at + 3]


def attend_kernel(
    rows, heads, ring, scale2, idx_ref, qo_ref, qx_ref, own_ref, b1_ref, b2_ref, b3_ref, b4_ref,
    keep_ref, send_ref, m_ref, l_ref, acc_ref, log_ref,
):
    y, zh, c = idx_ref[0], idx_ref[1], idx_ref[2]
    all_rows = 4 * rows
    local = lax.broadcasted_iota(jnp.int32, (rows, 1), 0)
    query_pos = jnp.concatenate(
        [((zh if z == 0 else 1 - zh) * 2 + cc) * rows + local for z in range(2) for cc in range(2)], axis=0
    )
    key_pos = (zh * 2 + c) * rows + lax.broadcasted_iota(jnp.int32, (1, rows), 1)

    def step(h, query, keys, values, masked):
        scores = lax.dot_general(
            query, keys, (((1,), (1,)), ((), ())), preferred_element_type=jnp.float32
        )
        scores = scores * scale2
        if masked:
            scores = jnp.where(key_pos <= query_pos, scores, LOW)
        old = m_ref[...]
        new = jnp.maximum(old, jnp.max(scores, axis=1, keepdims=True))
        weights = jnp.exp2(scores - new)
        if masked:
            weights = jnp.where(key_pos <= query_pos, weights, 0.0)
        fade = jnp.exp2(old - new)
        m_ref[...] = new
        l_ref[...] = l_ref[...] * fade + jnp.sum(weights, axis=1, keepdims=True)
        acc_ref[...] = acc_ref[...] * fade + jnp.dot(
            weights.astype(jnp.bfloat16), values, preferred_element_type=jnp.float32
        )

    def head(h, carry):
        query = jnp.concatenate([qo_ref[0, h], qo_ref[1, h], qx_ref[0, h], qx_ref[1, h]], axis=0)
        m_ref[...] = jnp.full_like(m_ref, LOW)
        l_ref[...] = jnp.zeros_like(l_ref)
        acc_ref[...] = jnp.zeros_like(acc_ref)
        step(h, query, own_ref[0, h], own_ref[1, h], True)
        for distance, block in ((1, b1_ref), (2, b2_ref), (3, b3_ref), (4, b4_ref)):
            source = jnp.where(c == 0, y + ring - distance, y + distance) % ring

            @pl.when(source < y)
            def _():
                if distance < 4:
                    keys = jnp.concatenate([block[0, 0, h], block[1, 0, h]], axis=0)
                    values = jnp.concatenate([block[0, 1, h], block[1, 1, h]], axis=0)
                else:
                    keys, values = block[0, h], block[1, h]
                step(h, query, keys, values, False)

        total = l_ref[...]
        seen = total > 0.0
        safe = jnp.where(seen, total, 1.0)
        low = (acc_ref[...] / safe).astype(jnp.bfloat16)
        log_ref[h] = jnp.where(seen, m_ref[...] + jnp.log2(safe), LOW)
        for z in range(2):
            first, second = low[2 * z * rows : (2 * z + 1) * rows], low[(2 * z + 1) * rows : (2 * z + 2) * rows]
            keep_ref[z, h] = jnp.where(c == 0, first, second)
            send_ref[z, h] = jnp.where(c == 0, second, first)
        return carry

    lax.fori_loop(0, heads, head, 0)
    planes = put_logs([log_ref[h] for h in range(heads)], all_rows)
    for z in range(2):
        first, second = planes[2 * z * rows : (2 * z + 1) * rows], planes[(2 * z + 1) * rows : (2 * z + 2) * rows]
        keep_ref[z, heads] = jnp.where(c == 0, first, second)
        send_ref[z, heads] = jnp.where(c == 0, second, first)


def attend(idx, qo, qx, own, b1, b2, b3, b4, ring):
    _, heads, rows, size = qo.shape
    scale2 = size ** (-0.5) * math.log2(math.e)
    out = jax.ShapeDtypeStruct((2, heads + 1, rows, size), jnp.bfloat16)
    keys = 8 * rows
    return pl.pallas_call(
        functools.partial(attend_kernel, rows, heads, ring, scale2),
        out_shape=(out, out),
        in_specs=[SMEM] + [VMEM] * 7,
        out_specs=(VMEM, VMEM),
        scratch_shapes=[
            pltpu.VMEM((4 * rows, 1), jnp.float32),
            pltpu.VMEM((4 * rows, 1), jnp.float32),
            pltpu.VMEM((4 * rows, size), jnp.float32),
            pltpu.VMEM((heads, 4 * rows, 1), jnp.float32),
        ],
        compiler_params=PARAMS,
        cost_estimate=pl.CostEstimate(
            flops=4 * 4 * rows * keys * size * heads, bytes_accessed=4 << 20, transcendentals=4 * rows * keys * heads
        ),
        name="attend",
    )(idx, qo, qx, own, b1, b2, b3, b4)


def merge(first, second, heads):
    values, logs = [], []
    for h in range(heads):
        log_a, log_b = get_log(first[heads], h), get_log(second[heads], h)
        top = jnp.maximum(log_a, log_b)
        a, b = jnp.exp2(log_a - top), jnp.exp2(log_b - top)
        total = a + b
        value = (first[h].astype(jnp.float32) * a + second[h].astype(jnp.float32) * b) / total
        values.append(value.astype(jnp.bfloat16))
        logs.append(top + jnp.log2(total))
    return values, logs


def merge_core_kernel(heads, a_ref, b_ref, keep_ref, send_ref):
    for z, out_ref in enumerate((keep_ref, send_ref)):
        values, logs = merge(a_ref[z], b_ref[z], heads)
        for h in range(heads):
            out_ref[h] = values[h]
        out_ref[heads] = put_logs(logs, a_ref.shape[2])


def merge_far_kernel(heads, a_ref, b_ref, out_ref):
    values, _ = merge(a_ref[...], b_ref[...], heads)
    for h in range(heads):
        out_ref[h] = values[h]


def project_kernel(att_ref, w_ref, out_ref):
    cores, cols, heads, rows, size = att_ref.shape
    total = None
    for col in range(cols):
        for h in range(heads):
            left = jnp.concatenate([att_ref[core, col, h] for core in range(cores)], axis=0)
            right = w_ref[:, col * heads + h].reshape(size, w_ref.shape[3])
            term = jnp.dot(left, right, preferred_element_type=jnp.float32)
            total = term if total is None else total + term
    low = total.astype(jnp.bfloat16)
    for core in range(cores):
        out_ref[core] = low[core * rows : (core + 1) * rows]


def on_device(query_rows, key_rows, value_rows, out_weight, out_bias):
    rows, heads, size = query_rows.shape
    ring = lax.axis_size("y")
    y, zh, c = lax.axis_index("y"), lax.axis_index("zh"), lax.axis_index("c")
    idx = jnp.stack([y, zh, c]).astype(jnp.int32)
    swap = [(0, 1), (1, 0)]
    both = []
    for at in range(ring):
        both.append((2 * at, 2 * ((at + 1) % ring)))
        both.append((2 * at + 1, 2 * ((at - 1) % ring) + 1))

    def onward(block):
        return lax.ppermute(block, ("y", "c"), both)

    own = jnp.stack([jnp.swapaxes(key_rows, 0, 1), jnp.swapaxes(value_rows, 0, 1)])
    chip = lax.all_gather(own, "c", axis=0)
    b1 = onward(chip)
    qo = lax.all_gather(jnp.swapaxes(query_rows, 0, 1), "c", axis=0)
    qx = lax.ppermute(qo, "zh", swap)
    b2 = onward(b1)

    w_heads, w_deep, w_wide = out_weight.shape
    half = w_wide // 2
    w_core = lax.all_to_all(out_weight.reshape(w_heads, w_deep, 2, half), "c", 2, 0)
    w_far = lax.ppermute(w_core, "zh", swap)
    w_both = jnp.where(zh == 0, jnp.stack([w_core, w_far]), jnp.stack([w_far, w_core]))
    w_both = jnp.transpose(w_both, (2, 0, 1, 3, 4)).reshape(w_heads, 4 * w_deep, half)
    w_all = lax.all_gather(w_both, "y", axis=0)

    b3 = onward(b2)
    b4 = onward(lax.dynamic_index_in_dim(b3, c, 0, keepdims=False))
    keep, send = attend(idx, qo, qx, own, b1, b2, b3, b4, ring)
    other = lax.ppermute(send, "c", swap)
    part = jax.ShapeDtypeStruct((heads + 1, rows, size), jnp.bfloat16)
    keep, send = pl.pallas_call(
        functools.partial(merge_core_kernel, heads),
        out_shape=(part, part),
        in_specs=[VMEM, VMEM],
        out_specs=(VMEM, VMEM),
        compiler_params=PARAMS,
        name="merge_core",
    )(keep, other)
    other = lax.ppermute(send, "zh", swap)
    attended = pl.pallas_call(
        functools.partial(merge_far_kernel, heads),
        out_shape=jax.ShapeDtypeStruct((heads, rows, size), jnp.bfloat16),
        in_specs=[VMEM, VMEM],
        out_specs=VMEM,
        compiler_params=PARAMS,
        name="merge_far",
    )(keep, other)
    attended = lax.all_gather(attended, "col", axis=0)
    attended = lax.all_gather(attended, "c", axis=0)
    projected = pl.pallas_call(
        project_kernel,
        out_shape=jax.ShapeDtypeStruct((2, rows, half), jnp.bfloat16),
        in_specs=[VMEM, VMEM],
        out_specs=VMEM,
        compiler_params=PARAMS,
        name="project",
    )(attended, w_all)
    parts = lax.axis_size("row")
    pieces = projected.reshape(2 * parts, rows // parts, half)
    pieces = lax.all_to_all(pieces, ("c", "row"), 0, 0, tiled=True)
    pieces = pieces.reshape(2, parts, rows // parts, half)
    summed = jnp.sum(pieces.astype(jnp.float32), axis=1)
    summed = jnp.swapaxes(summed, 0, 1).reshape(rows // parts, w_wide)
    return (summed + out_bias[None, :]).astype(jnp.bfloat16)


def solution(mesh):
    shape = mesh.devices.shape
    fine = Mesh(mesh.devices.reshape((shape[0] // 4, 2, 2) + shape[1:]), ("y", "zh", "c", "row", "col"))
    seq = ("y", "zh", "c")
    in_specs = (
        P(seq, ("row", "col"), None),
        P(seq, ("row", "col"), None),
        P(seq, ("row", "col"), None),
        P("row", seq, "col"),
        P("col"),
    )
    out_specs = P(seq + ("row",), "col")
    return jax.shard_map(
        on_device, mesh=fine, in_specs=in_specs, out_specs=out_specs, check_vma=False
    )
```

time: 380 us -> 181 us (0.48)
  the two profiles are of different devices: /device:TPU:1 before, /device:TPU:57 now
where the time goes in v1:
time: 181 us; the launch traced here: 180 us
  blocking collectives  50.2 us (28%)
  waiting for transfers between devices  43.4 us (24%)
  starting transfers between devices  38.9 us (21%)
  Pallas kernels  29.5 us (16%)
  between operations  13.6 us (8%)
  local copies, waits for them, and re-layouts  3.69 us (2%)
    ppermute x4, waiting for transfers between devices, onward(): return lax.ppermute(block, ('y', 'c'), both)  30.8 us
    pallas_call x1, Pallas kernels, attend(): pl.pallas_call(functools.partial(attend_kernel, rows, heads, ring, scale2...  26.4 us
    all_gather x1, blocking collectives, on_device(): attended = lax.all_gather(attended, 'col', axis=0)  16 us
    all_to_all x1, blocking collectives, on_device(): pieces = lax.all_to_all(pieces, ('c', 'row'), 0, 0, tiled=True)  13.6 us
    ppermute x1, starting transfers between devices, on_device(): w_far = lax.ppermute(w_core, 'zh', swap)  10.6 us
    ppermute x4, starting transfers between devices, onward(): return lax.ppermute(block, ('y', 'c'), both)  8.84 us
    ppermute x1, starting transfers between devices, on_device(): other = lax.ppermute(send, 'zh', swap)  8.77 us
    ppermute x1, starting transfers between devices, on_device(): qx = lax.ppermute(qo, 'zh', swap)  8.72 us
  transfers between devices with their start and end apart: 9, of which 8 were waited for; matrix products, arithmetic and copies ran while one was open for 0% of the time, Pallas kernels for 15%

profile of v1, /device:TPU:57, one launch (start us, length us, event | category | flops | bytes accessed | tf_op | source)
XLA Modules:
  0.0 180.3 jit_solution(3755506503252740281)
XLA Ops:
  6.5 0.0 copy-start.3
  6.5 0.0 copy-start.2
  6.5 0.0 copy-start.1
  6.5 0.0 all-gather.6.cloned.1.call-start
  6.5 1.0 broadcast_in_dim_reshape.3
  7.6 0.1 copy.7
  7.6 4.1 %all_to_all.20 = bf16[1,12,4,2,768]{4,2,1,0,3:T(4,128)(2,1)S(1)} all-to-all(bf16[1,12,4,2,768]{4,2,1,0,3:T(4,128)(2,1)S(1)} %copy.7), channel_id=1, replica_groups=mesh['y'=8,'zh'=2,'c'=2,'row'=4,'col'=4] {'c'}, dimensions={3} | all-to-all | bytes 294912 | tf_op jit(solution)/shard_map/all_to_all | solution.py:196
  11.8 10.6 %collective-permute-start.7 = (bf16[2,12,4,768]{3,2,1,0:T(4,128)(2,1)S(1)}, bf16[2,12,4,768]{3,2,1,0:T(4,128)(2,1)S(1)}, u32[]{:S(2)}, u32[]{:S(2)}) collective-permute-start(bf16[2,12,4,768]{3,2,1,0:T(4,128)(2,1)S(1)} %bitcast.40), channel_id=1, source_target_pairs={{0,32},{32,0},{1,33},{33,1},{2,34},{34,2},{3,35},{35,3},{4,36},{36... | collective-permute-start | bytes 442376 | tf_op jit(solution)/shard_map/ppermute | solution.py:197
  22.4 3.9 %collective-permute-done.7 = bf16[2,12,4,768]{3,2,1,0:T(4,128)(2,1)S(1)} collective-permute-done((bf16[2,12,4,768]{3,2,1,0:T(4,128)(2,1)S(1)}, bf16[2,12,4,768]{3,2,1,0:T(4,128)(2,1)S(1)}, u32[]{:S(2)}, u32[]{:S(2)}) %collective-permute-start.7) | collective-permute-done | bytes 147488 | tf_op jit(solution)/shard_map/ppermute | solution.py:197
  26.3 0.2 fusion
  26.5 0.1 copy.8
  26.7 0.8 all_gather_reshape.3
  27.5 0.0 all-gather.6.cloned.1.call-update
  27.5 0.0 copy-done.3
  27.5 0.0 copy-done.2
  27.5 2.8 %all-gather.1 = bf16[4,3,160,128]{3,2,1,0:T(8,128)(2,1)S(1)} all-gather(bf16[2,3,160,128]{3,2,1,0:T(8,128)(2,1)S(1)} %pad_maximum_fusion.own_ref), channel_id=3, replica_groups=mesh['y'=8,'zh'=2,'c'=2,'row'=4,'col'=4] {'c'}, dimensions={0}, use_global_device_ids=true | all-gather | bytes 737280 | tf_op jit(solution)/shard_map/all_gather | solution.py:188
  30.3 3.0 %collective-permute-start.1 = (bf16[2,2,3,160,128]{4,3,2,1,0:T(8,128)(2,1)S(1)}, bf16[2,2,3,160,128]{4,3,2,1,0:T(8,128)(2,1)S(1)}, u32[]{:S(2)}, u32[]{:S(2)}) collective-permute-start(bf16[2,2,3,160,128]{4,3,2,1,0:T(8,128)(2,1)S(1)} %bitcast.42), channel_id=1, source_target_pairs={{0,64},{16,464},{64,128},{80,16},{128,192},{144,80},{192,256},{208... | collective-permute-start | bytes 1474568 | tf_op jit(solution)/shard_map/ppermute | solution.py:185
  33.3 7.8 %collective-permute-done.1.b1_ref = bf16[2,2,3,160,128]{4,3,2,1,0:T(8,128)(2,1)S(1)} collective-permute-done((bf16[2,2,3,160,128]{4,3,2,1,0:T(8,128)(2,1)S(1)}, bf16[2,2,3,160,128]{4,3,2,1,0:T(8,128)(2,1)S(1)}, u32[]{:S(2)}, u32[]{:S(2)}) %collective-permute-start.1) | collective-permute-done | bytes 491552 | tf_op jit(solution)/shard_map/ppermute | solution.py:185
  41.1 2.0 %collective-permute-start.2 = (bf16[2,2,3,160,128]{4,3,2,1,0:T(8,128)(2,1)S(1)}, bf16[2,2,3,160,128]{4,3,2,1,0:T(8,128)(2,1)S(1)}, u32[]{:S(2)}, u32[]{:S(2)}) collective-permute-start(bf16[2,2,3,160,128]{4,3,2,1,0:T(8,128)(2,1)S(1)} %collective-permute-done.1.b1_ref), channel_id=1, source_target_pairs={{0,64},{16,464},{64,128},{80,16},{128,192},{144,80},{192,256},{208... | collective-permute-start | bytes 1474568 | tf_op jit(solution)/shard_map/ppermute | solution.py:185
  43.1 17.6 %collective-permute-done.2.b2_ref = bf16[2,2,3,160,128]{4,3,2,1,0:T(8,128)(2,1)S(1)} collective-permute-done((bf16[2,2,3,160,128]{4,3,2,1,0:T(8,128)(2,1)S(1)}, bf16[2,2,3,160,128]{4,3,2,1,0:T(8,128)(2,1)S(1)}, u32[]{:S(2)}, u32[]{:S(2)}) %collective-permute-start.2) | collective-permute-done | bytes 491552 | tf_op jit(solution)/shard_map/ppermute | solution.py:185
  60.7 1.9 %collective-permute-start.3 = (bf16[2,2,3,160,128]{4,3,2,1,0:T(8,128)(2,1)S(1)}, bf16[2,2,3,160,128]{4,3,2,1,0:T(8,128)(2,1)S(1)}, u32[]{:S(2)}, u32[]{:S(2)}) collective-permute-start(bf16[2,2,3,160,128]{4,3,2,1,0:T(8,128)(2,1)S(1)} %collective-permute-done.2.b2_ref), channel_id=1, source_target_pairs={{0,64},{16,464},{64,128},{80,16},{128,192},{144,80},{192,256},{208... | collective-permute-start | bytes 1474568 | tf_op jit(solution)/shard_map/ppermute | solution.py:185
  62.7 0.0 copy-done.1
  62.7 7.4 %all-gather = bf16[6,160,128]{2,1,0:T(8,128)(2,1)S(1)} all-gather(bf16[3,160,128]{2,1,0:T(8,128)(2,1)S(1)} %bitcast.44), channel_id=2, replica_groups=mesh['y'=8,'zh'=2,'c'=2,'row'=4,'col'=4] {'c'}, dimensions={0}, use_global_device_ids=true | all-gather | bytes 368640 | tf_op jit(solution)/shard_map/all_gather | solution.py:190
  70.1 8.7 %collective-permute-start = (bf16[2,3,160,128]{3,2,1,0:T(8,128)(2,1)S(1)}, bf16[2,3,160,128]{3,2,1,0:T(8,128)(2,1)S(1)}, u32[]{:S(2)}, u32[]{:S(2)}) collective-permute-start(bf16[2,3,160,128]{3,2,1,0:T(8,128)(2,1)S(1)} %bitcast.35), channel_id=1, source_target_pairs={{0,32},{32,0},{1,33},{33,1},{2,34},{34,2},{3,35},{35,3},{4,36},{36... | collective-permute-start | bytes 737288 | tf_op jit(solution)/shard_map/ppermute | solution.py:191
  78.8 2.1 %collective-permute-done.3.b3_ref = bf16[2,2,3,160,128]{4,3,2,1,0:T(8,128)(2,1)S(1)} collective-permute-done((bf16[2,2,3,160,128]{4,3,2,1,0:T(8,128)(2,1)S(1)}, bf16[2,2,3,160,128]{4,3,2,1,0:T(8,128)(2,1)S(1)}, u32[]{:S(2)}, u32[]{:S(2)}) %collective-permute-start.3) | collective-permute-done | bytes 491552 | tf_op jit(solution)/shard_map/ppermute | solution.py:185
  80.9 1.9 %collective-permute-start.4 = (bf16[2,3,160,128]{3,2,1,0:T(8,128)(2,1)S(1)}, bf16[2,3,160,128]{3,2,1,0:T(8,128)(2,1)S(1)}, u32[]{:S(2)}, u32[]{:S(2)}) collective-permute-start(bf16[2,3,160,128]{3,2,1,0:T(8,128)(2,1)S(1)} %dynamic-slice_bitcast_fusion), channel_id=1, source_target_pairs={{0,64},{16,464},{64,128},{80,16},{128,192},{144,80},{192,256},{208... | collective-permute-start | bytes 737288 | tf_op jit(solution)/shard_map/ppermute | solution.py:185
  82.8 0.1 pad_add_fusion.idx_ref
  82.9 2.9 %collective-permute-done.qx_ref = bf16[2,3,160,128]{3,2,1,0:T(8,128)(2,1)S(1)} collective-permute-done((bf16[2,3,160,128]{3,2,1,0:T(8,128)(2,1)S(1)}, bf16[2,3,160,128]{3,2,1,0:T(8,128)(2,1)S(1)}, u32[]{:S(2)}, u32[]{:S(2)}) %collective-permute-start) | collective-permute-done | bytes 245792 | tf_op jit(solution)/shard_map/ppermute | solution.py:191
  85.8 3.3 %collective-permute-done.4.b4_ref = bf16[2,3,160,128]{3,2,1,0:T(8,128)(2,1)S(1)} collective-permute-done((bf16[2,3,160,128]{3,2,1,0:T(8,128)(2,1)S(1)}, bf16[2,3,160,128]{3,2,1,0:T(8,128)(2,1)S(1)}, u32[]{:S(2)}, u32[]{:S(2)}) %collective-permute-start.4) | collective-permute-done | bytes 245792 | tf_op jit(solution)/shard_map/ppermute | solution.py:185
  89.1 26.4 %attend.1 = (bf16[2,4,160,128]{3,2,1,0:T(8,128)(2,1)S(1)}, bf16[2,4,160,128]{3,2,1,0:T(8,128)(2,1)S(1)}) custom-call(s32[3]{0:T(128)S(1)} %pad_add_fusion.idx_ref, bf16[2,3,160,128]{3,2,1,0:T(8,128)(2,1)S(1)} %bitcast.36, bf16[2,3,160,128]{3,2,1,0:T(8,128)(2,1)S(1)} %collective-permute-done.qx_ref, bf16[2,3,160,128]{3,2,1,0:T(8,128)(2,1)S(1)} %pad_maximum_fusion.own_ref, ...), custom_call_target="tpu_custom_call" | custom-call | flops 1258291200 | bytes 4194304 | tf_op jit(solution)/shard_map/attend/pallas_call | solution.py:113
  115.5 1.9 %collective-permute-start.5 = (bf16[2,4,160,128]{3,2,1,0:T(8,128)(2,1)S(1)}, bf16[2,4,160,128]{3,2,1,0:T(8,128)(2,1)S(1)}, u32[]{:S(2)}, u32[]{:S(2)}) collective-permute-start(bf16[2,4,160,128]{3,2,1,0:T(8,128)(2,1)S(1)} %get-tuple-element.10), channel_id=1, source_target_pairs={{0,16},{16,0},{1,17},{17,1},{2,18},{18,2},{3,19},{19,3},{4,20},{20... | collective-permute-start | bytes 983048 | tf_op jit(solution)/shard_map/ppermute | solution.py:205
  117.4 1.6 collective-permute-done.5.b_ref
  119.0 1.0 merge_core.1
  120.1 8.8 %collective-permute-start.6 = (bf16[4,160,128]{2,1,0:T(8,128)(2,1)S(1)}, bf16[4,160,128]{2,1,0:T(8,128)(2,1)S(1)}, u32[]{:S(2)}, u32[]{:S(2)}) collective-permute-start(bf16[4,160,128]{2,1,0:T(8,128)(2,1)S(1)} %get-tuple-element.12), channel_id=1, source_target_pairs={{0,32},{32,0},{1,33},{33,1},{2,34},{34,2},{3,35},{35,3},{4,36},{36... | collective-permute-start | bytes 491528 | tf_op jit(solution)/shard_map/ppermute | solution.py:215
  128.9 4.3 %collective-permute-done.6.b_ref = bf16[4,160,128]{2,1,0:T(8,128)(2,1)S(1)} collective-permute-done((bf16[4,160,128]{2,1,0:T(8,128)(2,1)S(1)}, bf16[4,160,128]{2,1,0:T(8,128)(2,1)S(1)}, u32[]{:S(2)}, u32[]{:S(2)}) %collective-permute-start.6) | collective-permute-done | bytes 163872 | tf_op jit(solution)/shard_map/ppermute | solution.py:215
  133.1 0.4 merge_far.1
  133.5 16.0 %all-gather.2 = bf16[12,160,128]{2,1,0:T(8,128)(2,1)S(1)} all-gather(bf16[3,160,128]{2,1,0:T(8,128)(2,1)S(1)} %merge_far.1), channel_id=4, replica_groups=mesh['y'=8,'zh'=2,'c'=2,'row'=4,'col'=4] {'col'}, dimensions={0}, use_global_device_ids=true | all-gather | bytes 614400 | tf_op jit(solution)/shard_map/all_gather | solution.py:224
  149.5 6.3 %all-gather.3 = bf16[8,3,160,128]{3,2,1,0:T(8,128)(2,1)S(1)} all-gather(bf16[4,3,160,128]{3,2,1,0:T(8,128)(2,1)S(1)} %bitcast.37), channel_id=5, replica_groups=mesh['y'=8,'zh'=2,'c'=2,'row'=4,'col'=4] {'c'}, dimensions={0}, use_global_device_ids=true | all-gather | bytes 1474560 | tf_op jit(solution)/shard_map/all_gather | solution.py:225
  155.8 0.0 all-gather.6.cloned.1.call-done.w_ref
  155.8 0.0 copy-start
  155.8 1.7 copy-done
  157.5 0.0 copy-start.4
  157.5 1.7 project.1
  159.2 13.6 %all_to_all.21 = bf16[8,40,768]{2,1,0:T(8,128)(2,1)S(1)} all-to-all(bf16[8,40,768]{2,1,0:T(8,128)(2,1)S(1)} %bitcast.34), channel_id=1, replica_groups=mesh['y'=8,'zh'=2,'c'=2,'row'=4,'col'=4] {'c','row'}, dimensions={0} | all-to-all | bytes 983040 | tf_op jit(solution)/shard_map/all_to_all | solution.py:236
  172.7 0.1 convert_reduce_fusion
  172.8 0.0 copy-done.4
  172.8 0.7 add_convert_fusion
  (3 shorter events, 0.1 us)
Async XLA Ops:
  6.5 20.9 %copy-start.3 = (bf16[160,3,128]{2,0,1:T(8,128)(2,1)S(1)}, bf16[160,3,128]{2,0,1:T(8,128)(2,1)}, u32[]{:S(2)}) copy-start(bf16[160,3,128]{2,0,1:T(8,128)(2,1)} %param.6) | copy-start | bytes 368644
  6.5 21.0 %copy-start.2 = (bf16[160,3,128]{2,0,1:T(8,128)(2,1)S(1)}, bf16[160,3,128]{2,0,1:T(8,128)(2,1)}, u32[]{:S(2)}) copy-start(bf16[160,3,128]{2,0,1:T(8,128)(2,1)} %param.7) | copy-start | bytes 368644
  6.5 56.1 %copy-start.1 = (bf16[160,3,128]{2,0,1:T(8,128)(2,1)S(1)}, bf16[160,3,128]{2,0,1:T(8,128)(2,1)}, u32[]{:S(2)}) copy-start(bf16[160,3,128]{2,0,1:T(8,128)(2,1)} %param.5) | copy-start | bytes 368644
  6.5 149.3 %all-gather.6.cloned.1.call-start = ((), (), s32[]{:S(2)}) async-start(), calls=%async_computation.2 | async-start | bytes 2654208 | tf_op jit(solution)/shard_map/all_gather | solution.py:200
  11.8 14.6 %collective-permute-start.7 = (bf16[2,12,4,768]{3,2,1,0:T(4,128)(2,1)S(1)}, bf16[2,12,4,768]{3,2,1,0:T(4,128)(2,1)S(1)}, u32[]{:S(2)}, u32[]{:S(2)}) collective-permute-start(bf16[2,12,4,768]{3,2,1,0:T(4,128)(2,1)S(1)} %bitcast.40), channel_id=1, source_target_pairs={{0,32},{32,0},{1,33},{33,1},{2,34},{34,2},{3,35},{35,3},{4,36},{36... | collective-permute-start | bytes 442376 | tf_op jit(solution)/shard_map/ppermute | solution.py:197
  30.3 10.8 %collective-permute-start.1 = (bf16[2,2,3,160,128]{4,3,2,1,0:T(8,128)(2,1)S(1)}, bf16[2,2,3,160,128]{4,3,2,1,0:T(8,128)(2,1)S(1)}, u32[]{:S(2)}, u32[]{:S(2)}) collective-permute-start(bf16[2,2,3,160,128]{4,3,2,1,0:T(8,128)(2,1)S(1)} %bitcast.42), channel_id=1, source_target_pairs={{0,64},{16,464},{64,128},{80,16},{128,192},{144,80},{192,256},{208... | collective-permute-start | bytes 1474568 | tf_op jit(solution)/shard_map/ppermute | solution.py:185
  41.1 19.7 %collective-permute-start.2 = (bf16[2,2,3,160,128]{4,3,2,1,0:T(8,128)(2,1)S(1)}, bf16[2,2,3,160,128]{4,3,2,1,0:T(8,128)(2,1)S(1)}, u32[]{:S(2)}, u32[]{:S(2)}) collective-permute-start(bf16[2,2,3,160,128]{4,3,2,1,0:T(8,128)(2,1)S(1)} %collective-permute-done.1.b1_ref), channel_id=1, source_target_pairs={{0,64},{16,464},{64,128},{80,16},{128,192},{144,80},{192,256},{208... | collective-permute-start | bytes 1474568 | tf_op jit(solution)/shard_map/ppermute | solution.py:185
  60.7 20.2 %collective-permute-start.3 = (bf16[2,2,3,160,128]{4,3,2,1,0:T(8,128)(2,1)S(1)}, bf16[2,2,3,160,128]{4,3,2,1,0:T(8,128)(2,1)S(1)}, u32[]{:S(2)}, u32[]{:S(2)}) collective-permute-start(bf16[2,2,3,160,128]{4,3,2,1,0:T(8,128)(2,1)S(1)} %collective-permute-done.2.b2_ref), channel_id=1, source_target_pairs={{0,64},{16,464},{64,128},{80,16},{128,192},{144,80},{192,256},{208... | collective-permute-start | bytes 1474568 | tf_op jit(solution)/shard_map/ppermute | solution.py:185
  70.1 15.7 %collective-permute-start = (bf16[2,3,160,128]{3,2,1,0:T(8,128)(2,1)S(1)}, bf16[2,3,160,128]{3,2,1,0:T(8,128)(2,1)S(1)}, u32[]{:S(2)}, u32[]{:S(2)}) collective-permute-start(bf16[2,3,160,128]{3,2,1,0:T(8,128)(2,1)S(1)} %bitcast.35), channel_id=1, source_target_pairs={{0,32},{32,0},{1,33},{33,1},{2,34},{34,2},{3,35},{35,3},{4,36},{36... | collective-permute-start | bytes 737288 | tf_op jit(solution)/shard_map/ppermute | solution.py:191
  80.9 8.2 %collective-permute-start.4 = (bf16[2,3,160,128]{3,2,1,0:T(8,128)(2,1)S(1)}, bf16[2,3,160,128]{3,2,1,0:T(8,128)(2,1)S(1)}, u32[]{:S(2)}, u32[]{:S(2)}) collective-permute-start(bf16[2,3,160,128]{3,2,1,0:T(8,128)(2,1)S(1)} %dynamic-slice_bitcast_fusion), channel_id=1, source_target_pairs={{0,64},{16,464},{64,128},{80,16},{128,192},{144,80},{192,256},{208... | collective-permute-start | bytes 737288 | tf_op jit(solution)/shard_map/ppermute | solution.py:185
  115.5 3.5 %collective-permute-start.5 = (bf16[2,4,160,128]{3,2,1,0:T(8,128)(2,1)S(1)}, bf16[2,4,160,128]{3,2,1,0:T(8,128)(2,1)S(1)}, u32[]{:S(2)}, u32[]{:S(2)}) collective-permute-start(bf16[2,4,160,128]{3,2,1,0:T(8,128)(2,1)S(1)} %get-tuple-element.10), channel_id=1, source_target_pairs={{0,16},{16,0},{1,17},{17,1},{2,18},{18,2},{3,19},{19,3},{4,20},{20... | collective-permute-start | bytes 983048 | tf_op jit(solution)/shard_map/ppermute | solution.py:205
  120.1 13.0 %collective-permute-start.6 = (bf16[4,160,128]{2,1,0:T(8,128)(2,1)S(1)}, bf16[4,160,128]{2,1,0:T(8,128)(2,1)S(1)}, u32[]{:S(2)}, u32[]{:S(2)}) collective-permute-start(bf16[4,160,128]{2,1,0:T(8,128)(2,1)S(1)} %get-tuple-element.12), channel_id=1, source_target_pairs={{0,32},{32,0},{1,33},{33,1},{2,34},{34,2},{3,35},{35,3},{4,36},{36... | collective-permute-start | bytes 491528 | tf_op jit(solution)/shard_map/ppermute | solution.py:215
  155.8 1.7 copy-start
  157.5 15.3 %copy-start.4 = (f32[1536]{0:T(1024)S(1)}, f32[1536]{0:T(1024)}, u32[]{:S(2)}) copy-start(f32[1536]{0:T(1024)} %param.9) | copy-start | bytes 18436
Sparse Core Ops, SparseCore 0:
  27.6 52.6 all-gather.5

commit v2 on v0

v2 whole, which is shorter than its diff:
```python
import functools
import math

import jax
import jax.numpy as jnp
from jax import lax
from jax.experimental import pallas as pl
from jax.experimental.pallas import tpu as pltpu
from jax.sharding import Mesh
from jax.sharding import PartitionSpec as P

LOW = -1e30
VMEM = pl.BlockSpec(memory_space=pltpu.VMEM)
SMEM = pl.BlockSpec(memory_space=pltpu.SMEM)
PARAMS = pltpu.CompilerParams(vmem_limit_bytes=48 * 1024 * 1024)


def split3(x):
    high = x.astype(jnp.bfloat16).astype(jnp.float32)
    rest = x - high
    mid = rest.astype(jnp.bfloat16).astype(jnp.float32)
    return high, mid, rest - mid


def first_state(m_ref, l_ref, acc_ref, h):
    m_ref[h] = jnp.full(m_ref.shape[1:], LOW, jnp.float32)
    l_ref[h] = jnp.zeros(l_ref.shape[1:], jnp.float32)
    acc_ref[h] = jnp.zeros(acc_ref.shape[1:], jnp.float32)


def attend_block(m_ref, l_ref, acc_ref, h, scale2, query, keys, values, allowed=None):
    scores = lax.dot_general(keys, query, (((1,), (1,)), ((), ())), preferred_element_type=jnp.float32)
    scores = scores * scale2
    if allowed is not None:
        scores = jnp.where(allowed, scores, LOW)
    old = m_ref[h]
    new = jnp.maximum(old, jnp.max(scores, axis=0, keepdims=True))
    weights = jnp.exp2(scores - new)
    if allowed is not None:
        weights = jnp.where(allowed, weights, 0.0)
    fade = jnp.exp2(old - new)
    m_ref[h] = new
    l_ref[h] = l_ref[h] * fade + jnp.sum(weights, axis=0, keepdims=True)
    acc_ref[h] = acc_ref[h] * fade + lax.dot_general(
        values, weights.astype(jnp.bfloat16), (((0,), (0,)), ((), ())), preferred_element_type=jnp.float32
    )


def chip_block(ref, h):
    keys = jnp.concatenate([ref[0, 0, h], ref[1, 0, h]], axis=0)
    values = jnp.concatenate([ref[0, 1, h], ref[1, 1, h]], axis=0)
    return keys, values


def source_of(idx_ref, ring, distance):
    y, c = idx_ref[0], idx_ref[2]
    return jnp.where(c == 0, y + ring - distance, y + distance) % ring


def pack_kernel(q_ref, k_ref, v_ref, w_ref, own_ref, qw_ref):
    heads, rows, size = q_ref.shape
    own_ref[0] = k_ref[...]
    own_ref[1] = v_ref[...]
    for h in range(heads):
        qw_ref[h * rows : (h + 1) * rows] = q_ref[h]
    w_heads, deep, wide = w_ref.shape
    group, tiles = 16 // deep, wide // 128
    for g in range(w_heads // group):
        lines = jnp.concatenate([w_ref[g * group + k].astype(jnp.float32) for k in range(group)], axis=0)
        lines = lines.astype(jnp.bfloat16)
        for t in range(tiles):
            at = heads * rows + (g * tiles + t) * 16
            qw_ref[at : at + 16] = lines[:, t * 128 : (t + 1) * 128]


def whole(shape):
    return pl.BlockSpec(shape, lambda i: (0,) * len(shape))


def pack(q, k, v, w):
    heads, rows, size = q.shape
    lines = heads * rows + math.prod(w.shape) // 128
    return pl.pallas_call(
        pack_kernel,
        out_shape=(
            jax.ShapeDtypeStruct((2, heads, rows, size), jnp.bfloat16),
            jax.ShapeDtypeStruct((lines, 128), jnp.bfloat16),
        ),
        grid=(1,),
        in_specs=[whole(x.shape) for x in (q, k, v, w)],
        out_specs=(whole((2, heads, rows, size)), whole((lines, 128))),
        compiler_params=pltpu.CompilerParams(vmem_limit_bytes=60 * 1024 * 1024),
        name="pack",
    )(q, k, v, w)


def unpack_kernel(heads, rows, deep, idx_ref, own_ref, far_ref, query_ref, w_ref):
    zh, c = idx_ref[1], idx_ref[2]
    first = zh == 0
    w_heads, _, half = w_ref.shape

    def lines(at, count):
        near = [own_ref[core, pl.ds(at, count), :] for core in range(2)]
        far = [far_ref[core, pl.ds(at, count), :] for core in range(2)]
        low = [jnp.where(first, a, b) for a, b in zip(near, far)]
        return low + [jnp.where(first, b, a) for a, b in zip(near, far)]

    for h in range(heads):
        for block, value in enumerate(lines(h * rows, rows)):
            query_ref[h, block * rows : (block + 1) * rows] = value
    group, tiles = 16 // deep, half // 128
    for g in range(w_heads // group):
        for t in range(tiles):
            tile = (g * 2 + c) * tiles + t
            wide = [x.astype(jnp.float32) for x in lines(pl.multiple_of(heads * rows + tile * 16, 16), 16)]
            for k in range(group):
                piece = jnp.concatenate([x[k * deep : (k + 1) * deep] for x in wide], axis=0).astype(jnp.bfloat16)
                w_ref[g * group + k, :, t * 128 : (t + 1) * 128] = piece


def unpack(idx, own, far, heads, rows, w_shape):
    w_heads, deep, wide = w_shape
    return pl.pallas_call(
        functools.partial(unpack_kernel, heads, rows, deep),
        out_shape=(
            jax.ShapeDtypeStruct((heads, 4 * rows, 128), jnp.bfloat16),
            jax.ShapeDtypeStruct((w_heads, 4 * deep, wide // 2), jnp.bfloat16),
        ),
        in_specs=[SMEM, VMEM, VMEM],
        out_specs=(VMEM, VMEM),
        compiler_params=PARAMS,
        name="unpack",
    )(idx, own, far)


def near_kernel(rows, heads, ring, scale2, idx_ref, q_ref, own_ref, b1_ref, b2_ref, m_ref, l_ref, acc_ref):
    y, zh, c = idx_ref[0], idx_ref[1], idx_ref[2]
    query_pos = lax.broadcasted_iota(jnp.int32, (1, 4 * rows), 1)
    key_pos = (zh * 2 + c) * rows + lax.broadcasted_iota(jnp.int32, (rows, 1), 0)
    allowed = key_pos <= query_pos
    for h in range(heads):
        first_state(m_ref, l_ref, acc_ref, h)
    for h in range(heads):
        attend_block(m_ref, l_ref, acc_ref, h, scale2, q_ref[h], own_ref[0, h], own_ref[1, h], allowed)
    for distance, block_ref in ((1, b1_ref), (2, b2_ref)):

        @pl.when(source_of(idx_ref, ring, distance) < y)
        def _():
            for h in range(heads):
                attend_block(m_ref, l_ref, acc_ref, h, scale2, q_ref[h], *chip_block(block_ref, h))


def far_kernel(
    rows, heads, ring, scale2, idx_ref, q_ref, b3_ref, b4_ref, m_in, l_in, acc_in,
    keep_ref, send_ref, m_ref, l_ref, acc_ref,
):
    y, zh, c = idx_ref[0], idx_ref[1], idx_ref[2]

    def put(z, at, first, second):
        place = jnp.where(zh == z, 0, 1)
        keep_ref[place, at : at + first.shape[0]] = jnp.where(c == 0, first, second)
        send_ref[place, at : at + first.shape[0]] = jnp.where(c == 0, second, first)

    m_ref[...] = m_in[...]
    l_ref[...] = l_in[...]
    acc_ref[...] = acc_in[...]

    @pl.when(source_of(idx_ref, ring, 3) < y)
    def _():
        for h in range(heads):
            attend_block(m_ref, l_ref, acc_ref, h, scale2, q_ref[h], *chip_block(b3_ref, h))

    @pl.when(source_of(idx_ref, ring, 4) < y)
    def _():
        for h in range(heads):
            attend_block(m_ref, l_ref, acc_ref, h, scale2, q_ref[h], b4_ref[0, h], b4_ref[1, h])

    line = lax.broadcasted_iota(jnp.int32, (16, 4 * rows), 0)
    plane = jnp.zeros((16, 4 * rows), jnp.float32)
    for h in range(heads):
        total = l_ref[h]
        seen = total > 0.0
        safe = jnp.where(seen, total, 1.0)
        low = jnp.transpose(acc_ref[h] * (1.0 / safe)).astype(jnp.bfloat16)
        for z in range(2):
            put(z, h * rows, low[2 * z * rows : (2 * z + 1) * rows], low[(2 * z + 1) * rows : (2 * z + 2) * rows])
        log = jnp.where(seen, m_ref[h] + jnp.log2(safe), LOW)
        for part, piece in enumerate(split3(log)):
            plane = jnp.where(line == 3 * h + part, piece, plane)
    plane = jnp.concatenate([plane, jnp.zeros((16, 128), jnp.float32)], axis=1)
    for z in range(2):
        first, second = [
            plane[:, block * rows : block * rows + 256].astype(jnp.bfloat16) for block in (2 * z, 2 * z + 1)
        ]
        put(z, heads * rows, first[:, :128], second[:, :128])
        put(z, heads * rows + 16, first[:, 128:], second[:, 128:])


def state_shapes(heads, rows, size, kind):
    return (
        kind((heads, 1, 4 * rows), jnp.float32),
        kind((heads, 1, 4 * rows), jnp.float32),
        kind((heads, size, 4 * rows), jnp.float32),
    )


def attend_near(idx, query, own, b1, b2, ring):
    heads, rows, size = query.shape[0], query.shape[1] // 4, query.shape[2]
    scale2 = size ** (-0.5) * math.log2(math.e)
    keys = 5 * rows
    return pl.pallas_call(
        functools.partial(near_kernel, rows, heads, ring, scale2),
        out_shape=state_shapes(heads, rows, size, jax.ShapeDtypeStruct),
        in_specs=[SMEM] + [VMEM] * 4,
        out_specs=(VMEM,) * 3,
        compiler_params=PARAMS,
        cost_estimate=pl.CostEstimate(
            flops=16 * rows * keys * size * heads, bytes_accessed=4 << 20, transcendentals=4 * rows * keys * heads
        ),
        name="attend_near",
    )(idx, query, own, b1, b2)


def attend_far(idx, query, b3, b4, state, ring):
    heads, rows, size = query.shape[0], query.shape[1] // 4, query.shape[2]
    scale2 = size ** (-0.5) * math.log2(math.e)
    out = jax.ShapeDtypeStruct((2, heads * rows + 32, size), jnp.bfloat16)
    keys = 3 * rows
    return pl.pallas_call(
        functools.partial(far_kernel, rows, heads, ring, scale2),
        out_shape=(out, out),
        in_specs=[SMEM] + [VMEM] * 6,
        out_specs=(VMEM, VMEM),
        scratch_shapes=state_shapes(heads, rows, size, pltpu.VMEM),
        compiler_params=PARAMS,
        cost_estimate=pl.CostEstimate(
            flops=16 * rows * keys * size * heads, bytes_accessed=4 << 20, transcendentals=4 * rows * keys * heads
        ),
        name="attend_far",
    )(idx, query, b3, b4, *state)


def merge_two(rows, heads, a, b, out_ref, last):
    at = heads * rows
    planes = [jnp.concatenate([x[at : at + 16], x[at + 16 : at + 32]], axis=1).astype(jnp.float32) for x in (a, b)]
    line = lax.broadcasted_iota(jnp.int32, (128, 256), 0)
    shares = jnp.zeros((128, 256), jnp.float32)
    logs = jnp.zeros((16, 256), jnp.float32)
    for h in range(heads):
        log_a, log_b = [p[3 * h : 3 * h + 1] + p[3 * h + 1 : 3 * h + 2] + p[3 * h + 2 : 3 * h + 3] for p in planes]
        top = jnp.maximum(log_a, log_b)
        part_a, part_b = jnp.exp2(log_a - top), jnp.exp2(log_b - top)
        total = part_a + part_b
        shares = jnp.where(line == 2 * h, part_a / total, shares)
        shares = jnp.where(line == 2 * h + 1, part_b / total, shares)
        for part, piece in enumerate(split3(top + jnp.log2(total))):
            logs = jnp.where(line[:16] == 3 * h + part, piece, logs)
    shares = jnp.transpose(shares)[:rows]
    for h in range(heads):
        value = a[h * rows : (h + 1) * rows].astype(jnp.float32) * shares[:, 2 * h : 2 * h + 1]
        value = value + b[h * rows : (h + 1) * rows].astype(jnp.float32) * shares[:, 2 * h + 1 : 2 * h + 2]
        out_ref[h * rows : (h + 1) * rows] = value.astype(jnp.bfloat16)
    if not last:
        low = logs.astype(jnp.bfloat16)
        out_ref[at : at + 16] = low[:, :128]
        out_ref[at + 16 : at + 32] = low[:, 128:]


def merge_core_kernel(rows, heads, a_ref, b_ref, keep_ref, send_ref):
    merge_two(rows, heads, a_ref[1], b_ref[1], send_ref, False)
    merge_two(rows, heads, a_ref[0], b_ref[0], keep_ref, False)


def merge_far_kernel(rows, heads, a_ref, b_ref, out_ref):
    merge_two(rows, heads, a_ref[...], b_ref[...], out_ref, True)


def merge_core(keep, other, heads):
    _, lines, size = keep.shape
    out = jax.ShapeDtypeStruct((lines, size), jnp.bfloat16)
    return pl.pallas_call(
        functools.partial(merge_core_kernel, (lines - 32) // heads, heads),
        out_shape=(out, out),
        in_specs=[VMEM, VMEM],
        out_specs=(VMEM, VMEM),
        compiler_params=PARAMS,
        name="merge_core",
    )(keep, other)


def merge_far(keep, other, heads):
    lines, size = keep.shape
    return pl.pallas_call(
        functools.partial(merge_far_kernel, (lines - 32) // heads, heads),
        out_shape=jax.ShapeDtypeStruct((lines - 32, size), jnp.bfloat16),
        in_specs=[VMEM, VMEM],
        out_specs=VMEM,
        compiler_params=PARAMS,
        name="merge_far",
    )(keep, other)


def project_kernel(hops, ring, idx_ref, att_ref, *refs):
    w_refs, out_ref, w_all = refs[: len(hops)], refs[-2], refs[-1]
    cores, heads, rows, size = att_ref.shape
    for hop, w_ref in zip(hops, w_refs):
        source = (idx_ref[0] + ring - hop) % ring
        for h in range(heads):
            w_all[h, source] = w_ref[h]
    total = None
    for h in range(heads):
        left = jnp.concatenate([att_ref[core, h] for core in range(cores)], axis=0)
        right = w_all[h].reshape(size, w_all.shape[3])
        term = jnp.dot(left, right, preferred_element_type=jnp.float32)
        total = term if total is None else total + term
    low = total.astype(jnp.bfloat16)
    for core in range(cores):
        out_ref[core] = low[core * rows : (core + 1) * rows]


def project(idx, attended, weights, ring):
    cores, heads, rows, _ = attended.shape
    _, deep, half = weights[0].shape
    return pl.pallas_call(
        functools.partial(project_kernel, tuple(weights), ring),
        out_shape=jax.ShapeDtypeStruct((cores, rows, half), jnp.bfloat16),
        in_specs=[SMEM] + [VMEM] * (1 + len(weights)),
        out_specs=VMEM,
        scratch_shapes=[pltpu.VMEM((heads, ring, deep, half), jnp.bfloat16)],
        compiler_params=PARAMS,
        name="project",
    )(idx, attended, *weights.values())


def on_device(query_rows, key_rows, value_rows, out_weight, out_bias):
    rows, heads, size = query_rows.shape
    ring = lax.axis_size("y")
    y, zh, c = lax.axis_index("y"), lax.axis_index("zh"), lax.axis_index("c")
    idx = jnp.stack([y, zh, c]).astype(jnp.int32)

    def onward(block, hops):
        pairs = []
        for at in range(ring):
            pairs.append((2 * at, 2 * ((at + hops) % ring)))
            pairs.append((2 * at + 1, 2 * ((at - hops) % ring) + 1))
        return lax.ppermute(block, ("y", "c"), pairs)

    own, qw = pack(
        jnp.swapaxes(query_rows, 0, 1), jnp.swapaxes(key_rows, 0, 1), jnp.swapaxes(value_rows, 0, 1), out_weight
    )
    chip = lax.all_gather(own, "c", axis=0)
    b1 = onward(chip, 1)
    b2 = onward(chip, 2)
    qw, _ = lax.optimization_barrier((qw, chip))
    qw_far = lax.ppermute(qw, "zh", [(0, 1), (1, 0)])
    qw_own = lax.all_gather(qw, "c", axis=0)
    qw_far = lax.all_gather(qw_far, "c", axis=0)
    b3 = onward(b2, 1)
    b4 = onward(lax.dynamic_index_in_dim(b2, c, 0, keepdims=False), 2)
    query, weight = unpack(idx, qw_own, qw_far, heads, rows, out_weight.shape)
    state = attend_near(idx, query, own, b1, b2, ring)

    def along(block, hops):
        return lax.ppermute(block, "y", [(at, (at + hops) % ring) for at in range(ring)])

    half = weight.shape[2]
    weight, state = lax.optimization_barrier((weight, state))
    weights = {0: weight}
    for hops in (1, -1, 2, -2):
        weights[hops] = along(weight, hops)
    weights[3] = along(weights[2], 1)
    weights[-3] = along(weights[-2], -1)
    weights[4] = along(weights[2], 2)
    keep, send = attend_far(idx, query, b3, b4, state, ring)
    keep, send = merge_core(keep, lax.ppermute(send, "c", [(0, 1), (1, 0)]), heads)
    attended = merge_far(keep, lax.ppermute(send, "zh", [(0, 1), (1, 0)]), heads)
    attended = attended.reshape(heads, rows, size)
    attended = lax.all_gather(attended, "col", axis=0, tiled=True)
    attended = lax.all_gather(attended, "c", axis=0)
    projected = project(idx, attended, weights, ring)
    parts = lax.axis_size("row")
    pieces = projected.reshape(2 * parts, rows // parts, half)
    pieces = lax.all_to_all(pieces, ("c", "row"), 0, 0, tiled=True)
    pieces = pieces.reshape(2, parts, rows // parts, half)
    summed = jnp.sum(pieces.astype(jnp.float32), axis=1)
    summed = jnp.swapaxes(summed, 0, 1).reshape(rows // parts, 2 * half)
    return (summed + out_bias[None, :]).astype(jnp.bfloat16)


def solution(mesh):
    shape = mesh.devices.shape
    fine = Mesh(mesh.devices.reshape((shape[0] // 4, 2, 2) + shape[1:]), ("y", "zh", "c", "row", "col"))
    seq = ("y", "zh", "c")
    in_specs = (
        P(seq, ("row", "col"), None),
        P(seq, ("row", "col"), None),
        P(seq, ("row", "col"), None),
        P("row", seq, "col"),
        P("col"),
    )
    out_specs = P(seq + ("row",), "col")
    return jax.shard_map(
        on_device, mesh=fine, in_specs=in_specs, out_specs=out_specs, check_vma=False
    )
```

time: 380 us -> 120 us (0.32)
  waiting for transfers between devices: 319 us -> 3.48 us
  starting transfers between devices: 0.12 us -> 56.8 us
  blocking collectives: 15.7 us -> 47.1 us
  matrix products: 20.9 us -> 0 us
  between operations: 13.2 us -> 0.27 us
  Pallas kernels: 0 us -> 8.61 us
  local copies, waits for them, and re-layouts: 5.38 us -> 0.91 us
  other arithmetic: 5.2 us -> 0.81 us
    all_gather x3 -> x0, waiting for transfers between devices: 299 us -> none  [the longest x1 112 us: on_device(): key_block = lax.all_gather(key_rows, 'seq', axis=0, tiled=True)]
    ppermute x0 -> x14, starting transfers between devices: none -> 56.8 us  [the longest x7 25.6 us: along(): lax.ppermute(block, 'y', [(at, (at + hops) % ring) for at in range(ring)])]
    dot_general x3 -> x0, matrix products: 20.9 us -> none  [the longest x1 8.88 us: on_device(): jnp.einsum('qhd,hdo->qo', row_block, lax.all_gather(out_weight, 'seq', ax...]
    reduce_scatter x1 -> x0, waiting for transfers between devices: 18.5 us -> none  [on_device(): lax.psum_scatter(projected.astype(jnp.bfloat16), 'row', scatter_dimension...]
    all_gather x1 -> x5, blocking collectives: 15.7 us -> 33.6 us  [the longest x1 13.3 us: on_device(): attended = lax.all_gather(attended, 'col', axis=0, tiled=True)]
    all_to_all x0 -> x1, blocking collectives: none -> 13.5 us  [on_device(): pieces = lax.all_to_all(pieces, ('c', 'row'), 0, 0, tiled=True)]
    pallas_call x0 -> x7, Pallas kernels: none -> 8.61 us  [the longest x1 2.38 us: project(): pl.pallas_call(functools.partial(project_kernel, tuple(weights), ring), o...]
    unnamed x7 -> x6, local copies, waits for them, and re-layouts: 5.38 us -> 0.87 us
  transfers between devices with their start and end apart: 4 -> 14, of which waited for: 4 -> 1; matrix products, arithmetic and copies ran while one was open for 5% -> 0% of each run, Pallas kernels for 0% -> 3%
where the time goes in v2:
time: 120 us; the launch traced here: 118 us
  starting transfers between devices  56.8 us (47%)
  blocking collectives  47.1 us (39%)
  Pallas kernels  8.61 us (7%)
  waiting for transfers between devices  3.48 us (3%)
    ppermute x7, starting transfers between devices, along(): lax.ppermute(block, 'y', [(at, (at + hops) % ring) for at in range(ring)])  25.6 us
    all_to_all x1, blocking collectives, on_device(): pieces = lax.all_to_all(pieces, ('c', 'row'), 0, 0, tiled=True)  13.5 us
    all_gather x1, blocking collectives, on_device(): attended = lax.all_gather(attended, 'col', axis=0, tiled=True)  13.3 us
    ppermute x1, starting transfers between devices, on_device(): qw_far = lax.ppermute(qw, 'zh', [(0, 1), (1, 0)])  10.3 us
    all_gather x1, blocking collectives, on_device(): chip = lax.all_gather(own, 'c', axis=0)  8.99 us
    ppermute x4, starting transfers between devices, onward(): return lax.ppermute(block, ('y', 'c'), pairs)  8.73 us
    ppermute x1, starting transfers between devices, on_device(): lax.ppermute(send, 'zh', [(0, 1), (1, 0)])  8.65 us
    all_gather x1, blocking collectives, on_device(): attended = lax.all_gather(attended, 'c', axis=0)  5.62 us
  transfers between devices with their start and end apart: 14, of which 1 were waited for; matrix products, arithmetic and copies ran while one was open for 0% of the time, Pallas kernels for 3%

profile of v2, /device:TPU:1, one launch (start us, length us, event | category | flops | bytes accessed | tf_op | source)
XLA Modules:
  0.0 118.0 jit_solution(9140068256277533284)
XLA Ops:
  0.0 1.9 %pack.1 = (bf16[2,3,160,128]{3,2,1,0:T(8,128)(2,1)}, bf16[1056,128]{1,0:T(8,128)(2,1)}) custom-call(bf16[3,160,128]{2,1,0:T(8,128)(2,1)} %bitcast.29, bf16[3,160,128]{2,1,0:T(8,128)(2,1)} %bitcast.30, bf16[3,160,128]{2,1,0:T(8,128)(2,1)} %bitcast.31, bf16[12,4,1536]{2,1,0:T(4,128)(2,1)} %w_ref.1), custom_call_target="tpu_custom_call" | custom-call | tf_op jit(solution)/shard_map/pack/pallas_call | solution.py:83
  1.9 0.0 copy-start.1
  1.9 9.0 %all-gather = bf16[4,3,160,128]{3,2,1,0:T(8,128)(2,1)S(1)} all-gather(bf16[2,3,160,128]{3,2,1,0:T(8,128)(2,1)} %get-tuple-element.22.own_ref), channel_id=2, replica_groups=mesh['y'=8,'zh'=2,'c'=2,'row'=4,'col'=4] {'c'}, dimensions={0}, use_global_device_ids=true | all-gather | bytes 737280 | tf_op jit(solution)/shard_map/all_gather | solution.py:351
  10.9 1.9 %collective-permute-start.1 = (bf16[2,2,3,160,128]{4,3,2,1,0:T(8,128)(2,1)S(1)}, bf16[2,2,3,160,128]{4,3,2,1,0:T(8,128)(2,1)S(1)}, u32[]{:S(2)}, u32[]{:S(2)}) collective-permute-start(bf16[2,2,3,160,128]{4,3,2,1,0:T(8,128)(2,1)S(1)} %bitcast.27), channel_id=1, source_target_pairs={{0,128},{16,400},{64,192},{80,464},{128,256},{144,16},{192,320},{2... | collective-permute-start | bytes 1474568 | tf_op jit(solution)/shard_map/ppermute | solution.py:346
  12.8 1.9 %collective-permute-start.4 = (bf16[2,2,3,160,128]{4,3,2,1,0:T(8,128)(2,1)S(1)}, bf16[2,2,3,160,128]{4,3,2,1,0:T(8,128)(2,1)S(1)}, u32[]{:S(2)}, u32[]{:S(2)}) collective-permute-start(bf16[2,2,3,160,128]{4,3,2,1,0:T(8,128)(2,1)S(1)} %bitcast.28), channel_id=1, source_target_pairs={{0,64},{16,464},{64,128},{80,16},{128,192},{144,80},{192,256},{208... | collective-permute-start | bytes 1474568 | tf_op jit(solution)/shard_map/ppermute | solution.py:346
  14.7 0.0 copy-done.1
  14.8 10.3 %collective-permute-start = (bf16[1056,128]{1,0:T(8,128)(2,1)S(1)}, bf16[1056,128]{1,0:T(8,128)(2,1)S(1)}, u32[]{:S(2)}, u32[]{:S(2)}) collective-permute-start(bf16[1056,128]{1,0:T(8,128)(2,1)S(1)} %copy-done.1), channel_id=1, source_target_pairs={{0,32},{32,0},{1,33},{33,1},{2,34},{34,2},{3,35},{35,3},{4,36},{36... | collective-permute-start | bytes 811016 | tf_op jit(solution)/shard_map/ppermute | solution.py:355
  25.0 0.0 collective-permute-done.1.b2_ref
  25.1 3.0 %collective-permute-start.2 = (bf16[2,2,3,160,128]{4,3,2,1,0:T(8,128)(2,1)S(1)}, bf16[2,2,3,160,128]{4,3,2,1,0:T(8,128)(2,1)S(1)}, u32[]{:S(2)}, u32[]{:S(2)}) collective-permute-start(bf16[2,2,3,160,128]{4,3,2,1,0:T(8,128)(2,1)S(1)} %collective-permute-done.1.b2_ref), channel_id=1, source_target_pairs={{0,64},{16,464},{64,128},{80,16},{128,192},{144,80},{192,256},{208... | collective-permute-start | bytes 1474568 | tf_op jit(solution)/shard_map/ppermute | solution.py:346
  28.0 3.5 %all-gather.1 = bf16[2112,128]{1,0:T(8,128)(2,1)S(1)} all-gather(bf16[1056,128]{1,0:T(8,128)(2,1)S(1)} %copy-done.1), channel_id=3, replica_groups=mesh['y'=8,'zh'=2,'c'=2,'row'=4,'col'=4] {'c'}, dimensions={0}, use_global_device_ids=true | all-gather | bytes 811008 | tf_op jit(solution)/shard_map/all_gather | solution.py:356
  31.6 1.9 %collective-permute-start.3 = (bf16[2,3,160,128]{3,2,1,0:T(8,128)(2,1)S(1)}, bf16[2,3,160,128]{3,2,1,0:T(8,128)(2,1)S(1)}, u32[]{:S(2)}, u32[]{:S(2)}) collective-permute-start(bf16[2,3,160,128]{3,2,1,0:T(8,128)(2,1)S(1)} %dynamic-slice_bitcast_fusion), channel_id=1, source_target_pairs={{0,128},{16,400},{64,192},{80,464},{128,256},{144,16},{192,320},{2... | collective-permute-start | bytes 737288 | tf_op jit(solution)/shard_map/ppermute | solution.py:346
  33.5 0.1 pad_add_fusion.idx_ref
  33.6 3.4 %collective-permute-done = bf16[1056,128]{1,0:T(8,128)(2,1)S(1)} collective-permute-done((bf16[1056,128]{1,0:T(8,128)(2,1)S(1)}, bf16[1056,128]{1,0:T(8,128)(2,1)S(1)}, u32[]{:S(2)}, u32[]{:S(2)}) %collective-permute-start) | collective-permute-done | bytes 270368 | tf_op jit(solution)/shard_map/ppermute | solution.py:355
  37.1 2.2 %all-gather.2 = bf16[2112,128]{1,0:T(8,128)(2,1)S(1)} all-gather(bf16[1056,128]{1,0:T(8,128)(2,1)S(1)} %collective-permute-done), channel_id=4, replica_groups=mesh['y'=8,'zh'=2,'c'=2,'row'=4,'col'=4] {'c'}, dimensions={0}, use_global_device_ids=true | all-gather | bytes 811008 | tf_op jit(solution)/shard_map/all_gather | solution.py:357
  39.2 0.0 copy-start
  39.2 0.7 unpack.1
  40.0 0.0 collective-permute-done.4.b1_ref
  40.0 0.2 copy-done
  40.2 1.8 %attend_near.1 = (f32[3,1,640]{2,1,0:T(1,128)S(1)}, f32[3,1,640]{2,1,0:T(1,128)S(1)}, f32[3,128,640]{2,1,0:T(8,128)S(1)}) custom-call(s32[3]{0:T(128)S(1)} %pad_add_fusion.idx_ref, bf16[3,640,128]{2,1,0:T(8,128)(2,1)S(1)} %get-tuple-element.24.q_ref, bf16[2,3,160,128]{3,2,1,0:T(8,128)(2,1)S(1)} %copy-done, ...), custom_call_target="tpu_custom_call" | custom-call | flops 786432000 | bytes 4194304 | tf_op jit(solution)/shard_map/attend_near/pallas_call | solution.py:211
  42.0 0.0 collective-permute-done.3.b4_ref
  42.0 0.0 collective-permute-done.2.b3_ref
  42.0 0.9 attend_far.1
  42.9 3.5 %collective-permute-start.5 = (bf16[2,512,128]{2,1,0:T(8,128)(2,1)S(1)}, bf16[2,512,128]{2,1,0:T(8,128)(2,1)S(1)}, u32[]{:S(2)}, u32[]{:S(2)}) collective-permute-start(bf16[2,512,128]{2,1,0:T(8,128)(2,1)S(1)} %get-tuple-element.33), channel_id=1, source_target_pairs={{0,16},{16,0},{1,17},{17,1},{2,18},{18,2},{3,19},{19,3},{4,20},{20... | collective-permute-start | bytes 786440 | tf_op jit(solution)/shard_map/ppermute | solution.py:375
  46.4 3.6 %collective-permute-start.9 = (bf16[12,16,768]{2,1,0:T(8,128)(2,1)S(1)}, bf16[12,16,768]{2,1,0:T(8,128)(2,1)S(1)}, u32[]{:S(2)}, u32[]{:S(2)}) collective-permute-start(bf16[12,16,768]{2,1,0:T(8,128)(2,1)S(1)} %get-tuple-element.36.refs_0_), channel_id=1, source_target_pairs={{0,128},{64,192},{128,256},{192,320},{256,384},{320,448},{384,0},{... | collective-permute-start | bytes 884744 | tf_op jit(solution)/shard_map/ppermute | solution.py:364
  50.0 5.5 %collective-permute-start.10 = (bf16[12,16,768]{2,1,0:T(8,128)(2,1)S(1)}, bf16[12,16,768]{2,1,0:T(8,128)(2,1)S(1)}, u32[]{:S(2)}, u32[]{:S(2)}) collective-permute-start(bf16[12,16,768]{2,1,0:T(8,128)(2,1)S(1)} %get-tuple-element.36.refs_0_), channel_id=1, source_target_pairs={{0,384},{64,448},{128,0},{192,64},{256,128},{320,192},{384,256},{4... | collective-permute-start | bytes 884744 | tf_op jit(solution)/shard_map/ppermute | solution.py:364
  55.5 0.0 collective-permute-done.5.b_ref
  55.6 0.5 merge_core.1
  56.1 8.7 %collective-permute-start.6 = (bf16[512,128]{1,0:T(8,128)(2,1)S(1)}, bf16[512,128]{1,0:T(8,128)(2,1)S(1)}, u32[]{:S(2)}, u32[]{:S(2)}) collective-permute-start(bf16[512,128]{1,0:T(8,128)(2,1)S(1)} %get-tuple-element.35), channel_id=1, source_target_pairs={{0,32},{32,0},{1,33},{33,1},{2,34},{34,2},{3,35},{35,3},{4,36},{36... | collective-permute-start | bytes 393224 | tf_op jit(solution)/shard_map/ppermute | solution.py:376
  64.8 3.2 %collective-permute-start.7 = (bf16[12,16,768]{2,1,0:T(8,128)(2,1)S(1)}, bf16[12,16,768]{2,1,0:T(8,128)(2,1)S(1)}, u32[]{:S(2)}, u32[]{:S(2)}) collective-permute-start(bf16[12,16,768]{2,1,0:T(8,128)(2,1)S(1)} %get-tuple-element.36.refs_0_), channel_id=1, source_target_pairs={{0,64},{64,128},{128,192},{192,256},{256,320},{320,384},{384,448},... | collective-permute-start | bytes 884744 | tf_op jit(solution)/shard_map/ppermute | solution.py:364
  68.0 3.6 %collective-permute-start.8 = (bf16[12,16,768]{2,1,0:T(8,128)(2,1)S(1)}, bf16[12,16,768]{2,1,0:T(8,128)(2,1)S(1)}, u32[]{:S(2)}, u32[]{:S(2)}) collective-permute-start(bf16[12,16,768]{2,1,0:T(8,128)(2,1)S(1)} %get-tuple-element.36.refs_0_), channel_id=1, source_target_pairs={{0,448},{64,0},{128,64},{192,128},{256,192},{320,256},{384,320},{4... | collective-permute-start | bytes 884744 | tf_op jit(solution)/shard_map/ppermute | solution.py:364
  71.5 0.0 collective-permute-done.9.refs_3_
  71.5 2.1 %collective-permute-start.11 = (bf16[12,16,768]{2,1,0:T(8,128)(2,1)S(1)}, bf16[12,16,768]{2,1,0:T(8,128)(2,1)S(1)}, u32[]{:S(2)}, u32[]{:S(2)}) collective-permute-start(bf16[12,16,768]{2,1,0:T(8,128)(2,1)S(1)} %collective-permute-done.9.refs_3_), channel_id=1, source_target_pairs={{0,64},{64,128},{128,192},{192,256},{256,320},{320,384},{384,448},... | collective-permute-start | bytes 884744 | tf_op jit(solution)/shard_map/ppermute | solution.py:364
  73.7 0.0 collective-permute-done.10.refs_4_
  73.7 5.5 %collective-permute-start.13 = (bf16[12,16,768]{2,1,0:T(8,128)(2,1)S(1)}, bf16[12,16,768]{2,1,0:T(8,128)(2,1)S(1)}, u32[]{:S(2)}, u32[]{:S(2)}) collective-permute-start(bf16[12,16,768]{2,1,0:T(8,128)(2,1)S(1)} %collective-permute-done.9.refs_3_), channel_id=1, source_target_pairs={{0,128},{64,192},{128,256},{192,320},{256,384},{320,448},{384,0},{... | collective-permute-start | bytes 884744 | tf_op jit(solution)/shard_map/ppermute | solution.py:364
  79.2 0.0 collective-permute-done.6.b_ref
  79.2 2.2 %collective-permute-start.12 = (bf16[12,16,768]{2,1,0:T(8,128)(2,1)S(1)}, bf16[12,16,768]{2,1,0:T(8,128)(2,1)S(1)}, u32[]{:S(2)}, u32[]{:S(2)}) collective-permute-start(bf16[12,16,768]{2,1,0:T(8,128)(2,1)S(1)} %collective-permute-done.10.refs_4_), channel_id=1, source_target_pairs={{0,448},{64,0},{128,64},{192,128},{256,192},{320,256},{384,320},{4... | collective-permute-start | bytes 884744 | tf_op jit(solution)/shard_map/ppermute | solution.py:364
  81.4 0.4 merge_far.1
  81.7 13.3 %all_gather.33 = bf16[12,160,128]{2,1,0:T(8,128)(2,1)S(1)} all-gather(bf16[3,160,128]{2,1,0:T(8,128)(2,1)S(1)} %bitcast.24), channel_id=1, replica_groups=mesh['y'=8,'zh'=2,'c'=2,'row'=4,'col'=4] {'col'}, dimensions={0}, use_global_device_ids=true | all-gather | bytes 614400 | tf_op jit(solution)/shard_map/all_gather | solution.py:378
  95.0 5.6 %all-gather.3 = bf16[24,160,128]{2,1,0:T(8,128)(2,1)S(1)} all-gather(bf16[12,160,128]{2,1,0:T(8,128)(2,1)S(1)} %all_gather.33), channel_id=5, replica_groups=mesh['y'=8,'zh'=2,'c'=2,'row'=4,'col'=4] {'c'}, dimensions={0}, use_global_device_ids=true | all-gather | bytes 1474560 | tf_op jit(solution)/shard_map/all_gather | solution.py:379
  100.7 0.0 collective-permute-done.7.refs_1_
  100.7 0.0 collective-permute-done.8.refs_2_
  100.7 0.0 collective-permute-done.11.refs_5_
  100.7 0.0 collective-permute-done.12.refs_6_
  100.7 0.0 collective-permute-done.13.refs_7_
  100.7 2.4 %project.1 = bf16[2,160,768]{2,1,0:T(8,128)(2,1)S(1)} custom-call(s32[3]{0:T(128)S(1)} %pad_add_fusion.idx_ref, bf16[2,12,160,128]{3,2,1,0:T(8,128)(2,1)S(1)} %bitcast.20, bf16[12,16,768]{2,1,0:T(8,128)(2,1)S(1)} %get-tuple-element.36.refs_0_, bf16[12,16,768]{2,1,0:T(8,128)(2,1)S(1)} %collective-permute-done.7.refs_1_, ...), custom_call_target="tpu_custom_call" | custom-call | tf_op jit(solution)/shard_map/project/pallas_call | solution.py:324
  103.1 13.5 %all_to_all.5 = bf16[8,40,768]{2,1,0:T(8,128)(2,1)S(1)} all-to-all(bf16[8,40,768]{2,1,0:T(8,128)(2,1)S(1)} %bitcast.23), channel_id=1, replica_groups=mesh['y'=8,'zh'=2,'c'=2,'row'=4,'col'=4] {'c','row'}, dimensions={0} | all-to-all | bytes 983040 | tf_op jit(solution)/shard_map/all_to_all | solution.py:383
  116.6 0.1 convert_reduce_fusion
  116.6 0.0 copy-start.2
  116.7 0.7 copy-done.2
  117.3 0.7 add_convert_fusion
  (2 shorter events, 0.0 us)
Async XLA Ops:
  1.9 12.8 %copy-start.1 = (bf16[1056,128]{1,0:T(8,128)(2,1)S(1)}, bf16[1056,128]{1,0:T(8,128)(2,1)}, u32[]{:S(2)}) copy-start(bf16[1056,128]{1,0:T(8,128)(2,1)} %get-tuple-element.23) | copy-start | bytes 811012
  10.9 14.1 %collective-permute-start.1 = (bf16[2,2,3,160,128]{4,3,2,1,0:T(8,128)(2,1)S(1)}, bf16[2,2,3,160,128]{4,3,2,1,0:T(8,128)(2,1)S(1)}, u32[]{:S(2)}, u32[]{:S(2)}) collective-permute-start(bf16[2,2,3,160,128]{4,3,2,1,0:T(8,128)(2,1)S(1)} %bitcast.27), channel_id=1, source_target_pairs={{0,128},{16,400},{64,192},{80,464},{128,256},{144,16},{192,320},{2... | collective-permute-start | bytes 1474568 | tf_op jit(solution)/shard_map/ppermute | solution.py:346
  12.8 27.2 %collective-permute-start.4 = (bf16[2,2,3,160,128]{4,3,2,1,0:T(8,128)(2,1)S(1)}, bf16[2,2,3,160,128]{4,3,2,1,0:T(8,128)(2,1)S(1)}, u32[]{:S(2)}, u32[]{:S(2)}) collective-permute-start(bf16[2,2,3,160,128]{4,3,2,1,0:T(8,128)(2,1)S(1)} %bitcast.28), channel_id=1, source_target_pairs={{0,64},{16,464},{64,128},{80,16},{128,192},{144,80},{192,256},{208... | collective-permute-start | bytes 1474568 | tf_op jit(solution)/shard_map/ppermute | solution.py:346
  14.8 22.3 %collective-permute-start = (bf16[1056,128]{1,0:T(8,128)(2,1)S(1)}, bf16[1056,128]{1,0:T(8,128)(2,1)S(1)}, u32[]{:S(2)}, u32[]{:S(2)}) collective-permute-start(bf16[1056,128]{1,0:T(8,128)(2,1)S(1)} %copy-done.1), channel_id=1, source_target_pairs={{0,32},{32,0},{1,33},{33,1},{2,34},{34,2},{3,35},{35,3},{4,36},{36... | collective-permute-start | bytes 811016 | tf_op jit(solution)/shard_map/ppermute | solution.py:355
  25.1 16.9 %collective-permute-start.2 = (bf16[2,2,3,160,128]{4,3,2,1,0:T(8,128)(2,1)S(1)}, bf16[2,2,3,160,128]{4,3,2,1,0:T(8,128)(2,1)S(1)}, u32[]{:S(2)}, u32[]{:S(2)}) collective-permute-start(bf16[2,2,3,160,128]{4,3,2,1,0:T(8,128)(2,1)S(1)} %collective-permute-done.1.b2_ref), channel_id=1, source_target_pairs={{0,64},{16,464},{64,128},{80,16},{128,192},{144,80},{192,256},{208... | collective-permute-start | bytes 1474568 | tf_op jit(solution)/shard_map/ppermute | solution.py:346
  31.6 10.4 %collective-permute-start.3 = (bf16[2,3,160,128]{3,2,1,0:T(8,128)(2,1)S(1)}, bf16[2,3,160,128]{3,2,1,0:T(8,128)(2,1)S(1)}, u32[]{:S(2)}, u32[]{:S(2)}) collective-permute-start(bf16[2,3,160,128]{3,2,1,0:T(8,128)(2,1)S(1)} %dynamic-slice_bitcast_fusion), channel_id=1, source_target_pairs={{0,128},{16,400},{64,192},{80,464},{128,256},{144,16},{192,320},{2... | collective-permute-start | bytes 737288 | tf_op jit(solution)/shard_map/ppermute | solution.py:346
  39.2 0.9 copy-start
  42.9 12.7 %collective-permute-start.5 = (bf16[2,512,128]{2,1,0:T(8,128)(2,1)S(1)}, bf16[2,512,128]{2,1,0:T(8,128)(2,1)S(1)}, u32[]{:S(2)}, u32[]{:S(2)}) collective-permute-start(bf16[2,512,128]{2,1,0:T(8,128)(2,1)S(1)} %get-tuple-element.33), channel_id=1, source_target_pairs={{0,16},{16,0},{1,17},{17,1},{2,18},{18,2},{3,19},{19,3},{4,20},{20... | collective-permute-start | bytes 786440 | tf_op jit(solution)/shard_map/ppermute | solution.py:375
  46.4 25.1 %collective-permute-start.9 = (bf16[12,16,768]{2,1,0:T(8,128)(2,1)S(1)}, bf16[12,16,768]{2,1,0:T(8,128)(2,1)S(1)}, u32[]{:S(2)}, u32[]{:S(2)}) collective-permute-start(bf16[12,16,768]{2,1,0:T(8,128)(2,1)S(1)} %get-tuple-element.36.refs_0_), channel_id=1, source_target_pairs={{0,128},{64,192},{128,256},{192,320},{256,384},{320,448},{384,0},{... | collective-permute-start | bytes 884744 | tf_op jit(solution)/shard_map/ppermute | solution.py:364
  50.0 23.7 %collective-permute-start.10 = (bf16[12,16,768]{2,1,0:T(8,128)(2,1)S(1)}, bf16[12,16,768]{2,1,0:T(8,128)(2,1)S(1)}, u32[]{:S(2)}, u32[]{:S(2)}) collective-permute-start(bf16[12,16,768]{2,1,0:T(8,128)(2,1)S(1)} %get-tuple-element.36.refs_0_), channel_id=1, source_target_pairs={{0,384},{64,448},{128,0},{192,64},{256,128},{320,192},{384,256},{4... | collective-permute-start | bytes 884744 | tf_op jit(solution)/shard_map/ppermute | solution.py:364
  56.1 23.1 %collective-permute-start.6 = (bf16[512,128]{1,0:T(8,128)(2,1)S(1)}, bf16[512,128]{1,0:T(8,128)(2,1)S(1)}, u32[]{:S(2)}, u32[]{:S(2)}) collective-permute-start(bf16[512,128]{1,0:T(8,128)(2,1)S(1)} %get-tuple-element.35), channel_id=1, source_target_pairs={{0,32},{32,0},{1,33},{33,1},{2,34},{34,2},{3,35},{35,3},{4,36},{36... | collective-permute-start | bytes 393224 | tf_op jit(solution)/shard_map/ppermute | solution.py:376
  64.8 35.9 %collective-permute-start.7 = (bf16[12,16,768]{2,1,0:T(8,128)(2,1)S(1)}, bf16[12,16,768]{2,1,0:T(8,128)(2,1)S(1)}, u32[]{:S(2)}, u32[]{:S(2)}) collective-permute-start(bf16[12,16,768]{2,1,0:T(8,128)(2,1)S(1)} %get-tuple-element.36.refs_0_), channel_id=1, source_target_pairs={{0,64},{64,128},{128,192},{192,256},{256,320},{320,384},{384,448},... | collective-permute-start | bytes 884744 | tf_op jit(solution)/shard_map/ppermute | solution.py:364
  68.0 32.7 %collective-permute-start.8 = (bf16[12,16,768]{2,1,0:T(8,128)(2,1)S(1)}, bf16[12,16,768]{2,1,0:T(8,128)(2,1)S(1)}, u32[]{:S(2)}, u32[]{:S(2)}) collective-permute-start(bf16[12,16,768]{2,1,0:T(8,128)(2,1)S(1)} %get-tuple-element.36.refs_0_), channel_id=1, source_target_pairs={{0,448},{64,0},{128,64},{192,128},{256,192},{320,256},{384,320},{4... | collective-permute-start | bytes 884744 | tf_op jit(solution)/shard_map/ppermute | solution.py:364
  71.5 29.1 %collective-permute-start.11 = (bf16[12,16,768]{2,1,0:T(8,128)(2,1)S(1)}, bf16[12,16,768]{2,1,0:T(8,128)(2,1)S(1)}, u32[]{:S(2)}, u32[]{:S(2)}) collective-permute-start(bf16[12,16,768]{2,1,0:T(8,128)(2,1)S(1)} %collective-permute-done.9.refs_3_), channel_id=1, source_target_pairs={{0,64},{64,128},{128,192},{192,256},{256,320},{320,384},{384,448},... | collective-permute-start | bytes 884744 | tf_op jit(solution)/shard_map/ppermute | solution.py:364
  73.7 27.0 %collective-permute-start.13 = (bf16[12,16,768]{2,1,0:T(8,128)(2,1)S(1)}, bf16[12,16,768]{2,1,0:T(8,128)(2,1)S(1)}, u32[]{:S(2)}, u32[]{:S(2)}) collective-permute-start(bf16[12,16,768]{2,1,0:T(8,128)(2,1)S(1)} %collective-permute-done.9.refs_3_), channel_id=1, source_target_pairs={{0,128},{64,192},{128,256},{192,320},{256,384},{320,448},{384,0},{... | collective-permute-start | bytes 884744 | tf_op jit(solution)/shard_map/ppermute | solution.py:364
  79.2 21.5 %collective-permute-start.12 = (bf16[12,16,768]{2,1,0:T(8,128)(2,1)S(1)}, bf16[12,16,768]{2,1,0:T(8,128)(2,1)S(1)}, u32[]{:S(2)}, u32[]{:S(2)}) collective-permute-start(bf16[12,16,768]{2,1,0:T(8,128)(2,1)S(1)} %collective-permute-done.10.refs_4_), channel_id=1, source_target_pairs={{0,448},{64,0},{128,64},{192,128},{256,192},{320,256},{384,320},{4... | collective-permute-start | bytes 884744 | tf_op jit(solution)/shard_map/ppermute | solution.py:364
  116.6 0.7 copy-start.2

commit v3 on v2

--- a/solution.py
+++ b/solution.py
@@ -12,6 +12,7 @@
 LOW = -1e30
 VMEM = pl.BlockSpec(memory_space=pltpu.VMEM)
 SMEM = pl.BlockSpec(memory_space=pltpu.SMEM)
+ROOMY = pltpu.CompilerParams(vmem_limit_bytes=60 * 1024 * 1024)
 PARAMS = pltpu.CompilerParams(vmem_limit_bytes=48 * 1024 * 1024)
 
 
@@ -57,10 +58,12 @@
     return jnp.where(c == 0, y + ring - distance, y + distance) % ring
 
 
-def pack_kernel(q_ref, k_ref, v_ref, w_ref, own_ref, qw_ref):
+def whole(shape):
+    return pl.BlockSpec(shape, lambda i: (0,) * len(shape))
+
+
+def pack_kernel(q_ref, w_ref, qw_ref):
     heads, rows, size = q_ref.shape
-    own_ref[0] = k_ref[...]
-    own_ref[1] = v_ref[...]
     for h in range(heads):
         qw_ref[h * rows : (h + 1) * rows] = q_ref[h]
     w_heads, deep, wide = w_ref.shape
@@ -73,48 +76,39 @@
             qw_ref[at : at + 16] = lines[:, t * 128 : (t + 1) * 128]
 
 
-def whole(shape):
-    return pl.BlockSpec(shape, lambda i: (0,) * len(shape))
-
-
-def pack(q, k, v, w):
+def pack(q, w):
     heads, rows, size = q.shape
     lines = heads * rows + math.prod(w.shape) // 128
     return pl.pallas_call(
         pack_kernel,
-        out_shape=(
-            jax.ShapeDtypeStruct((2, heads, rows, size), jnp.bfloat16),
-            jax.ShapeDtypeStruct((lines, 128), jnp.bfloat16),
-        ),
+        out_shape=jax.ShapeDtypeStruct((lines, 128), jnp.bfloat16),
         grid=(1,),
-        in_specs=[whole(x.shape) for x in (q, k, v, w)],
-        out_specs=(whole((2, heads, rows, size)), whole((lines, 128))),
-        compiler_params=pltpu.CompilerParams(vmem_limit_bytes=60 * 1024 * 1024),
+        in_specs=[whole(q.shape), whole(w.shape)],
+        out_specs=whole((lines, 128)),
+        compiler_params=ROOMY,
         name="pack",
-    )(q, k, v, w)
+    )(q, w)
 
 
 def unpack_kernel(heads, rows, deep, idx_ref, own_ref, far_ref, query_ref, w_ref):
-    zh, c = idx_ref[1], idx_ref[2]
-    first = zh == 0
-    w_heads, _, half = w_ref.shape
+    first = idx_ref[1] == 0
+    w_heads, _, wide = w_ref.shape
 
     def lines(at, count):
-        near = [own_ref[core, pl.ds(at, count), :] for core in range(2)]
-        far = [far_ref[core, pl.ds(at, count), :] for core in range(2)]
+        near = [own_ref[core, at : at + count] for core in range(2)]
+        far = [far_ref[core, at : at + count] for core in range(2)]
         low = [jnp.where(first, a, b) for a, b in zip(near, far)]
         return low + [jnp.where(first, b, a) for a, b in zip(near, far)]
 
     for h in range(heads):
         for block, value in enumerate(lines(h * rows, rows)):
             query_ref[h, block * rows : (block + 1) * rows] = value
-    group, tiles = 16 // deep, half // 128
+    group, tiles = 16 // deep, wide // 128
     for g in range(w_heads // group):
         for t in range(tiles):
-            tile = (g * 2 + c) * tiles + t
-            wide = [x.astype(jnp.float32) for x in lines(pl.multiple_of(heads * rows + tile * 16, 16), 16)]
+            tile = [x.astype(jnp.float32) for x in lines(heads * rows + (g * tiles + t) * 16, 16)]
             for k in range(group):
-                piece = jnp.concatenate([x[k * deep : (k + 1) * deep] for x in wide], axis=0).astype(jnp.bfloat16)
+                piece = jnp.concatenate([x[k * deep : (k + 1) * deep] for x in tile], axis=0).astype(jnp.bfloat16)
                 w_ref[g * group + k, :, t * 128 : (t + 1) * 128] = piece
 
 
@@ -124,7 +118,7 @@
         functools.partial(unpack_kernel, heads, rows, deep),
         out_shape=(
             jax.ShapeDtypeStruct((heads, 4 * rows, 128), jnp.bfloat16),
-            jax.ShapeDtypeStruct((w_heads, 4 * deep, wide // 2), jnp.bfloat16),
+            jax.ShapeDtypeStruct((w_heads, 4 * deep, wide), jnp.bfloat16),
         ),
         in_specs=[SMEM, VMEM, VMEM],
         out_specs=(VMEM, VMEM),
@@ -300,36 +294,83 @@
     )(keep, other)
 
 
-def project_kernel(hops, ring, idx_ref, att_ref, *refs):
-    w_refs, out_ref, w_all = refs[: len(hops)], refs[-2], refs[-1]
+def project_kernel(ring, idx_ref, att_ref, w0_ref, w1_ref, w2_ref, w3_ref, w4_ref, keep_ref, send_ref):
+    y, c = idx_ref[0], idx_ref[2]
     cores, heads, rows, size = att_ref.shape
-    for hop, w_ref in zip(hops, w_refs):
-        source = (idx_ref[0] + ring - hop) % ring
-        for h in range(heads):
-            w_all[h, source] = w_ref[h]
+    deep = w0_ref.shape[1]
+    line = lax.broadcasted_iota(jnp.int32, (size, size), 0)
+    lane = lax.broadcasted_iota(jnp.int32, (size, size), 1)
+    sources = [jnp.where(c == 0, y, (y + 4) % ring)]
+    for hops in (1, 2, 3):
+        sources.append(jnp.where(c == 0, (y + ring - hops) % ring, (y + hops) % ring))
+    moves = []
+    for side in range(2):
+        wanted = jnp.full((size, size), -1, jnp.int32)
+        for slot, source in enumerate(sources):
+            at = side * size // 2 + slot * deep
+            inside = jnp.logical_and(lane >= at, lane < at + deep)
+            wanted = jnp.where(inside, lane + (source * deep - at), wanted)
+        moves.append(jnp.where(line == wanted, 1.0, 0.0).astype(jnp.bfloat16))
     total = None
-    for h in range(heads):
-        left = jnp.concatenate([att_ref[core, h] for core in range(cores)], axis=0)
-        right = w_all[h].reshape(size, w_all.shape[3])
-        term = jnp.dot(left, right, preferred_element_type=jnp.float32)
+    for h in range(0, heads, 2):
+        left, right = None, []
+        for side in range(2):
+            columns = jnp.concatenate([att_ref[core, h + side] for core in range(cores)], axis=0)
+            moved = jnp.dot(columns, moves[side], preferred_element_type=jnp.float32)
+            left = moved if left is None else left + moved
+            right.append(jnp.where(c == 0, w0_ref[h + side], w4_ref[h + side]))
+            right += [ref[h + side] for ref in (w1_ref, w2_ref, w3_ref)]
+        term = jnp.dot(left.astype(jnp.bfloat16), jnp.concatenate(right, axis=0), preferred_element_type=jnp.float32)
         total = term if total is None else total + term
-    low = total.astype(jnp.bfloat16)
-    for core in range(cores):
-        out_ref[core] = low[core * rows : (core + 1) * rows]
+    first, second = total[:rows], total[rows:]
+    keep_ref[...] = jnp.where(c == 0, first, second)
+    send_ref[...] = jnp.where(c == 0, second, first).astype(jnp.bfloat16)
 
 
 def project(idx, attended, weights, ring):
-    cores, heads, rows, _ = attended.shape
-    _, deep, half = weights[0].shape
-    return pl.pallas_call(
-        functools.partial(project_kernel, tuple(weights), ring),
-        out_shape=jax.ShapeDtypeStruct((cores, rows, half), jnp.bfloat16),
+    _, _, rows, _ = attended.shape
+    shape = (rows, weights[0].shape[2])
+    return pl.pallas_call(
+        functools.partial(project_kernel, ring),
+        out_shape=(jax.ShapeDtypeStruct(shape, jnp.float32), jax.ShapeDtypeStruct(shape, jnp.bfloat16)),
         in_specs=[SMEM] + [VMEM] * (1 + len(weights)),
+        out_specs=(VMEM, VMEM),
+        compiler_params=PARAMS,
+        name="project",
+    )(idx, attended, *weights)
+
+
+def join_kernel(keep_ref, other_ref, out_ref):
+    out_ref[...] = (keep_ref[...] + other_ref[...].astype(jnp.float32)).astype(jnp.bfloat16)
+
+
+def join(keep, other):
+    return pl.pallas_call(
+        join_kernel,
+        out_shape=jax.ShapeDtypeStruct(other.shape, jnp.bfloat16),
+        in_specs=[VMEM, VMEM],
         out_specs=VMEM,
-        scratch_shapes=[pltpu.VMEM((heads, ring, deep, half), jnp.bfloat16)],
-        compiler_params=PARAMS,
-        name="project",
-    )(idx, attended, *weights.values())
+        compiler_params=PARAMS,
+        name="join",
+    )(keep, other)
+
+
+def finish_kernel(pieces_ref, bias_ref, out_ref):
+    total = pieces_ref[0].astype(jnp.float32)
+    for part in range(1, pieces_ref.shape[0]):
+        total = total + pieces_ref[part].astype(jnp.float32)
+    out_ref[...] = (total + bias_ref[...]).astype(jnp.bfloat16)
+
+
+def finish(pieces, bias):
+    return pl.pallas_call(
+        finish_kernel,
+        out_shape=jax.ShapeDtypeStruct(pieces.shape[1:], jnp.bfloat16),
+        in_specs=[VMEM, VMEM],
+        out_specs=VMEM,
+        compiler_params=PARAMS,
+        name="finish",
+    )(pieces, bias)
 
 
 def on_device(query_rows, key_rows, value_rows, out_weight, out_bias):
@@ -345,14 +386,15 @@
             pairs.append((2 * at + 1, 2 * ((at - hops) % ring) + 1))
         return lax.ppermute(block, ("y", "c"), pairs)
 
-    own, qw = pack(
-        jnp.swapaxes(query_rows, 0, 1), jnp.swapaxes(key_rows, 0, 1), jnp.swapaxes(value_rows, 0, 1), out_weight
-    )
+    swap = [(0, 1), (1, 0)]
+
+    own = jnp.stack([jnp.swapaxes(key_rows, 0, 1), jnp.swapaxes(value_rows, 0, 1)])
     chip = lax.all_gather(own, "c", axis=0)
+    b2 = onward(chip, 2)
     b1 = onward(chip, 1)
-    b2 = onward(chip, 2)
-    qw, _ = lax.optimization_barrier((qw, chip))
-    qw_far = lax.ppermute(qw, "zh", [(0, 1), (1, 0)])
+    query, weight, _ = lax.optimization_barrier((jnp.swapaxes(query_rows, 0, 1), out_weight, chip))
+    qw = pack(query, weight)
+    qw_far = lax.ppermute(qw, "zh", swap)
     qw_own = lax.all_gather(qw, "c", axis=0)
     qw_far = lax.all_gather(qw_far, "c", axis=0)
     b3 = onward(b2, 1)
@@ -360,31 +402,25 @@
     query, weight = unpack(idx, qw_own, qw_far, heads, rows, out_weight.shape)
     state = attend_near(idx, query, own, b1, b2, ring)
 
-    def along(block, hops):
-        return lax.ppermute(block, "y", [(at, (at + hops) % ring) for at in range(ring)])
-
-    half = weight.shape[2]
-    weight, state = lax.optimization_barrier((weight, state))
-    weights = {0: weight}
-    for hops in (1, -1, 2, -2):
-        weights[hops] = along(weight, hops)
-    weights[3] = along(weights[2], 1)
-    weights[-3] = along(weights[-2], -1)
-    weights[4] = along(weights[2], 2)
+    weight, state, b3, b4 = lax.optimization_barrier((weight, state, b3, b4))
+    w2 = onward(weight, 2)
+    w1 = onward(weight, 1)
     keep, send = attend_far(idx, query, b3, b4, state, ring)
-    keep, send = merge_core(keep, lax.ppermute(send, "c", [(0, 1), (1, 0)]), heads)
-    attended = merge_far(keep, lax.ppermute(send, "zh", [(0, 1), (1, 0)]), heads)
+    keep, send = merge_core(keep, lax.ppermute(send, "c", swap), heads)
+    other = lax.ppermute(send, "zh", swap)
+    w2, other = lax.optimization_barrier((w2, other))
+    w3 = onward(w2, 1)
+    w4 = lax.ppermute(w2, ("y", "c"), [(2 * at + 1, 2 * ((at - 2) % ring) + 1) for at in range(ring)])
+    attended = merge_far(keep, other, heads)
     attended = attended.reshape(heads, rows, size)
     attended = lax.all_gather(attended, "col", axis=0, tiled=True)
     attended = lax.all_gather(attended, "c", axis=0)
-    projected = project(idx, attended, weights, ring)
+    keep, send = project(idx, attended, (weight, w1, w2, w3, w4), ring)
+    joined = join(keep, lax.ppermute(send, "c", swap))
     parts = lax.axis_size("row")
-    pieces = projected.reshape(2 * parts, rows // parts, half)
-    pieces = lax.all_to_all(pieces, ("c", "row"), 0, 0, tiled=True)
-    pieces = pieces.reshape(2, parts, rows // parts, half)
-    summed = jnp.sum(pieces.astype(jnp.float32), axis=1)
-    summed = jnp.swapaxes(summed, 0, 1).reshape(rows // parts, 2 * half)
-    return (summed + out_bias[None, :]).astype(jnp.bfloat16)
+    pieces = joined.reshape(parts, rows // parts, joined.shape[1])
+    pieces = lax.all_to_all(pieces, "row", 0, 0, tiled=True)
+    return finish(pieces, out_bias[None, :])
 
 
 def solution(mesh):

time: 120 us -> 116 us (0.967); the launches traced: 118 us -> 116 us
  blocking collectives: 47.1 us -> 33.6 us
  waiting for transfers between devices: 3.48 us -> 15.6 us
  starting transfers between devices: 56.8 us -> 54.4 us
  Pallas kernels: 8.61 us -> 10.9 us
    ppermute x10 -> x5, starting transfers between devices: 48.1 us -> 29.2 us  [the longest x1 10.3 us: on_device(): qw_far = lax.ppermute(qw, 'zh', swap)]
    all_to_all x1 -> x0, blocking collectives: 13.5 us -> none  [on_device(): pieces = lax.all_to_all(pieces, ('c', 'row'), 0, 0, tiled=True)]
    ppermute x4 -> x7, starting transfers between devices: 8.73 us -> 21 us  [onward(): return lax.ppermute(block, ('y', 'c'), pairs)]
    all_to_all x0 -> x1, waiting for transfers between devices: none -> 8.8 us  [on_device(): pieces = lax.all_to_all(pieces, 'row', 0, 0, tiled=True)]
    all_to_all x0 -> x1, starting transfers between devices: none -> 4.17 us  [on_device(): pieces = lax.all_to_all(pieces, 'row', 0, 0, tiled=True)]
    all_gather x1, blocking collectives: 13.3 us -> 16.7 us  [on_device(): attended = lax.all_gather(attended, 'col', axis=0, tiled=True)]
    all_gather x1, blocking collectives: 5.62 us -> 2.5 us  [on_device(): attended = lax.all_gather(attended, 'c', axis=0)]
    ppermute x10 -> x5, waiting for transfers between devices: 3.47 us -> 6.58 us  [the longest x1 3.73 us: on_device(): qw_far = lax.ppermute(qw, 'zh', swap)]
  transfers between devices with their start and end apart: 14 -> 13, of which waited for: 1 -> 5; matrix products, arithmetic and copies ran while one was open for 0% -> 0% of each run, Pallas kernels for 3% -> 5%
where the time goes in v3:
time: 116 us
  starting transfers between devices  54.4 us (47%)
  blocking collectives  33.6 us (29%)
  waiting for transfers between devices  15.6 us (13%)
  Pallas kernels  10.9 us (9%)
    ppermute x7, starting transfers between devices, onward(): return lax.ppermute(block, ('y', 'c'), pairs)  21 us
    all_gather x1, blocking collectives, on_device(): attended = lax.all_gather(attended, 'col', axis=0, tiled=True)  16.7 us
    ppermute x1, starting transfers between devices, on_device(): qw_far = lax.ppermute(qw, 'zh', swap)  10.3 us
    ppermute x1, starting transfers between devices, on_device(): other = lax.ppermute(send, 'zh', swap)  9.91 us
    all_to_all x1, waiting for transfers between devices, on_device(): pieces = lax.all_to_all(pieces, 'row', 0, 0, tiled=True)  8.8 us
    all_gather x1, blocking collectives, on_device(): chip = lax.all_gather(own, 'c', axis=0)  8.66 us
    ppermute x1, starting transfers between devices, on_device(): lax.ppermute(w2, ('y', 'c'), [(2 * at + 1, 2 * ((at - 2) % ring) + 1) for...  4.23 us
    all_to_all x1, starting transfers between devices, on_device(): pieces = lax.all_to_all(pieces, 'row', 0, 0, tiled=True)  4.17 us
  transfers between devices with their start and end apart: 13, of which 5 were waited for; matrix products, arithmetic and copies ran while one was open for 0% of the time, Pallas kernels for 5%

profile of v3, /device:TPU:1, one launch (start us, length us, event | category | flops | bytes accessed | tf_op | source)
XLA Modules:
  0.0 115.8 jit_solution(15250492642148489742)
XLA Ops:
  0.0 1.0 pad_maximum_fusion.own_ref
  1.0 8.7 %all-gather = bf16[4,3,160,128]{3,2,1,0:T(8,128)(2,1)S(1)} all-gather(bf16[2,3,160,128]{3,2,1,0:T(8,128)(2,1)S(1)} %pad_maximum_fusion.own_ref), channel_id=2, replica_groups=mesh['y'=8,'zh'=2,'c'=2,'row'=4,'col'=4] {'c'}, dimensions={0}, use_global_device_ids=true | all-gather | bytes 737280 | tf_op jit(solution)/shard_map/all_gather | solution.py:392
  9.7 1.9 %collective-permute-start.2 = (bf16[2,2,3,160,128]{4,3,2,1,0:T(8,128)(2,1)S(1)}, bf16[2,2,3,160,128]{4,3,2,1,0:T(8,128)(2,1)S(1)}, u32[]{:S(2)}, u32[]{:S(2)}) collective-permute-start(bf16[2,2,3,160,128]{4,3,2,1,0:T(8,128)(2,1)S(1)} %bitcast.22), channel_id=1, source_target_pairs={{0,128},{16,400},{64,192},{80,464},{128,256},{144,16},{192,320},{2... | collective-permute-start | bytes 1474568 | tf_op jit(solution)/shard_map/ppermute | solution.py:387
  11.6 1.9 %collective-permute-start.1 = (bf16[2,2,3,160,128]{4,3,2,1,0:T(8,128)(2,1)S(1)}, bf16[2,2,3,160,128]{4,3,2,1,0:T(8,128)(2,1)S(1)}, u32[]{:S(2)}, u32[]{:S(2)}) collective-permute-start(bf16[2,2,3,160,128]{4,3,2,1,0:T(8,128)(2,1)S(1)} %bitcast.23), channel_id=1, source_target_pairs={{0,64},{16,464},{64,128},{80,16},{128,192},{144,80},{192,256},{208... | collective-permute-start | bytes 1474568 | tf_op jit(solution)/shard_map/ppermute | solution.py:387
  13.5 1.7 %pack.1 = bf16[1056,128]{1,0:T(8,128)(2,1)} custom-call(bf16[3,160,128]{2,1,0:T(8,128)(2,1)} %bitcast.24, bf16[12,4,1536]{2,1,0:T(4,128)(2,1)} %w_ref), custom_call_target="tpu_custom_call" | custom-call | tf_op jit(solution)/shard_map/pack/pallas_call | solution.py:82
  15.2 10.3 %collective-permute-start = (bf16[1056,128]{1,0:T(8,128)(2,1)}, bf16[1056,128]{1,0:T(8,128)(2,1)S(1)}, u32[]{:S(2)}, u32[]{:S(2)}) collective-permute-start(bf16[1056,128]{1,0:T(8,128)(2,1)} %pack.1), channel_id=1, source_target_pairs={{0,32},{32,0},{1,33},{33,1},{2,34},{34,2},{3,35},{35,3},{4,36},{36... | collective-permute-start | bytes 811016 | tf_op jit(solution)/shard_map/ppermute | solution.py:397
  25.5 0.0 collective-permute-done.2.b2_ref
  25.5 3.0 %collective-permute-start.3 = (bf16[2,2,3,160,128]{4,3,2,1,0:T(8,128)(2,1)S(1)}, bf16[2,2,3,160,128]{4,3,2,1,0:T(8,128)(2,1)S(1)}, u32[]{:S(2)}, u32[]{:S(2)}) collective-permute-start(bf16[2,2,3,160,128]{4,3,2,1,0:T(8,128)(2,1)S(1)} %collective-permute-done.2.b2_ref), channel_id=1, source_target_pairs={{0,64},{16,464},{64,128},{80,16},{128,192},{144,80},{192,256},{208... | collective-permute-start | bytes 1474568 | tf_op jit(solution)/shard_map/ppermute | solution.py:387
  28.5 3.5 %all-gather.1 = bf16[2112,128]{1,0:T(8,128)(2,1)S(1)} all-gather(bf16[1056,128]{1,0:T(8,128)(2,1)} %pack.1), channel_id=3, replica_groups=mesh['y'=8,'zh'=2,'c'=2,'row'=4,'col'=4] {'c'}, dimensions={0}, use_global_device_ids=true | all-gather | bytes 811008 | tf_op jit(solution)/shard_map/all_gather | solution.py:398
  32.0 2.0 %collective-permute-start.4 = (bf16[2,3,160,128]{3,2,1,0:T(8,128)(2,1)S(1)}, bf16[2,3,160,128]{3,2,1,0:T(8,128)(2,1)S(1)}, u32[]{:S(2)}, u32[]{:S(2)}) collective-permute-start(bf16[2,3,160,128]{3,2,1,0:T(8,128)(2,1)S(1)} %dynamic-slice_bitcast_fusion), channel_id=1, source_target_pairs={{0,128},{16,400},{64,192},{80,464},{128,256},{144,16},{192,320},{2... | collective-permute-start | bytes 737288 | tf_op jit(solution)/shard_map/ppermute | solution.py:387
  34.0 0.1 pad_add_fusion.idx_ref
  34.1 3.7 %collective-permute-done = bf16[1056,128]{1,0:T(8,128)(2,1)S(1)} collective-permute-done((bf16[1056,128]{1,0:T(8,128)(2,1)}, bf16[1056,128]{1,0:T(8,128)(2,1)S(1)}, u32[]{:S(2)}, u32[]{:S(2)}) %collective-permute-start) | collective-permute-done | bytes 270368 | tf_op jit(solution)/shard_map/ppermute | solution.py:397
  37.8 2.2 %all-gather.2 = bf16[2112,128]{1,0:T(8,128)(2,1)S(1)} all-gather(bf16[1056,128]{1,0:T(8,128)(2,1)S(1)} %collective-permute-done), channel_id=4, replica_groups=mesh['y'=8,'zh'=2,'c'=2,'row'=4,'col'=4] {'c'}, dimensions={0}, use_global_device_ids=true | all-gather | bytes 811008 | tf_op jit(solution)/shard_map/all_gather | solution.py:399
  40.0 0.8 unpack.1
  40.8 0.0 collective-permute-done.1.b1_ref
  40.8 1.8 %attend_near.1 = (f32[3,1,640]{2,1,0:T(1,128)S(1)}, f32[3,1,640]{2,1,0:T(1,128)S(1)}, f32[3,128,640]{2,1,0:T(8,128)S(1)}) custom-call(s32[3]{0:T(128)S(1)} %pad_add_fusion.idx_ref, bf16[3,640,128]{2,1,0:T(8,128)(2,1)S(1)} %get-tuple-element.28.q_ref, bf16[2,3,160,128]{3,2,1,0:T(8,128)(2,1)S(1)} %pad_maximum_fusion.own_ref, ...), custom_call_target="tpu_custom_call" | custom-call | flops 786432000 | bytes 4194304 | tf_op jit(solution)/shard_map/attend_near/pallas_call | solution.py:205
  42.6 0.2 collective-permute-done.4.b4_ref
  42.8 0.0 collective-permute-done.3.b3_ref
  42.9 3.4 %collective-permute-start.6 = (bf16[12,16,1536]{2,1,0:T(8,128)(2,1)S(1)}, bf16[12,16,1536]{2,1,0:T(8,128)(2,1)S(1)}, u32[]{:S(2)}, u32[]{:S(2)}) collective-permute-start(bf16[12,16,1536]{2,1,0:T(8,128)(2,1)S(1)} %get-tuple-element.41.w0_ref), channel_id=1, source_target_pairs={{0,128},{16,400},{64,192},{80,464},{128,256},{144,16},{192,320},{2... | collective-permute-start | bytes 1769480 | tf_op jit(solution)/shard_map/ppermute | solution.py:387
  46.3 0.9 attend_far.1
  47.2 2.8 %collective-permute-start.5 = (bf16[2,512,128]{2,1,0:T(8,128)(2,1)S(1)}, bf16[2,512,128]{2,1,0:T(8,128)(2,1)S(1)}, u32[]{:S(2)}, u32[]{:S(2)}) collective-permute-start(bf16[2,512,128]{2,1,0:T(8,128)(2,1)S(1)} %get-tuple-element.39), channel_id=1, source_target_pairs={{0,16},{16,0},{1,17},{17,1},{2,18},{18,2},{3,19},{19,3},{4,20},{20... | collective-permute-start | bytes 786440 | tf_op jit(solution)/shard_map/ppermute | solution.py:409
  50.0 1.1 collective-permute-done.5.b_ref
  51.1 0.5 merge_core.1
  51.7 9.9 %collective-permute-start.7 = (bf16[512,128]{1,0:T(8,128)(2,1)S(1)}, bf16[512,128]{1,0:T(8,128)(2,1)S(1)}, u32[]{:S(2)}, u32[]{:S(2)}) collective-permute-start(bf16[512,128]{1,0:T(8,128)(2,1)S(1)} %get-tuple-element.42), channel_id=1, source_target_pairs={{0,32},{32,0},{1,33},{33,1},{2,34},{34,2},{3,35},{35,3},{4,36},{36... | collective-permute-start | bytes 393224 | tf_op jit(solution)/shard_map/ppermute | solution.py:410
  61.6 5.3 %collective-permute-start.8 = (bf16[12,16,1536]{2,1,0:T(8,128)(2,1)S(1)}, bf16[12,16,1536]{2,1,0:T(8,128)(2,1)S(1)}, u32[]{:S(2)}, u32[]{:S(2)}) collective-permute-start(bf16[12,16,1536]{2,1,0:T(8,128)(2,1)S(1)} %get-tuple-element.41.w0_ref), channel_id=1, source_target_pairs={{0,64},{16,464},{64,128},{80,16},{128,192},{144,80},{192,256},{208... | collective-permute-start | bytes 1769480 | tf_op jit(solution)/shard_map/ppermute | solution.py:387
  66.9 0.0 collective-permute-done.7.b_ref
  66.9 0.0 collective-permute-done.6.w2_ref
  66.9 4.2 %collective-permute-start.10 = (bf16[12,16,1536]{2,1,0:T(8,128)(2,1)S(1)}, bf16[12,16,1536]{2,1,0:T(8,128)(2,1)S(1)}, u32[]{:S(2)}, u32[]{:S(2)}) collective-permute-start(bf16[12,16,1536]{2,1,0:T(8,128)(2,1)S(1)} %collective-permute-done.6.w2_ref), channel_id=1, source_target_pairs={{16,400},{80,464},{144,16},{208,80},{272,144},{336,208},{400,272},... | collective-permute-start | bytes 1769480 | tf_op jit(solution)/shard_map/ppermute | solution.py:413
  71.1 3.5 %collective-permute-start.9 = (bf16[12,16,1536]{2,1,0:T(8,128)(2,1)S(1)}, bf16[12,16,1536]{2,1,0:T(8,128)(2,1)S(1)}, u32[]{:S(2)}, u32[]{:S(2)}) collective-permute-start(bf16[12,16,1536]{2,1,0:T(8,128)(2,1)S(1)} %collective-permute-done.6.w2_ref), channel_id=1, source_target_pairs={{0,64},{16,464},{64,128},{80,16},{128,192},{144,80},{192,256},{208... | collective-permute-start | bytes 1769480 | tf_op jit(solution)/shard_map/ppermute | solution.py:387
  74.7 0.4 merge_far.1
  75.0 16.7 %all_gather.33 = bf16[12,160,128]{2,1,0:T(8,128)(2,1)S(1)} all-gather(bf16[3,160,128]{2,1,0:T(8,128)(2,1)S(1)} %bitcast.21), channel_id=1, replica_groups=mesh['y'=8,'zh'=2,'c'=2,'row'=4,'col'=4] {'col'}, dimensions={0}, use_global_device_ids=true | all-gather | bytes 614400 | tf_op jit(solution)/shard_map/all_gather | solution.py:416
  91.8 2.5 %all-gather.3 = bf16[24,160,128]{2,1,0:T(8,128)(2,1)S(1)} all-gather(bf16[12,160,128]{2,1,0:T(8,128)(2,1)S(1)} %all_gather.33), channel_id=5, replica_groups=mesh['y'=8,'zh'=2,'c'=2,'row'=4,'col'=4] {'c'}, dimensions={0}, use_global_device_ids=true | all-gather | bytes 1474560 | tf_op jit(solution)/shard_map/all_gather | solution.py:417
  94.2 0.0 collective-permute-done.8.w1_ref
  94.3 0.0 collective-permute-done.10.w4_ref
  94.3 0.0 collective-permute-done.9.w3_ref
  94.3 3.1 %project.1 = (f32[160,1536]{1,0:T(8,128)S(1)}, bf16[160,1536]{1,0:T(8,128)(2,1)S(1)}) custom-call(s32[3]{0:T(128)S(1)} %pad_add_fusion.idx_ref, bf16[2,12,160,128]{3,2,1,0:T(8,128)(2,1)S(1)} %bitcast.18, bf16[12,16,1536]{2,1,0:T(8,128)(2,1)S(1)} %get-tuple-element.41.w0_ref, bf16[12,16,1536]{2,1,0:T(8,128)(2,1)S(1)} %collective-permute-done.8.w1_ref, ...), custom_call_target="tpu_custom_call" | custom-call | tf_op jit(solution)/shard_map/project/pallas_call | solution.py:333
  97.4 2.0 %collective-permute-start.11 = (bf16[160,1536]{1,0:T(8,128)(2,1)S(1)}, bf16[160,1536]{1,0:T(8,128)(2,1)S(1)}, u32[]{:S(2)}, u32[]{:S(2)}) collective-permute-start(bf16[160,1536]{1,0:T(8,128)(2,1)S(1)} %get-tuple-element.46), channel_id=1, source_target_pairs={{0,16},{16,0},{1,17},{17,1},{2,18},{18,2},{3,19},{19,3},{4,20},{20... | collective-permute-start | bytes 1474568 | tf_op jit(solution)/shard_map/ppermute | solution.py:419
  99.5 1.7 %collective-permute-done.11.other_ref = bf16[160,1536]{1,0:T(8,128)(2,1)S(1)} collective-permute-done((bf16[160,1536]{1,0:T(8,128)(2,1)S(1)}, bf16[160,1536]{1,0:T(8,128)(2,1)S(1)}, u32[]{:S(2)}, u32[]{:S(2)}) %collective-permute-start.11) | collective-permute-done | bytes 491552 | tf_op jit(solution)/shard_map/ppermute | solution.py:419
  101.2 0.9 join.1
  102.1 0.0 copy-start
  102.1 4.2 %all-to-all-start = ((bf16[4,40,1536]{2,1,0:T(8,128)(2,1)}), bf16[4,40,1536]{2,1,0:T(8,128)(2,1)S(1)}, u32[]{:S(2)}, u32[]{:S(2)}) async-start(bf16[4,40,1536]{2,1,0:T(8,128)(2,1)} %bitcast.14), calls=%async_computation | async-start | bytes 983040 | tf_op jit(solution)/shard_map/all_to_all | solution.py:422
  106.2 0.0 copy-done
  106.2 8.8 %all-to-all-done.pieces_ref = bf16[4,40,1536]{2,1,0:T(8,128)(2,1)S(1)} async-done(((bf16[4,40,1536]{2,1,0:T(8,128)(2,1)}), bf16[4,40,1536]{2,1,0:T(8,128)(2,1)S(1)}, u32[]{:S(2)}, u32[]{:S(2)}) %all-to-all-start) | async-done | bytes 491552 | tf_op jit(solution)/shard_map/all_to_all | solution.py:422
  115.0 0.7 finish.1
  (2 shorter events, 0.0 us)
Async XLA Ops:
  9.7 15.8 %collective-permute-start.2 = (bf16[2,2,3,160,128]{4,3,2,1,0:T(8,128)(2,1)S(1)}, bf16[2,2,3,160,128]{4,3,2,1,0:T(8,128)(2,1)S(1)}, u32[]{:S(2)}, u32[]{:S(2)}) collective-permute-start(bf16[2,2,3,160,128]{4,3,2,1,0:T(8,128)(2,1)S(1)} %bitcast.22), channel_id=1, source_target_pairs={{0,128},{16,400},{64,192},{80,464},{128,256},{144,16},{192,320},{2... | collective-permute-start | bytes 1474568 | tf_op jit(solution)/shard_map/ppermute | solution.py:387
  11.6 29.3 %collective-permute-start.1 = (bf16[2,2,3,160,128]{4,3,2,1,0:T(8,128)(2,1)S(1)}, bf16[2,2,3,160,128]{4,3,2,1,0:T(8,128)(2,1)S(1)}, u32[]{:S(2)}, u32[]{:S(2)}) collective-permute-start(bf16[2,2,3,160,128]{4,3,2,1,0:T(8,128)(2,1)S(1)} %bitcast.23), channel_id=1, source_target_pairs={{0,64},{16,464},{64,128},{80,16},{128,192},{144,80},{192,256},{208... | collective-permute-start | bytes 1474568 | tf_op jit(solution)/shard_map/ppermute | solution.py:387
  15.2 22.6 %collective-permute-start = (bf16[1056,128]{1,0:T(8,128)(2,1)}, bf16[1056,128]{1,0:T(8,128)(2,1)S(1)}, u32[]{:S(2)}, u32[]{:S(2)}) collective-permute-start(bf16[1056,128]{1,0:T(8,128)(2,1)} %pack.1), channel_id=1, source_target_pairs={{0,32},{32,0},{1,33},{33,1},{2,34},{34,2},{3,35},{35,3},{4,36},{36... | collective-permute-start | bytes 811016 | tf_op jit(solution)/shard_map/ppermute | solution.py:397
  25.5 17.3 %collective-permute-start.3 = (bf16[2,2,3,160,128]{4,3,2,1,0:T(8,128)(2,1)S(1)}, bf16[2,2,3,160,128]{4,3,2,1,0:T(8,128)(2,1)S(1)}, u32[]{:S(2)}, u32[]{:S(2)}) collective-permute-start(bf16[2,2,3,160,128]{4,3,2,1,0:T(8,128)(2,1)S(1)} %collective-permute-done.2.b2_ref), channel_id=1, source_target_pairs={{0,64},{16,464},{64,128},{80,16},{128,192},{144,80},{192,256},{208... | collective-permute-start | bytes 1474568 | tf_op jit(solution)/shard_map/ppermute | solution.py:387
  32.0 10.8 %collective-permute-start.4 = (bf16[2,3,160,128]{3,2,1,0:T(8,128)(2,1)S(1)}, bf16[2,3,160,128]{3,2,1,0:T(8,128)(2,1)S(1)}, u32[]{:S(2)}, u32[]{:S(2)}) collective-permute-start(bf16[2,3,160,128]{3,2,1,0:T(8,128)(2,1)S(1)} %dynamic-slice_bitcast_fusion), channel_id=1, source_target_pairs={{0,128},{16,400},{64,192},{80,464},{128,256},{144,16},{192,320},{2... | collective-permute-start | bytes 737288 | tf_op jit(solution)/shard_map/ppermute | solution.py:387
  42.9 24.0 %collective-permute-start.6 = (bf16[12,16,1536]{2,1,0:T(8,128)(2,1)S(1)}, bf16[12,16,1536]{2,1,0:T(8,128)(2,1)S(1)}, u32[]{:S(2)}, u32[]{:S(2)}) collective-permute-start(bf16[12,16,1536]{2,1,0:T(8,128)(2,1)S(1)} %get-tuple-element.41.w0_ref), channel_id=1, source_target_pairs={{0,128},{16,400},{64,192},{80,464},{128,256},{144,16},{192,320},{2... | collective-permute-start | bytes 1769480 | tf_op jit(solution)/shard_map/ppermute | solution.py:387
  47.2 3.9 %collective-permute-start.5 = (bf16[2,512,128]{2,1,0:T(8,128)(2,1)S(1)}, bf16[2,512,128]{2,1,0:T(8,128)(2,1)S(1)}, u32[]{:S(2)}, u32[]{:S(2)}) collective-permute-start(bf16[2,512,128]{2,1,0:T(8,128)(2,1)S(1)} %get-tuple-element.39), channel_id=1, source_target_pairs={{0,16},{16,0},{1,17},{17,1},{2,18},{18,2},{3,19},{19,3},{4,20},{20... | collective-permute-start | bytes 786440 | tf_op jit(solution)/shard_map/ppermute | solution.py:409
  51.7 15.2 %collective-permute-start.7 = (bf16[512,128]{1,0:T(8,128)(2,1)S(1)}, bf16[512,128]{1,0:T(8,128)(2,1)S(1)}, u32[]{:S(2)}, u32[]{:S(2)}) collective-permute-start(bf16[512,128]{1,0:T(8,128)(2,1)S(1)} %get-tuple-element.42), channel_id=1, source_target_pairs={{0,32},{32,0},{1,33},{33,1},{2,34},{34,2},{3,35},{35,3},{4,36},{36... | collective-permute-start | bytes 393224 | tf_op jit(solution)/shard_map/ppermute | solution.py:410
  61.6 32.7 %collective-permute-start.8 = (bf16[12,16,1536]{2,1,0:T(8,128)(2,1)S(1)}, bf16[12,16,1536]{2,1,0:T(8,128)(2,1)S(1)}, u32[]{:S(2)}, u32[]{:S(2)}) collective-permute-start(bf16[12,16,1536]{2,1,0:T(8,128)(2,1)S(1)} %get-tuple-element.41.w0_ref), channel_id=1, source_target_pairs={{0,64},{16,464},{64,128},{80,16},{128,192},{144,80},{192,256},{208... | collective-permute-start | bytes 1769480 | tf_op jit(solution)/shard_map/ppermute | solution.py:387
  66.9 27.4 %collective-permute-start.10 = (bf16[12,16,1536]{2,1,0:T(8,128)(2,1)S(1)}, bf16[12,16,1536]{2,1,0:T(8,128)(2,1)S(1)}, u32[]{:S(2)}, u32[]{:S(2)}) collective-permute-start(bf16[12,16,1536]{2,1,0:T(8,128)(2,1)S(1)} %collective-permute-done.6.w2_ref), channel_id=1, source_target_pairs={{16,400},{80,464},{144,16},{208,80},{272,144},{336,208},{400,272},... | collective-permute-start | bytes 1769480 | tf_op jit(solution)/shard_map/ppermute | solution.py:413
  71.1 23.1 %collective-permute-start.9 = (bf16[12,16,1536]{2,1,0:T(8,128)(2,1)S(1)}, bf16[12,16,1536]{2,1,0:T(8,128)(2,1)S(1)}, u32[]{:S(2)}, u32[]{:S(2)}) collective-permute-start(bf16[12,16,1536]{2,1,0:T(8,128)(2,1)S(1)} %collective-permute-done.6.w2_ref), channel_id=1, source_target_pairs={{0,64},{16,464},{64,128},{80,16},{128,192},{144,80},{192,256},{208... | collective-permute-start | bytes 1769480 | tf_op jit(solution)/shard_map/ppermute | solution.py:387
  97.4 3.8 %collective-permute-start.11 = (bf16[160,1536]{1,0:T(8,128)(2,1)S(1)}, bf16[160,1536]{1,0:T(8,128)(2,1)S(1)}, u32[]{:S(2)}, u32[]{:S(2)}) collective-permute-start(bf16[160,1536]{1,0:T(8,128)(2,1)S(1)} %get-tuple-element.46), channel_id=1, source_target_pairs={{0,16},{16,0},{1,17},{17,1},{2,18},{18,2},{3,19},{19,3},{4,20},{20... | collective-permute-start | bytes 1474568 | tf_op jit(solution)/shard_map/ppermute | solution.py:419
  102.1 4.2 %copy-start = (f32[1536]{0:T(1024)S(1)}, f32[1536]{0:T(1024)}, u32[]{:S(2)}) copy-start(f32[1536]{0:T(1024)} %param.9) | copy-start | bytes 18436
  102.1 13.0 %all-to-all-start = ((bf16[4,40,1536]{2,1,0:T(8,128)(2,1)}), bf16[4,40,1536]{2,1,0:T(8,128)(2,1)S(1)}, u32[]{:S(2)}, u32[]{:S(2)}) async-start(bf16[4,40,1536]{2,1,0:T(8,128)(2,1)} %bitcast.14), calls=%async_computation | async-start | bytes 983040 | tf_op jit(solution)/shard_map/all_to_all | solution.py:422

commit v4 on v3

--- a/solution.py
+++ b/solution.py
@@ -123,6 +123,7 @@
         in_specs=[SMEM, VMEM, VMEM],
         out_specs=(VMEM, VMEM),
         compiler_params=PARAMS,
+        cost_estimate=pl.CostEstimate(flops=1 << 28, bytes_accessed=1 << 20, transcendentals=0),
         name="unpack",
     )(idx, own, far)
 
@@ -208,9 +209,7 @@
         in_specs=[SMEM] + [VMEM] * 4,
         out_specs=(VMEM,) * 3,
         compiler_params=PARAMS,
-        cost_estimate=pl.CostEstimate(
-            flops=16 * rows * keys * size * heads, bytes_accessed=4 << 20, transcendentals=4 * rows * keys * heads
-        ),
+        cost_estimate=pl.CostEstimate(flops=1 << 28, bytes_accessed=1 << 18, transcendentals=0),
         name="attend_near",
     )(idx, query, own, b1, b2)
 
@@ -290,6 +289,7 @@
         in_specs=[VMEM, VMEM],
         out_specs=VMEM,
         compiler_params=PARAMS,
+        cost_estimate=pl.CostEstimate(flops=1 << 31, bytes_accessed=7 << 20, transcendentals=0),
         name="merge_far",
     )(keep, other)
 
@@ -311,20 +311,27 @@
             inside = jnp.logical_and(lane >= at, lane < at + deep)
             wanted = jnp.where(inside, lane + (source * deep - at), wanted)
         moves.append(jnp.where(line == wanted, 1.0, 0.0).astype(jnp.bfloat16))
-    total = None
+    lefts, rights = [], []
     for h in range(0, heads, 2):
-        left, right = None, []
+        left = None
         for side in range(2):
             columns = jnp.concatenate([att_ref[core, h + side] for core in range(cores)], axis=0)
             moved = jnp.dot(columns, moves[side], preferred_element_type=jnp.float32)
             left = moved if left is None else left + moved
-            right.append(jnp.where(c == 0, w0_ref[h + side], w4_ref[h + side]))
-            right += [ref[h + side] for ref in (w1_ref, w2_ref, w3_ref)]
-        term = jnp.dot(left.astype(jnp.bfloat16), jnp.concatenate(right, axis=0), preferred_element_type=jnp.float32)
-        total = term if total is None else total + term
-    first, second = total[:rows], total[rows:]
-    keep_ref[...] = jnp.where(c == 0, first, second)
-    send_ref[...] = jnp.where(c == 0, second, first).astype(jnp.bfloat16)
+            rights.append((w0_ref, w4_ref, h + side))
+            rights += [(ref, None, h + side) for ref in (w1_ref, w2_ref, w3_ref)]
+        lefts.append(left.astype(jnp.bfloat16))
+    left = jnp.concatenate(lefts, axis=1)
+    wide = w0_ref.shape[2]
+    for at in range(0, wide, 256):
+        pieces = []
+        for ref, other, h in rights:
+            piece = ref[h, :, at : at + 256]
+            pieces.append(piece if other is None else jnp.where(c == 0, piece, other[h, :, at : at + 256]))
+        total = jnp.dot(left, jnp.concatenate(pieces, axis=0), preferred_element_type=jnp.float32)
+        first, second = total[:rows], total[rows:]
+        keep_ref[:, at : at + 256] = jnp.where(c == 0, first, second)
+        send_ref[:, at : at + 256] = jnp.where(c == 0, second, first).astype(jnp.bfloat16)
 
 
 def project(idx, attended, weights, ring):
@@ -391,24 +398,25 @@
     own = jnp.stack([jnp.swapaxes(key_rows, 0, 1), jnp.swapaxes(value_rows, 0, 1)])
     chip = lax.all_gather(own, "c", axis=0)
     b2 = onward(chip, 2)
-    b1 = onward(chip, 1)
     query, weight, _ = lax.optimization_barrier((jnp.swapaxes(query_rows, 0, 1), out_weight, chip))
     qw = pack(query, weight)
+    near_chip, qw = lax.optimization_barrier((chip, qw))
+    b1 = onward(near_chip, 1)
     qw_far = lax.ppermute(qw, "zh", swap)
     qw_own = lax.all_gather(qw, "c", axis=0)
     qw_far = lax.all_gather(qw_far, "c", axis=0)
+    b2, qw_own = lax.optimization_barrier((b2, qw_own))
     b3 = onward(b2, 1)
     b4 = onward(lax.dynamic_index_in_dim(b2, c, 0, keepdims=False), 2)
     query, weight = unpack(idx, qw_own, qw_far, heads, rows, out_weight.shape)
     state = attend_near(idx, query, own, b1, b2, ring)
 
-    weight, state, b3, b4 = lax.optimization_barrier((weight, state, b3, b4))
+    weight, state = lax.optimization_barrier((weight, state))
     w2 = onward(weight, 2)
     w1 = onward(weight, 1)
     keep, send = attend_far(idx, query, b3, b4, state, ring)
     keep, send = merge_core(keep, lax.ppermute(send, "c", swap), heads)
     other = lax.ppermute(send, "zh", swap)
-    w2, other = lax.optimization_barrier((w2, other))
     w3 = onward(w2, 1)
     w4 = lax.ppermute(w2, ("y", "c"), [(2 * at + 1, 2 * ((at - 2) % ring) + 1) for at in range(ring)])
     attended = merge_far(keep, other, heads)

time: 116 us -> 111 us (0.957)
  blocking collectives: 33.6 us -> 29.3 us
  waiting for transfers between devices: 15.6 us -> 18.1 us
  starting transfers between devices: 54.4 us -> 52 us
  Pallas kernels: 10.9 us -> 9.48 us
    ppermute x7, waiting for transfers between devices: 0.24 us -> 4.62 us  [onward(): return lax.ppermute(block, ('y', 'c'), pairs)]
    all_gather x1, blocking collectives: 16.7 us -> 13 us  [on_device(): attended = lax.all_gather(attended, 'col', axis=0, tiled=True)]
    ppermute x7, starting transfers between devices: 21 us -> 24.3 us  [onward(): return lax.ppermute(block, ('y', 'c'), pairs)]
    ppermute x1, starting transfers between devices: 9.91 us -> 7.17 us  [on_device(): other = lax.ppermute(send, 'zh', swap)]
    ppermute x1, waiting for transfers between devices: 3.73 us -> 1.38 us  [on_device(): qw_far = lax.ppermute(qw, 'zh', swap)]
    pallas_call x1, Pallas kernels: 3.14 us -> 1.77 us  [project(): pl.pallas_call(functools.partial(project_kernel, ring), out_shape=(jax.Sh...]
  transfers between devices with their start and end apart: 13 -> 13, of which waited for: 5 -> 5; matrix products, arithmetic and copies ran while one was open for 0% -> 0% of each run, Pallas kernels for 5% -> 6%
where the time goes in v4:
time: 111 us; the launch traced here: 110 us
  starting transfers between devices  52 us (47%)
  blocking collectives  29.3 us (26%)
  waiting for transfers between devices  18.1 us (16%)
  Pallas kernels  9.48 us (9%)
    ppermute x7, starting transfers between devices, onward(): return lax.ppermute(block, ('y', 'c'), pairs)  24.3 us
    all_gather x1, blocking collectives, on_device(): attended = lax.all_gather(attended, 'col', axis=0, tiled=True)  13 us
    ppermute x1, starting transfers between devices, on_device(): qw_far = lax.ppermute(qw, 'zh', swap)  9.21 us
    all_to_all x1, waiting for transfers between devices, on_device(): pieces = lax.all_to_all(pieces, 'row', 0, 0, tiled=True)  8.8 us
    all_gather x1, blocking collectives, on_device(): chip = lax.all_gather(own, 'c', axis=0)  8.66 us
    ppermute x1, starting transfers between devices, on_device(): other = lax.ppermute(send, 'zh', swap)  7.17 us
    ppermute x7, waiting for transfers between devices, onward(): return lax.ppermute(block, ('y', 'c'), pairs)  4.62 us
    all_to_all x1, starting transfers between devices, on_device(): pieces = lax.all_to_all(pieces, 'row', 0, 0, tiled=True)  4.15 us
  transfers between devices with their start and end apart: 13, of which 5 were waited for; matrix products, arithmetic and copies ran while one was open for 0% of the time, Pallas kernels for 6%

profile of v4, /device:TPU:1, one launch (start us, length us, event | category | flops | bytes accessed | tf_op | source)
XLA Modules:
  0.0 110.2 jit_solution(18180691962729280853)
XLA Ops:
  0.0 1.0 pad_maximum_fusion.own_ref
  1.0 8.7 %all-gather = bf16[4,3,160,128]{3,2,1,0:T(8,128)(2,1)S(1)} all-gather(bf16[2,3,160,128]{3,2,1,0:T(8,128)(2,1)S(1)} %pad_maximum_fusion.own_ref), channel_id=2, replica_groups=mesh['y'=8,'zh'=2,'c'=2,'row'=4,'col'=4] {'c'}, dimensions={0}, use_global_device_ids=true | all-gather | bytes 737280 | tf_op jit(solution)/shard_map/all_gather | solution.py:399
  9.7 1.9 %collective-permute-start = (bf16[2,2,3,160,128]{4,3,2,1,0:T(8,128)(2,1)S(1)}, bf16[2,2,3,160,128]{4,3,2,1,0:T(8,128)(2,1)S(1)}, u32[]{:S(2)}, u32[]{:S(2)}) collective-permute-start(bf16[2,2,3,160,128]{4,3,2,1,0:T(8,128)(2,1)S(1)} %bitcast.22), channel_id=1, source_target_pairs={{0,128},{16,400},{64,192},{80,464},{128,256},{144,16},{192,320},{2... | collective-permute-start | bytes 1474568 | tf_op jit(solution)/shard_map/ppermute | solution.py:394
  11.6 1.7 %pack.1 = bf16[1056,128]{1,0:T(8,128)(2,1)} custom-call(bf16[3,160,128]{2,1,0:T(8,128)(2,1)} %bitcast.24, bf16[12,4,1536]{2,1,0:T(4,128)(2,1)} %w_ref), custom_call_target="tpu_custom_call" | custom-call | tf_op jit(solution)/shard_map/pack/pallas_call | solution.py:82
  13.3 9.2 %collective-permute-start.1 = (bf16[1056,128]{1,0:T(8,128)(2,1)}, bf16[1056,128]{1,0:T(8,128)(2,1)S(1)}, u32[]{:S(2)}, u32[]{:S(2)}) collective-permute-start(bf16[1056,128]{1,0:T(8,128)(2,1)} %pack.1), channel_id=1, source_target_pairs={{0,32},{32,0},{1,33},{33,1},{2,34},{34,2},{3,35},{35,3},{4,36},{36... | collective-permute-start | bytes 811016 | tf_op jit(solution)/shard_map/ppermute | solution.py:405
  22.5 3.0 %collective-permute-start.4 = (bf16[2,2,3,160,128]{4,3,2,1,0:T(8,128)(2,1)S(1)}, bf16[2,2,3,160,128]{4,3,2,1,0:T(8,128)(2,1)S(1)}, u32[]{:S(2)}, u32[]{:S(2)}) collective-permute-start(bf16[2,2,3,160,128]{4,3,2,1,0:T(8,128)(2,1)S(1)} %bitcast.23), channel_id=1, source_target_pairs={{0,64},{16,464},{64,128},{80,16},{128,192},{144,80},{192,256},{208... | collective-permute-start | bytes 1474568 | tf_op jit(solution)/shard_map/ppermute | solution.py:394
  25.5 2.4 %all-gather.1 = bf16[2112,128]{1,0:T(8,128)(2,1)S(1)} all-gather(bf16[1056,128]{1,0:T(8,128)(2,1)} %pack.1), channel_id=3, replica_groups=mesh['y'=8,'zh'=2,'c'=2,'row'=4,'col'=4] {'c'}, dimensions={0}, use_global_device_ids=true | all-gather | bytes 811008 | tf_op jit(solution)/shard_map/all_gather | solution.py:406
  27.9 0.0 collective-permute-done.b2_ref
  27.9 3.0 %collective-permute-start.2 = (bf16[2,2,3,160,128]{4,3,2,1,0:T(8,128)(2,1)S(1)}, bf16[2,2,3,160,128]{4,3,2,1,0:T(8,128)(2,1)S(1)}, u32[]{:S(2)}, u32[]{:S(2)}) collective-permute-start(bf16[2,2,3,160,128]{4,3,2,1,0:T(8,128)(2,1)S(1)} %collective-permute-done.b2_ref), channel_id=1, source_target_pairs={{0,64},{16,464},{64,128},{80,16},{128,192},{144,80},{192,256},{208... | collective-permute-start | bytes 1474568 | tf_op jit(solution)/shard_map/ppermute | solution.py:394
  30.9 0.1 pad_add_fusion.idx_ref
  31.0 2.0 %collective-permute-start.3 = (bf16[2,3,160,128]{3,2,1,0:T(8,128)(2,1)S(1)}, bf16[2,3,160,128]{3,2,1,0:T(8,128)(2,1)S(1)}, u32[]{:S(2)}, u32[]{:S(2)}) collective-permute-start(bf16[2,3,160,128]{3,2,1,0:T(8,128)(2,1)S(1)} %dynamic-slice_bitcast_fusion), channel_id=1, source_target_pairs={{0,128},{16,400},{64,192},{80,464},{128,256},{144,16},{192,320},{2... | collective-permute-start | bytes 737288 | tf_op jit(solution)/shard_map/ppermute | solution.py:394
  32.9 1.4 %collective-permute-done.1 = bf16[1056,128]{1,0:T(8,128)(2,1)S(1)} collective-permute-done((bf16[1056,128]{1,0:T(8,128)(2,1)}, bf16[1056,128]{1,0:T(8,128)(2,1)S(1)}, u32[]{:S(2)}, u32[]{:S(2)}) %collective-permute-start.1) | collective-permute-done | bytes 270368 | tf_op jit(solution)/shard_map/ppermute | solution.py:405
  34.3 2.7 %all-gather.2 = bf16[2112,128]{1,0:T(8,128)(2,1)S(1)} all-gather(bf16[1056,128]{1,0:T(8,128)(2,1)S(1)} %collective-permute-done.1), channel_id=4, replica_groups=mesh['y'=8,'zh'=2,'c'=2,'row'=4,'col'=4] {'c'}, dimensions={0}, use_global_device_ids=true | all-gather | bytes 811008 | tf_op jit(solution)/shard_map/all_gather | solution.py:407
  37.0 0.8 unpack.1
  37.8 0.0 collective-permute-done.4.b1_ref
  37.8 1.8 %attend_near.1 = (f32[3,1,640]{2,1,0:T(1,128)S(1)}, f32[3,1,640]{2,1,0:T(1,128)S(1)}, f32[3,128,640]{2,1,0:T(8,128)S(1)}) custom-call(s32[3]{0:T(128)S(1)} %pad_add_fusion.idx_ref, bf16[3,640,128]{2,1,0:T(8,128)(2,1)S(1)} %get-tuple-element.30.q_ref, bf16[2,3,160,128]{3,2,1,0:T(8,128)(2,1)S(1)} %pad_maximum_fusion.own_ref, ...), custom_call_target="tpu_custom_call" | custom-call | flops 268435456 | bytes 262144 | tf_op jit(solution)/shard_map/attend_near/pallas_call | solution.py:206
  39.6 6.6 %collective-permute-start.8 = (bf16[12,16,1536]{2,1,0:T(8,128)(2,1)S(1)}, bf16[12,16,1536]{2,1,0:T(8,128)(2,1)S(1)}, u32[]{:S(2)}, u32[]{:S(2)}) collective-permute-start(bf16[12,16,1536]{2,1,0:T(8,128)(2,1)S(1)} %get-tuple-element.44.w0_ref), channel_id=1, source_target_pairs={{0,128},{16,400},{64,192},{80,464},{128,256},{144,16},{192,320},{2... | collective-permute-start | bytes 1769480 | tf_op jit(solution)/shard_map/ppermute | solution.py:394
  46.3 0.0 collective-permute-done.3.b4_ref
  46.3 0.0 collective-permute-done.2.b3_ref
  46.3 0.9 attend_far.1
  47.2 1.9 %collective-permute-start.5 = (bf16[2,512,128]{2,1,0:T(8,128)(2,1)S(1)}, bf16[2,512,128]{2,1,0:T(8,128)(2,1)S(1)}, u32[]{:S(2)}, u32[]{:S(2)}) collective-permute-start(bf16[2,512,128]{2,1,0:T(8,128)(2,1)S(1)} %get-tuple-element.41), channel_id=1, source_target_pairs={{0,16},{16,0},{1,17},{17,1},{2,18},{18,2},{3,19},{19,3},{4,20},{20... | collective-permute-start | bytes 786440 | tf_op jit(solution)/shard_map/ppermute | solution.py:418
  49.1 1.5 %collective-permute-done.5.b_ref = bf16[2,512,128]{2,1,0:T(8,128)(2,1)S(1)} collective-permute-done((bf16[2,512,128]{2,1,0:T(8,128)(2,1)S(1)}, bf16[2,512,128]{2,1,0:T(8,128)(2,1)S(1)}, u32[]{:S(2)}, u32[]{:S(2)}) %collective-permute-start.5) | collective-permute-done | bytes 262176 | tf_op jit(solution)/shard_map/ppermute | solution.py:418
  50.6 0.5 merge_core.1
  51.2 7.2 %collective-permute-start.6 = (bf16[512,128]{1,0:T(8,128)(2,1)S(1)}, bf16[512,128]{1,0:T(8,128)(2,1)S(1)}, u32[]{:S(2)}, u32[]{:S(2)}) collective-permute-start(bf16[512,128]{1,0:T(8,128)(2,1)S(1)} %get-tuple-element.43), channel_id=1, source_target_pairs={{0,32},{32,0},{1,33},{33,1},{2,34},{34,2},{3,35},{35,3},{4,36},{36... | collective-permute-start | bytes 393224 | tf_op jit(solution)/shard_map/ppermute | solution.py:419
  58.4 6.0 %collective-permute-start.7 = (bf16[12,16,1536]{2,1,0:T(8,128)(2,1)S(1)}, bf16[12,16,1536]{2,1,0:T(8,128)(2,1)S(1)}, u32[]{:S(2)}, u32[]{:S(2)}) collective-permute-start(bf16[12,16,1536]{2,1,0:T(8,128)(2,1)S(1)} %get-tuple-element.44.w0_ref), channel_id=1, source_target_pairs={{0,64},{16,464},{64,128},{80,16},{128,192},{144,80},{192,256},{208... | collective-permute-start | bytes 1769480 | tf_op jit(solution)/shard_map/ppermute | solution.py:394
  64.3 0.0 collective-permute-done.8.w2_ref
  64.3 3.3 %collective-permute-start.10 = (bf16[12,16,1536]{2,1,0:T(8,128)(2,1)S(1)}, bf16[12,16,1536]{2,1,0:T(8,128)(2,1)S(1)}, u32[]{:S(2)}, u32[]{:S(2)}) collective-permute-start(bf16[12,16,1536]{2,1,0:T(8,128)(2,1)S(1)} %collective-permute-done.8.w2_ref), channel_id=1, source_target_pairs={{16,400},{80,464},{144,16},{208,80},{272,144},{336,208},{400,272},... | collective-permute-start | bytes 1769480 | tf_op jit(solution)/shard_map/ppermute | solution.py:421
  67.7 1.9 %collective-permute-start.9 = (bf16[12,16,1536]{2,1,0:T(8,128)(2,1)S(1)}, bf16[12,16,1536]{2,1,0:T(8,128)(2,1)S(1)}, u32[]{:S(2)}, u32[]{:S(2)}) collective-permute-start(bf16[12,16,1536]{2,1,0:T(8,128)(2,1)S(1)} %collective-permute-done.8.w2_ref), channel_id=1, source_target_pairs={{0,64},{16,464},{64,128},{80,16},{128,192},{144,80},{192,256},{208... | collective-permute-start | bytes 1769480 | tf_op jit(solution)/shard_map/ppermute | solution.py:394
  69.6 0.0 collective-permute-done.6.b_ref
  69.6 0.4 merge_far.1
  70.0 13.0 %all_gather.33 = bf16[12,160,128]{2,1,0:T(8,128)(2,1)S(1)} all-gather(bf16[3,160,128]{2,1,0:T(8,128)(2,1)S(1)} %bitcast.21), channel_id=1, replica_groups=mesh['y'=8,'zh'=2,'c'=2,'row'=4,'col'=4] {'col'}, dimensions={0}, use_global_device_ids=true | all-gather | bytes 614400 | tf_op jit(solution)/shard_map/all_gather | solution.py:424
  83.0 2.5 %all-gather.3 = bf16[24,160,128]{2,1,0:T(8,128)(2,1)S(1)} all-gather(bf16[12,160,128]{2,1,0:T(8,128)(2,1)S(1)} %all_gather.33), channel_id=5, replica_groups=mesh['y'=8,'zh'=2,'c'=2,'row'=4,'col'=4] {'c'}, dimensions={0}, use_global_device_ids=true | all-gather | bytes 1474560 | tf_op jit(solution)/shard_map/all_gather | solution.py:425
  85.5 0.0 collective-permute-done.7.w1_ref
  85.5 0.0 collective-permute-done.10.w4_ref
  85.5 4.6 %collective-permute-done.9.w3_ref = bf16[12,16,1536]{2,1,0:T(8,128)(2,1)S(1)} collective-permute-done((bf16[12,16,1536]{2,1,0:T(8,128)(2,1)S(1)}, bf16[12,16,1536]{2,1,0:T(8,128)(2,1)S(1)}, u32[]{:S(2)}, u32[]{:S(2)}) %collective-permute-start.9) | collective-permute-done | bytes 589856 | tf_op jit(solution)/shard_map/ppermute | solution.py:394
  90.1 1.8 %project.1 = (f32[160,1536]{1,0:T(8,128)S(1)}, bf16[160,1536]{1,0:T(8,128)(2,1)S(1)}) custom-call(s32[3]{0:T(128)S(1)} %pad_add_fusion.idx_ref, bf16[2,12,160,128]{3,2,1,0:T(8,128)(2,1)S(1)} %bitcast.18, bf16[12,16,1536]{2,1,0:T(8,128)(2,1)S(1)} %get-tuple-element.44.w0_ref, bf16[12,16,1536]{2,1,0:T(8,128)(2,1)S(1)} %collective-permute-done.7.w1_ref, ...), custom_call_target="tpu_custom_call" | custom-call | tf_op jit(solution)/shard_map/project/pallas_call | solution.py:340
  91.9 1.9 %collective-permute-start.11 = (bf16[160,1536]{1,0:T(8,128)(2,1)S(1)}, bf16[160,1536]{1,0:T(8,128)(2,1)S(1)}, u32[]{:S(2)}, u32[]{:S(2)}) collective-permute-start(bf16[160,1536]{1,0:T(8,128)(2,1)S(1)} %get-tuple-element.46), channel_id=1, source_target_pairs={{0,16},{16,0},{1,17},{17,1},{2,18},{18,2},{3,19},{19,3},{4,20},{20... | collective-permute-start | bytes 1474568 | tf_op jit(solution)/shard_map/ppermute | solution.py:427
  93.8 1.8 %collective-permute-done.11.other_ref = bf16[160,1536]{1,0:T(8,128)(2,1)S(1)} collective-permute-done((bf16[160,1536]{1,0:T(8,128)(2,1)S(1)}, bf16[160,1536]{1,0:T(8,128)(2,1)S(1)}, u32[]{:S(2)}, u32[]{:S(2)}) %collective-permute-start.11) | collective-permute-done | bytes 491552 | tf_op jit(solution)/shard_map/ppermute | solution.py:427
  95.7 0.9 join.1
  96.5 0.0 copy-start
  96.5 4.1 %all-to-all-start = ((bf16[4,40,1536]{2,1,0:T(8,128)(2,1)}), bf16[4,40,1536]{2,1,0:T(8,128)(2,1)S(1)}, u32[]{:S(2)}, u32[]{:S(2)}) async-start(bf16[4,40,1536]{2,1,0:T(8,128)(2,1)} %bitcast.14), calls=%async_computation | async-start | bytes 983040 | tf_op jit(solution)/shard_map/all_to_all | solution.py:430
  100.7 0.0 copy-done
  100.7 8.8 %all-to-all-done.pieces_ref = bf16[4,40,1536]{2,1,0:T(8,128)(2,1)S(1)} async-done(((bf16[4,40,1536]{2,1,0:T(8,128)(2,1)}), bf16[4,40,1536]{2,1,0:T(8,128)(2,1)S(1)}, u32[]{:S(2)}, u32[]{:S(2)}) %all-to-all-start) | async-done | bytes 491552 | tf_op jit(solution)/shard_map/all_to_all | solution.py:430
  109.5 0.7 finish.1
  (2 shorter events, 0.0 us)
Async XLA Ops:
  9.7 18.2 %collective-permute-start = (bf16[2,2,3,160,128]{4,3,2,1,0:T(8,128)(2,1)S(1)}, bf16[2,2,3,160,128]{4,3,2,1,0:T(8,128)(2,1)S(1)}, u32[]{:S(2)}, u32[]{:S(2)}) collective-permute-start(bf16[2,2,3,160,128]{4,3,2,1,0:T(8,128)(2,1)S(1)} %bitcast.22), channel_id=1, source_target_pairs={{0,128},{16,400},{64,192},{80,464},{128,256},{144,16},{192,320},{2... | collective-permute-start | bytes 1474568 | tf_op jit(solution)/shard_map/ppermute | solution.py:394
  13.3 21.0 %collective-permute-start.1 = (bf16[1056,128]{1,0:T(8,128)(2,1)}, bf16[1056,128]{1,0:T(8,128)(2,1)S(1)}, u32[]{:S(2)}, u32[]{:S(2)}) collective-permute-start(bf16[1056,128]{1,0:T(8,128)(2,1)} %pack.1), channel_id=1, source_target_pairs={{0,32},{32,0},{1,33},{33,1},{2,34},{34,2},{3,35},{35,3},{4,36},{36... | collective-permute-start | bytes 811016 | tf_op jit(solution)/shard_map/ppermute | solution.py:405
  22.5 15.3 %collective-permute-start.4 = (bf16[2,2,3,160,128]{4,3,2,1,0:T(8,128)(2,1)S(1)}, bf16[2,2,3,160,128]{4,3,2,1,0:T(8,128)(2,1)S(1)}, u32[]{:S(2)}, u32[]{:S(2)}) collective-permute-start(bf16[2,2,3,160,128]{4,3,2,1,0:T(8,128)(2,1)S(1)} %bitcast.23), channel_id=1, source_target_pairs={{0,64},{16,464},{64,128},{80,16},{128,192},{144,80},{192,256},{208... | collective-permute-start | bytes 1474568 | tf_op jit(solution)/shard_map/ppermute | solution.py:394
  27.9 18.4 %collective-permute-start.2 = (bf16[2,2,3,160,128]{4,3,2,1,0:T(8,128)(2,1)S(1)}, bf16[2,2,3,160,128]{4,3,2,1,0:T(8,128)(2,1)S(1)}, u32[]{:S(2)}, u32[]{:S(2)}) collective-permute-start(bf16[2,2,3,160,128]{4,3,2,1,0:T(8,128)(2,1)S(1)} %collective-permute-done.b2_ref), channel_id=1, source_target_pairs={{0,64},{16,464},{64,128},{80,16},{128,192},{144,80},{192,256},{208... | collective-permute-start | bytes 1474568 | tf_op jit(solution)/shard_map/ppermute | solution.py:394
  31.0 15.3 %collective-permute-start.3 = (bf16[2,3,160,128]{3,2,1,0:T(8,128)(2,1)S(1)}, bf16[2,3,160,128]{3,2,1,0:T(8,128)(2,1)S(1)}, u32[]{:S(2)}, u32[]{:S(2)}) collective-permute-start(bf16[2,3,160,128]{3,2,1,0:T(8,128)(2,1)S(1)} %dynamic-slice_bitcast_fusion), channel_id=1, source_target_pairs={{0,128},{16,400},{64,192},{80,464},{128,256},{144,16},{192,320},{2... | collective-permute-start | bytes 737288 | tf_op jit(solution)/shard_map/ppermute | solution.py:394
  39.6 24.7 %collective-permute-start.8 = (bf16[12,16,1536]{2,1,0:T(8,128)(2,1)S(1)}, bf16[12,16,1536]{2,1,0:T(8,128)(2,1)S(1)}, u32[]{:S(2)}, u32[]{:S(2)}) collective-permute-start(bf16[12,16,1536]{2,1,0:T(8,128)(2,1)S(1)} %get-tuple-element.44.w0_ref), channel_id=1, source_target_pairs={{0,128},{16,400},{64,192},{80,464},{128,256},{144,16},{192,320},{2... | collective-permute-start | bytes 1769480 | tf_op jit(solution)/shard_map/ppermute | solution.py:394
  47.2 3.4 %collective-permute-start.5 = (bf16[2,512,128]{2,1,0:T(8,128)(2,1)S(1)}, bf16[2,512,128]{2,1,0:T(8,128)(2,1)S(1)}, u32[]{:S(2)}, u32[]{:S(2)}) collective-permute-start(bf16[2,512,128]{2,1,0:T(8,128)(2,1)S(1)} %get-tuple-element.41), channel_id=1, source_target_pairs={{0,16},{16,0},{1,17},{17,1},{2,18},{18,2},{3,19},{19,3},{4,20},{20... | collective-permute-start | bytes 786440 | tf_op jit(solution)/shard_map/ppermute | solution.py:418
  51.2 18.4 %collective-permute-start.6 = (bf16[512,128]{1,0:T(8,128)(2,1)S(1)}, bf16[512,128]{1,0:T(8,128)(2,1)S(1)}, u32[]{:S(2)}, u32[]{:S(2)}) collective-permute-start(bf16[512,128]{1,0:T(8,128)(2,1)S(1)} %get-tuple-element.43), channel_id=1, source_target_pairs={{0,32},{32,0},{1,33},{33,1},{2,34},{34,2},{3,35},{35,3},{4,36},{36... | collective-permute-start | bytes 393224 | tf_op jit(solution)/shard_map/ppermute | solution.py:419
  58.4 27.2 %collective-permute-start.7 = (bf16[12,16,1536]{2,1,0:T(8,128)(2,1)S(1)}, bf16[12,16,1536]{2,1,0:T(8,128)(2,1)S(1)}, u32[]{:S(2)}, u32[]{:S(2)}) collective-permute-start(bf16[12,16,1536]{2,1,0:T(8,128)(2,1)S(1)} %get-tuple-element.44.w0_ref), channel_id=1, source_target_pairs={{0,64},{16,464},{64,128},{80,16},{128,192},{144,80},{192,256},{208... | collective-permute-start | bytes 1769480 | tf_op jit(solution)/shard_map/ppermute | solution.py:394
  64.3 21.2 %collective-permute-start.10 = (bf16[12,16,1536]{2,1,0:T(8,128)(2,1)S(1)}, bf16[12,16,1536]{2,1,0:T(8,128)(2,1)S(1)}, u32[]{:S(2)}, u32[]{:S(2)}) collective-permute-start(bf16[12,16,1536]{2,1,0:T(8,128)(2,1)S(1)} %collective-permute-done.8.w2_ref), channel_id=1, source_target_pairs={{16,400},{80,464},{144,16},{208,80},{272,144},{336,208},{400,272},... | collective-permute-start | bytes 1769480 | tf_op jit(solution)/shard_map/ppermute | solution.py:421
  67.7 22.4 %collective-permute-start.9 = (bf16[12,16,1536]{2,1,0:T(8,128)(2,1)S(1)}, bf16[12,16,1536]{2,1,0:T(8,128)(2,1)S(1)}, u32[]{:S(2)}, u32[]{:S(2)}) collective-permute-start(bf16[12,16,1536]{2,1,0:T(8,128)(2,1)S(1)} %collective-permute-done.8.w2_ref), channel_id=1, source_target_pairs={{0,64},{16,464},{64,128},{80,16},{128,192},{144,80},{192,256},{208... | collective-permute-start | bytes 1769480 | tf_op jit(solution)/shard_map/ppermute | solution.py:394
  91.9 3.8 %collective-permute-start.11 = (bf16[160,1536]{1,0:T(8,128)(2,1)S(1)}, bf16[160,1536]{1,0:T(8,128)(2,1)S(1)}, u32[]{:S(2)}, u32[]{:S(2)}) collective-permute-start(bf16[160,1536]{1,0:T(8,128)(2,1)S(1)} %get-tuple-element.46), channel_id=1, source_target_pairs={{0,16},{16,0},{1,17},{17,1},{2,18},{18,2},{3,19},{19,3},{4,20},{20... | collective-permute-start | bytes 1474568 | tf_op jit(solution)/shard_map/ppermute | solution.py:427
  96.5 4.2 %copy-start = (f32[1536]{0:T(1024)S(1)}, f32[1536]{0:T(1024)}, u32[]{:S(2)}) copy-start(f32[1536]{0:T(1024)} %param.9) | copy-start | bytes 18436
  96.5 13.0 %all-to-all-start = ((bf16[4,40,1536]{2,1,0:T(8,128)(2,1)}), bf16[4,40,1536]{2,1,0:T(8,128)(2,1)S(1)}, u32[]{:S(2)}, u32[]{:S(2)}) async-start(bf16[4,40,1536]{2,1,0:T(8,128)(2,1)} %bitcast.14), calls=%async_computation | async-start | bytes 983040 | tf_op jit(solution)/shard_map/all_to_all | solution.py:430

commit v5 on v4

--- a/solution.py
+++ b/solution.py
@@ -23,28 +23,22 @@
     return high, mid, rest - mid
 
 
-def first_state(m_ref, l_ref, acc_ref, h):
-    m_ref[h] = jnp.full(m_ref.shape[1:], LOW, jnp.float32)
-    l_ref[h] = jnp.zeros(l_ref.shape[1:], jnp.float32)
-    acc_ref[h] = jnp.zeros(acc_ref.shape[1:], jnp.float32)
-
-
-def attend_block(m_ref, l_ref, acc_ref, h, scale2, query, keys, values, allowed=None):
+def attend_block(state, scale2, query, keys, values, seen, allowed=None):
     scores = lax.dot_general(keys, query, (((1,), (1,)), ((), ())), preferred_element_type=jnp.float32)
-    scores = scores * scale2
     if allowed is not None:
         scores = jnp.where(allowed, scores, LOW)
-    old = m_ref[h]
-    new = jnp.maximum(old, jnp.max(scores, axis=0, keepdims=True))
-    weights = jnp.exp2(scores - new)
-    if allowed is not None:
-        weights = jnp.where(allowed, weights, 0.0)
-    fade = jnp.exp2(old - new)
-    m_ref[h] = new
-    l_ref[h] = l_ref[h] * fade + jnp.sum(weights, axis=0, keepdims=True)
-    acc_ref[h] = acc_ref[h] * fade + lax.dot_general(
+    top = jnp.where(seen, jnp.max(scores, axis=0, keepdims=True) * scale2, LOW)
+    new = top if state is None else jnp.maximum(state[0], top)
+    shift = jnp.where(jnp.logical_and(new > 0.5 * LOW, seen), new, -LOW)
+    weights = jnp.exp2(scores * scale2 - shift)
+    total = jnp.sum(weights, axis=0, keepdims=True)
+    sums = lax.dot_general(
         values, weights.astype(jnp.bfloat16), (((0,), (0,)), ((), ())), preferred_element_type=jnp.float32
     )
+    if state is None:
+        return new, total, sums
+    fade = jnp.exp2(state[0] - new)
+    return new, state[1] * fade + total, state[2] * fade + sums
 
 
 def chip_block(ref, h):
@@ -93,6 +87,7 @@
 def unpack_kernel(heads, rows, deep, idx_ref, own_ref, far_ref, query_ref, w_ref):
     first = idx_ref[1] == 0
     w_heads, _, wide = w_ref.shape
+    turn = jnp.where(idx_ref[2] == 0, w_heads // 2, 0)
 
     def lines(at, count):
         near = [own_ref[core, at : at + count] for core in range(2)]
@@ -109,7 +104,7 @@
             tile = [x.astype(jnp.float32) for x in lines(heads * rows + (g * tiles + t) * 16, 16)]
             for k in range(group):
                 piece = jnp.concatenate([x[k * deep : (k + 1) * deep] for x in tile], axis=0).astype(jnp.bfloat16)
-                w_ref[g * group + k, :, t * 128 : (t + 1) * 128] = piece
+                w_ref[(g * group + k + turn) % w_heads, :, t * 128 : (t + 1) * 128] = piece
 
 
 def unpack(idx, own, far, heads, rows, w_shape):
@@ -132,23 +127,19 @@
     y, zh, c = idx_ref[0], idx_ref[1], idx_ref[2]
     query_pos = lax.broadcasted_iota(jnp.int32, (1, 4 * rows), 1)
     key_pos = (zh * 2 + c) * rows + lax.broadcasted_iota(jnp.int32, (rows, 1), 0)
-    allowed = key_pos <= query_pos
-    for h in range(heads):
-        first_state(m_ref, l_ref, acc_ref, h)
-    for h in range(heads):
-        attend_block(m_ref, l_ref, acc_ref, h, scale2, q_ref[h], own_ref[0, h], own_ref[1, h], allowed)
-    for distance, block_ref in ((1, b1_ref), (2, b2_ref)):
-
-        @pl.when(source_of(idx_ref, ring, distance) < y)
-        def _():
-            for h in range(heads):
-                attend_block(m_ref, l_ref, acc_ref, h, scale2, q_ref[h], *chip_block(block_ref, h))
-
-
-def far_kernel(
-    rows, heads, ring, scale2, idx_ref, q_ref, b3_ref, b4_ref, m_in, l_in, acc_in,
-    keep_ref, send_ref, m_ref, l_ref, acc_ref,
-):
+    own_seen = query_pos >= (zh * 2 + c) * rows
+    for h in range(heads):
+        query = q_ref[h]
+        state = attend_block(
+            None, scale2, query, own_ref[0, h], own_ref[1, h], own_seen, key_pos <= query_pos
+        )
+        for distance, block_ref in ((1, b1_ref), (2, b2_ref)):
+            seen = source_of(idx_ref, ring, distance) < y
+            state = attend_block(state, scale2, query, *chip_block(block_ref, h), seen)
+        m_ref[h], l_ref[h], acc_ref[h] = state
+
+
+def far_kernel(rows, heads, ring, scale2, idx_ref, q_ref, b3_ref, b4_ref, m_ref, l_ref, acc_ref, keep_ref, send_ref):
     y, zh, c = idx_ref[0], idx_ref[1], idx_ref[2]
 
     def put(z, at, first, second):
@@ -156,30 +147,21 @@
         keep_ref[place, at : at + first.shape[0]] = jnp.where(c == 0, first, second)
         send_ref[place, at : at + first.shape[0]] = jnp.where(c == 0, second, first)
 
-    m_ref[...] = m_in[...]
-    l_ref[...] = l_in[...]
-    acc_ref[...] = acc_in[...]
-
-    @pl.when(source_of(idx_ref, ring, 3) < y)
-    def _():
-        for h in range(heads):
-            attend_block(m_ref, l_ref, acc_ref, h, scale2, q_ref[h], *chip_block(b3_ref, h))
-
-    @pl.when(source_of(idx_ref, ring, 4) < y)
-    def _():
-        for h in range(heads):
-            attend_block(m_ref, l_ref, acc_ref, h, scale2, q_ref[h], b4_ref[0, h], b4_ref[1, h])
-
     line = lax.broadcasted_iota(jnp.int32, (16, 4 * rows), 0)
     plane = jnp.zeros((16, 4 * rows), jnp.float32)
     for h in range(heads):
-        total = l_ref[h]
+        query = q_ref[h]
+        state = m_ref[h], l_ref[h], acc_ref[h]
+        seen = source_of(idx_ref, ring, 4) < y
+        state = attend_block(state, scale2, query, b4_ref[0, h], b4_ref[1, h], seen)
+        seen = source_of(idx_ref, ring, 3) < y
+        most, total, sums = attend_block(state, scale2, query, *chip_block(b3_ref, h), seen)
         seen = total > 0.0
         safe = jnp.where(seen, total, 1.0)
-        low = jnp.transpose(acc_ref[h] * (1.0 / safe)).astype(jnp.bfloat16)
+        low = jnp.transpose(sums * (1.0 / safe)).astype(jnp.bfloat16)
         for z in range(2):
             put(z, h * rows, low[2 * z * rows : (2 * z + 1) * rows], low[(2 * z + 1) * rows : (2 * z + 2) * rows])
-        log = jnp.where(seen, m_ref[h] + jnp.log2(safe), LOW)
+        log = jnp.where(seen, most + jnp.log2(safe), LOW)
         for part, piece in enumerate(split3(log)):
             plane = jnp.where(line == 3 * h + part, piece, plane)
     plane = jnp.concatenate([plane, jnp.zeros((16, 128), jnp.float32)], axis=1)
@@ -224,7 +206,6 @@
         out_shape=(out, out),
         in_specs=[SMEM] + [VMEM] * 6,
         out_specs=(VMEM, VMEM),
-        scratch_shapes=state_shapes(heads, rows, size, pltpu.VMEM),
         compiler_params=PARAMS,
         cost_estimate=pl.CostEstimate(
             flops=16 * rows * keys * size * heads, bytes_accessed=4 << 20, transcendentals=4 * rows * keys * heads
@@ -300,35 +281,31 @@
     deep = w0_ref.shape[1]
     line = lax.broadcasted_iota(jnp.int32, (size, size), 0)
     lane = lax.broadcasted_iota(jnp.int32, (size, size), 1)
-    sources = [jnp.where(c == 0, y, (y + 4) % ring)]
-    for hops in (1, 2, 3):
-        sources.append(jnp.where(c == 0, (y + ring - hops) % ring, (y + hops) % ring))
-    moves = []
-    for side in range(2):
-        wanted = jnp.full((size, size), -1, jnp.int32)
-        for slot, source in enumerate(sources):
-            at = side * size // 2 + slot * deep
-            inside = jnp.logical_and(lane >= at, lane < at + deep)
-            wanted = jnp.where(inside, lane + (source * deep - at), wanted)
-        moves.append(jnp.where(line == wanted, 1.0, 0.0).astype(jnp.bfloat16))
+    sources = [jnp.where(c == 0, (y + ring - hops) % ring, (y + hops) % ring) for hops in (1, 2, 3)]
     lefts, rights = [], []
     for h in range(0, heads, 2):
+        opposite = h < heads // 2
+        if h % (heads // 2) == 0:
+            moves = []
+            for side in range(2):
+                wanted = jnp.full((size, size), -1, jnp.int32)
+                for slot, source in enumerate([(y + 4) % ring if opposite else y] + sources):
+                    at = side * size // 2 + slot * deep
+                    inside = jnp.logical_and(lane >= at, lane < at + deep)
+                    wanted = jnp.where(inside, lane + (source * deep - at), wanted)
+                moves.append(jnp.where(line == wanted, 1.0, 0.0).astype(jnp.bfloat16))
         left = None
         for side in range(2):
-            columns = jnp.concatenate([att_ref[core, h + side] for core in range(cores)], axis=0)
+            place = (h + side + jnp.where(c == 0, heads // 2, 0)) % heads
+            columns = jnp.concatenate([att_ref[core, place] for core in range(cores)], axis=0)
             moved = jnp.dot(columns, moves[side], preferred_element_type=jnp.float32)
             left = moved if left is None else left + moved
-            rights.append((w0_ref, w4_ref, h + side))
-            rights += [(ref, None, h + side) for ref in (w1_ref, w2_ref, w3_ref)]
+            rights += [(ref, h + side) for ref in (w4_ref if opposite else w0_ref, w1_ref, w2_ref, w3_ref)]
         lefts.append(left.astype(jnp.bfloat16))
     left = jnp.concatenate(lefts, axis=1)
-    wide = w0_ref.shape[2]
-    for at in range(0, wide, 256):
-        pieces = []
-        for ref, other, h in rights:
-            piece = ref[h, :, at : at + 256]
-            pieces.append(piece if other is None else jnp.where(c == 0, piece, other[h, :, at : at + 256]))
-        total = jnp.dot(left, jnp.concatenate(pieces, axis=0), preferred_element_type=jnp.float32)
+    for at in range(0, w0_ref.shape[2], 256):
+        right = jnp.concatenate([ref[h, :, at : at + 256] for ref, h in rights], axis=0)
+        total = jnp.dot(left, right, preferred_element_type=jnp.float32)
         first, second = total[:rows], total[rows:]
         keep_ref[:, at : at + 256] = jnp.where(c == 0, first, second)
         send_ref[:, at : at + 256] = jnp.where(c == 0, second, first).astype(jnp.bfloat16)
@@ -418,7 +395,7 @@
     keep, send = merge_core(keep, lax.ppermute(send, "c", swap), heads)
     other = lax.ppermute(send, "zh", swap)
     w3 = onward(w2, 1)
-    w4 = lax.ppermute(w2, ("y", "c"), [(2 * at + 1, 2 * ((at - 2) % ring) + 1) for at in range(ring)])
+    w4 = onward(w2[: w2.shape[0] // 2], 2)
     attended = merge_far(keep, other, heads)
     attended = attended.reshape(heads, rows, size)
     attended = lax.all_gather(attended, "col", axis=0, tiled=True)

time: 111 us -> 109 us (0.982)
  waiting for transfers between devices: 18.1 us -> 12.9 us
  Pallas kernels: 9.48 us -> 14.5 us
  starting transfers between devices: 52 us -> 47.1 us
  blocking collectives: 29.3 us -> 32.1 us
    ppermute x7 -> x8, waiting for transfers between devices: 4.62 us -> 0.02 us  [onward(): return lax.ppermute(block, ('y', 'c'), pairs)]
    ppermute x1 -> x0, starting transfers between devices: 3.34 us -> none  [on_device(): lax.ppermute(w2, ('y', 'c'), [(2 * at + 1, 2 * ((at - 2) % ring) + 1) for...]
    pallas_call x1, Pallas kernels: 1.77 us -> 4.35 us  [attend_near(): pl.pallas_call(functools.partial(near_kernel, rows, heads, ring, scale2),...]
    all_gather x1, blocking collectives: 2.5 us -> 4.96 us  [on_device(): attended = lax.all_gather(attended, 'c', axis=0)]
    pallas_call x1, Pallas kernels: 0.91 us -> 3.29 us  [attend_far(): pl.pallas_call(functools.partial(far_kernel, rows, heads, ring, scale2),...]
    ppermute x1, starting transfers between devices: 7.17 us -> 5.49 us  [on_device(): other = lax.ppermute(send, 'zh', swap)]
    ppermute x7 -> x8, starting transfers between devices: 24.3 us -> 24.1 us  [onward(): return lax.ppermute(block, ('y', 'c'), pairs)]
  transfers between devices with their start and end apart: 13 -> 13, of which waited for: 5 -> 4; matrix products, arithmetic and copies ran while one was open for 0% -> 0% of each run, Pallas kernels for 6% -> 10%
where the time goes in v5:
time: 109 us; the launch traced here: 108 us
  starting transfers between devices  47.1 us (43%)
  blocking collectives  32.1 us (29%)
  Pallas kernels  14.5 us (13%)
  waiting for transfers between devices  12.9 us (12%)
    ppermute x8, starting transfers between devices, onward(): return lax.ppermute(block, ('y', 'c'), pairs)  24.1 us
    all_gather x1, blocking collectives, on_device(): attended = lax.all_gather(attended, 'col', axis=0, tiled=True)  13.3 us
    ppermute x1, starting transfers between devices, on_device(): qw_far = lax.ppermute(qw, 'zh', swap)  9.21 us
    all_gather x1, blocking collectives, on_device(): chip = lax.all_gather(own, 'c', axis=0)  8.66 us
    all_to_all x1, waiting for transfers between devices, on_device(): pieces = lax.all_to_all(pieces, 'row', 0, 0, tiled=True)  8.56 us
    ppermute x1, starting transfers between devices, on_device(): other = lax.ppermute(send, 'zh', swap)  5.49 us
    all_gather x1, blocking collectives, on_device(): attended = lax.all_gather(attended, 'c', axis=0)  4.96 us
    pallas_call x1, Pallas kernels, attend_near(): pl.pallas_call(functools.partial(near_kernel, rows, heads, ring, scale2),...  4.35 us
  transfers between devices with their start and end apart: 13, of which 4 were waited for; matrix products, arithmetic and copies ran while one was open for 0% of the time, Pallas kernels for 10%

profile of v5, /device:TPU:1, one launch (start us, length us, event | category | flops | bytes accessed | tf_op | source)
XLA Modules:
  0.0 107.9 jit_solution(1789315652806929570)
XLA Ops:
  0.0 1.0 pad_maximum_fusion.own_ref
  1.0 8.7 %all-gather = bf16[4,3,160,128]{3,2,1,0:T(8,128)(2,1)S(1)} all-gather(bf16[2,3,160,128]{3,2,1,0:T(8,128)(2,1)S(1)} %pad_maximum_fusion.own_ref), channel_id=2, replica_groups=mesh['y'=8,'zh'=2,'c'=2,'row'=4,'col'=4] {'c'}, dimensions={0}, use_global_device_ids=true | all-gather | bytes 737280 | tf_op jit(solution)/shard_map/all_gather | solution.py:376
  9.7 1.9 %collective-permute-start = (bf16[2,2,3,160,128]{4,3,2,1,0:T(8,128)(2,1)S(1)}, bf16[2,2,3,160,128]{4,3,2,1,0:T(8,128)(2,1)S(1)}, u32[]{:S(2)}, u32[]{:S(2)}) collective-permute-start(bf16[2,2,3,160,128]{4,3,2,1,0:T(8,128)(2,1)S(1)} %bitcast.22), channel_id=1, source_target_pairs={{0,128},{16,400},{64,192},{80,464},{128,256},{144,16},{192,320},{2... | collective-permute-start | bytes 1474568 | tf_op jit(solution)/shard_map/ppermute | solution.py:371
  11.6 1.7 %pack.1 = bf16[1056,128]{1,0:T(8,128)(2,1)} custom-call(bf16[3,160,128]{2,1,0:T(8,128)(2,1)} %bitcast.24, bf16[12,4,1536]{2,1,0:T(4,128)(2,1)} %w_ref), custom_call_target="tpu_custom_call" | custom-call | tf_op jit(solution)/shard_map/pack/pallas_call | solution.py:76
  13.3 9.2 %collective-permute-start.1 = (bf16[1056,128]{1,0:T(8,128)(2,1)}, bf16[1056,128]{1,0:T(8,128)(2,1)S(1)}, u32[]{:S(2)}, u32[]{:S(2)}) collective-permute-start(bf16[1056,128]{1,0:T(8,128)(2,1)} %pack.1), channel_id=1, source_target_pairs={{0,32},{32,0},{1,33},{33,1},{2,34},{34,2},{3,35},{35,3},{4,36},{36... | collective-permute-start | bytes 811016 | tf_op jit(solution)/shard_map/ppermute | solution.py:382
  22.5 3.0 %collective-permute-start.4 = (bf16[2,2,3,160,128]{4,3,2,1,0:T(8,128)(2,1)S(1)}, bf16[2,2,3,160,128]{4,3,2,1,0:T(8,128)(2,1)S(1)}, u32[]{:S(2)}, u32[]{:S(2)}) collective-permute-start(bf16[2,2,3,160,128]{4,3,2,1,0:T(8,128)(2,1)S(1)} %bitcast.23), channel_id=1, source_target_pairs={{0,64},{16,464},{64,128},{80,16},{128,192},{144,80},{192,256},{208... | collective-permute-start | bytes 1474568 | tf_op jit(solution)/shard_map/ppermute | solution.py:371
  25.5 2.4 %all-gather.1 = bf16[2112,128]{1,0:T(8,128)(2,1)S(1)} all-gather(bf16[1056,128]{1,0:T(8,128)(2,1)} %pack.1), channel_id=3, replica_groups=mesh['y'=8,'zh'=2,'c'=2,'row'=4,'col'=4] {'c'}, dimensions={0}, use_global_device_ids=true | all-gather | bytes 811008 | tf_op jit(solution)/shard_map/all_gather | solution.py:383
  27.9 0.0 collective-permute-done.b2_ref
  27.9 3.0 %collective-permute-start.2 = (bf16[2,2,3,160,128]{4,3,2,1,0:T(8,128)(2,1)S(1)}, bf16[2,2,3,160,128]{4,3,2,1,0:T(8,128)(2,1)S(1)}, u32[]{:S(2)}, u32[]{:S(2)}) collective-permute-start(bf16[2,2,3,160,128]{4,3,2,1,0:T(8,128)(2,1)S(1)} %collective-permute-done.b2_ref), channel_id=1, source_target_pairs={{0,64},{16,464},{64,128},{80,16},{128,192},{144,80},{192,256},{208... | collective-permute-start | bytes 1474568 | tf_op jit(solution)/shard_map/ppermute | solution.py:371
  30.9 0.1 pad_add_fusion.idx_ref
  31.0 2.0 %collective-permute-start.3 = (bf16[2,3,160,128]{3,2,1,0:T(8,128)(2,1)S(1)}, bf16[2,3,160,128]{3,2,1,0:T(8,128)(2,1)S(1)}, u32[]{:S(2)}, u32[]{:S(2)}) collective-permute-start(bf16[2,3,160,128]{3,2,1,0:T(8,128)(2,1)S(1)} %dynamic-slice_bitcast_fusion), channel_id=1, source_target_pairs={{0,128},{16,400},{64,192},{80,464},{128,256},{144,16},{192,320},{2... | collective-permute-start | bytes 737288 | tf_op jit(solution)/shard_map/ppermute | solution.py:371
  32.9 1.4 %collective-permute-done.1 = bf16[1056,128]{1,0:T(8,128)(2,1)S(1)} collective-permute-done((bf16[1056,128]{1,0:T(8,128)(2,1)}, bf16[1056,128]{1,0:T(8,128)(2,1)S(1)}, u32[]{:S(2)}, u32[]{:S(2)}) %collective-permute-start.1) | collective-permute-done | bytes 270368 | tf_op jit(solution)/shard_map/ppermute | solution.py:382
  34.3 2.7 %all-gather.2 = bf16[2112,128]{1,0:T(8,128)(2,1)S(1)} all-gather(bf16[1056,128]{1,0:T(8,128)(2,1)S(1)} %collective-permute-done.1), channel_id=4, replica_groups=mesh['y'=8,'zh'=2,'c'=2,'row'=4,'col'=4] {'c'}, dimensions={0}, use_global_device_ids=true | all-gather | bytes 811008 | tf_op jit(solution)/shard_map/all_gather | solution.py:384
  37.0 0.8 unpack.1
  37.9 0.0 collective-permute-done.4.b1_ref
  37.9 4.3 %attend_near.1 = (f32[3,1,640]{2,1,0:T(1,128)S(1)}, f32[3,1,640]{2,1,0:T(1,128)S(1)}, f32[3,128,640]{2,1,0:T(8,128)S(1)}) custom-call(s32[3]{0:T(128)S(1)} %pad_add_fusion.idx_ref, bf16[3,640,128]{2,1,0:T(8,128)(2,1)S(1)} %get-tuple-element.30.q_ref, bf16[2,3,160,128]{3,2,1,0:T(8,128)(2,1)S(1)} %pad_maximum_fusion.own_ref, ...), custom_call_target="tpu_custom_call" | custom-call | flops 268435456 | bytes 262144 | tf_op jit(solution)/shard_map/attend_near/pallas_call | solution.py:188
  42.2 5.0 %collective-permute-start.8 = (bf16[12,16,1536]{2,1,0:T(8,128)(2,1)S(1)}, bf16[12,16,1536]{2,1,0:T(8,128)(2,1)S(1)}, u32[]{:S(2)}, u32[]{:S(2)}) collective-permute-start(bf16[12,16,1536]{2,1,0:T(8,128)(2,1)S(1)} %get-tuple-element.44.w0_ref), channel_id=1, source_target_pairs={{0,128},{16,400},{64,192},{80,464},{128,256},{144,16},{192,320},{2... | collective-permute-start | bytes 1769480 | tf_op jit(solution)/shard_map/ppermute | solution.py:371
  47.2 0.0 collective-permute-done.3.b4_ref
  47.2 0.0 collective-permute-done.2.b3_ref
  47.2 3.3 %attend_far.1 = (bf16[2,512,128]{2,1,0:T(8,128)(2,1)S(1)}, bf16[2,512,128]{2,1,0:T(8,128)(2,1)S(1)}) custom-call(s32[3]{0:T(128)S(1)} %pad_add_fusion.idx_ref, bf16[3,640,128]{2,1,0:T(8,128)(2,1)S(1)} %get-tuple-element.30.q_ref, bf16[2,2,3,160,128]{4,3,2,1,0:T(8,128)(2,1)S(1)} %collective-permute-done.2.b3_ref, ...), custom_call_target="tpu_custom_call" | custom-call | flops 471859200 | bytes 4194304 | tf_op jit(solution)/shard_map/attend_far/pallas_call | solution.py:204
  50.5 1.9 %collective-permute-start.5 = (bf16[2,512,128]{2,1,0:T(8,128)(2,1)S(1)}, bf16[2,512,128]{2,1,0:T(8,128)(2,1)S(1)}, u32[]{:S(2)}, u32[]{:S(2)}) collective-permute-start(bf16[2,512,128]{2,1,0:T(8,128)(2,1)S(1)} %get-tuple-element.41), channel_id=1, source_target_pairs={{0,16},{16,0},{1,17},{17,1},{2,18},{18,2},{3,19},{19,3},{4,20},{20... | collective-permute-start | bytes 786440 | tf_op jit(solution)/shard_map/ppermute | solution.py:395
  52.5 1.5 %collective-permute-done.5.b_ref = bf16[2,512,128]{2,1,0:T(8,128)(2,1)S(1)} collective-permute-done((bf16[2,512,128]{2,1,0:T(8,128)(2,1)S(1)}, bf16[2,512,128]{2,1,0:T(8,128)(2,1)S(1)}, u32[]{:S(2)}, u32[]{:S(2)}) %collective-permute-start.5) | collective-permute-done | bytes 262176 | tf_op jit(solution)/shard_map/ppermute | solution.py:395
  54.0 0.5 merge_core.1
  54.5 5.5 %collective-permute-start.6 = (bf16[512,128]{1,0:T(8,128)(2,1)S(1)}, bf16[512,128]{1,0:T(8,128)(2,1)S(1)}, u32[]{:S(2)}, u32[]{:S(2)}) collective-permute-start(bf16[512,128]{1,0:T(8,128)(2,1)S(1)} %get-tuple-element.43), channel_id=1, source_target_pairs={{0,32},{32,0},{1,33},{33,1},{2,34},{34,2},{3,35},{35,3},{4,36},{36... | collective-permute-start | bytes 393224 | tf_op jit(solution)/shard_map/ppermute | solution.py:396
  60.0 4.9 %collective-permute-start.7 = (bf16[12,16,1536]{2,1,0:T(8,128)(2,1)S(1)}, bf16[12,16,1536]{2,1,0:T(8,128)(2,1)S(1)}, u32[]{:S(2)}, u32[]{:S(2)}) collective-permute-start(bf16[12,16,1536]{2,1,0:T(8,128)(2,1)S(1)} %get-tuple-element.44.w0_ref), channel_id=1, source_target_pairs={{0,64},{16,464},{64,128},{80,16},{128,192},{144,80},{192,256},{208... | collective-permute-start | bytes 1769480 | tf_op jit(solution)/shard_map/ppermute | solution.py:371
  64.9 0.0 collective-permute-done.8.w2_ref
  64.9 2.3 %collective-permute-start.10 = (bf16[6,16,1536]{2,1,0:T(8,128)(2,1)S(1)}, bf16[6,16,1536]{2,1,0:T(8,128)(2,1)S(1)}, u32[]{:S(2)}, u32[]{:S(2)}) collective-permute-start(bf16[6,16,1536]{2,1,0:T(8,128)(2,1)S(1)} %slice.4), channel_id=1, source_target_pairs={{0,128},{16,400},{64,192},{80,464},{128,256},{144,16},{192,320},{2... | collective-permute-start | bytes 884744 | tf_op jit(solution)/shard_map/ppermute | solution.py:371
  67.2 2.1 %collective-permute-start.9 = (bf16[12,16,1536]{2,1,0:T(8,128)(2,1)S(1)}, bf16[12,16,1536]{2,1,0:T(8,128)(2,1)S(1)}, u32[]{:S(2)}, u32[]{:S(2)}) collective-permute-start(bf16[12,16,1536]{2,1,0:T(8,128)(2,1)S(1)} %collective-permute-done.8.w2_ref), channel_id=1, source_target_pairs={{0,64},{16,464},{64,128},{80,16},{128,192},{144,80},{192,256},{208... | collective-permute-start | bytes 1769480 | tf_op jit(solution)/shard_map/ppermute | solution.py:371
  69.4 0.0 collective-permute-done.6.b_ref
  69.4 0.4 merge_far.1
  69.8 13.3 %all_gather.33 = bf16[12,160,128]{2,1,0:T(8,128)(2,1)S(1)} all-gather(bf16[3,160,128]{2,1,0:T(8,128)(2,1)S(1)} %bitcast.21), channel_id=1, replica_groups=mesh['y'=8,'zh'=2,'c'=2,'row'=4,'col'=4] {'col'}, dimensions={0}, use_global_device_ids=true | all-gather | bytes 614400 | tf_op jit(solution)/shard_map/all_gather | solution.py:401
  83.1 5.0 %all-gather.3 = bf16[24,160,128]{2,1,0:T(8,128)(2,1)S(1)} all-gather(bf16[12,160,128]{2,1,0:T(8,128)(2,1)S(1)} %all_gather.33), channel_id=5, replica_groups=mesh['y'=8,'zh'=2,'c'=2,'row'=4,'col'=4] {'c'}, dimensions={0}, use_global_device_ids=true | all-gather | bytes 1474560 | tf_op jit(solution)/shard_map/all_gather | solution.py:402
  88.1 0.0 collective-permute-done.7.w1_ref
  88.1 0.0 collective-permute-done.10.w4_ref
  88.1 0.0 collective-permute-done.9.w3_ref
  88.1 1.8 %project.1 = (f32[160,1536]{1,0:T(8,128)S(1)}, bf16[160,1536]{1,0:T(8,128)(2,1)S(1)}) custom-call(s32[3]{0:T(128)S(1)} %pad_add_fusion.idx_ref, bf16[2,12,160,128]{3,2,1,0:T(8,128)(2,1)S(1)} %bitcast.18, bf16[12,16,1536]{2,1,0:T(8,128)(2,1)S(1)} %get-tuple-element.44.w0_ref, bf16[12,16,1536]{2,1,0:T(8,128)(2,1)S(1)} %collective-permute-done.7.w1_ref, ...), custom_call_target="tpu_custom_call" | custom-call | tf_op jit(solution)/shard_map/project/pallas_call | solution.py:317
  89.9 2.3 %collective-permute-start.11 = (bf16[160,1536]{1,0:T(8,128)(2,1)S(1)}, bf16[160,1536]{1,0:T(8,128)(2,1)S(1)}, u32[]{:S(2)}, u32[]{:S(2)}) collective-permute-start(bf16[160,1536]{1,0:T(8,128)(2,1)S(1)} %get-tuple-element.46), channel_id=1, source_target_pairs={{0,16},{16,0},{1,17},{17,1},{2,18},{18,2},{3,19},{19,3},{4,20},{20... | collective-permute-start | bytes 1474568 | tf_op jit(solution)/shard_map/ppermute | solution.py:404
  92.1 1.5 %collective-permute-done.11.other_ref = bf16[160,1536]{1,0:T(8,128)(2,1)S(1)} collective-permute-done((bf16[160,1536]{1,0:T(8,128)(2,1)S(1)}, bf16[160,1536]{1,0:T(8,128)(2,1)S(1)}, u32[]{:S(2)}, u32[]{:S(2)}) %collective-permute-start.11) | collective-permute-done | bytes 491552 | tf_op jit(solution)/shard_map/ppermute | solution.py:404
  93.6 0.9 join.1
  94.5 0.0 copy-start
  94.5 4.1 %all-to-all-start = ((bf16[4,40,1536]{2,1,0:T(8,128)(2,1)}), bf16[4,40,1536]{2,1,0:T(8,128)(2,1)S(1)}, u32[]{:S(2)}, u32[]{:S(2)}) async-start(bf16[4,40,1536]{2,1,0:T(8,128)(2,1)} %bitcast.14), calls=%async_computation | async-start | bytes 983040 | tf_op jit(solution)/shard_map/all_to_all | solution.py:407
  98.6 0.0 copy-done
  98.6 8.6 %all-to-all-done.pieces_ref = bf16[4,40,1536]{2,1,0:T(8,128)(2,1)S(1)} async-done(((bf16[4,40,1536]{2,1,0:T(8,128)(2,1)}), bf16[4,40,1536]{2,1,0:T(8,128)(2,1)S(1)}, u32[]{:S(2)}, u32[]{:S(2)}) %all-to-all-start) | async-done | bytes 491552 | tf_op jit(solution)/shard_map/all_to_all | solution.py:407
  107.2 0.7 finish.1
  (3 shorter events, 0.0 us)
Async XLA Ops:
  9.7 18.2 %collective-permute-start = (bf16[2,2,3,160,128]{4,3,2,1,0:T(8,128)(2,1)S(1)}, bf16[2,2,3,160,128]{4,3,2,1,0:T(8,128)(2,1)S(1)}, u32[]{:S(2)}, u32[]{:S(2)}) collective-permute-start(bf16[2,2,3,160,128]{4,3,2,1,0:T(8,128)(2,1)S(1)} %bitcast.22), channel_id=1, source_target_pairs={{0,128},{16,400},{64,192},{80,464},{128,256},{144,16},{192,320},{2... | collective-permute-start | bytes 1474568 | tf_op jit(solution)/shard_map/ppermute | solution.py:371
  13.3 21.0 %collective-permute-start.1 = (bf16[1056,128]{1,0:T(8,128)(2,1)}, bf16[1056,128]{1,0:T(8,128)(2,1)S(1)}, u32[]{:S(2)}, u32[]{:S(2)}) collective-permute-start(bf16[1056,128]{1,0:T(8,128)(2,1)} %pack.1), channel_id=1, source_target_pairs={{0,32},{32,0},{1,33},{33,1},{2,34},{34,2},{3,35},{35,3},{4,36},{36... | collective-permute-start | bytes 811016 | tf_op jit(solution)/shard_map/ppermute | solution.py:382
  22.5 15.3 %collective-permute-start.4 = (bf16[2,2,3,160,128]{4,3,2,1,0:T(8,128)(2,1)S(1)}, bf16[2,2,3,160,128]{4,3,2,1,0:T(8,128)(2,1)S(1)}, u32[]{:S(2)}, u32[]{:S(2)}) collective-permute-start(bf16[2,2,3,160,128]{4,3,2,1,0:T(8,128)(2,1)S(1)} %bitcast.23), channel_id=1, source_target_pairs={{0,64},{16,464},{64,128},{80,16},{128,192},{144,80},{192,256},{208... | collective-permute-start | bytes 1474568 | tf_op jit(solution)/shard_map/ppermute | solution.py:371
  27.9 19.3 %collective-permute-start.2 = (bf16[2,2,3,160,128]{4,3,2,1,0:T(8,128)(2,1)S(1)}, bf16[2,2,3,160,128]{4,3,2,1,0:T(8,128)(2,1)S(1)}, u32[]{:S(2)}, u32[]{:S(2)}) collective-permute-start(bf16[2,2,3,160,128]{4,3,2,1,0:T(8,128)(2,1)S(1)} %collective-permute-done.b2_ref), channel_id=1, source_target_pairs={{0,64},{16,464},{64,128},{80,16},{128,192},{144,80},{192,256},{208... | collective-permute-start | bytes 1474568 | tf_op jit(solution)/shard_map/ppermute | solution.py:371
  31.0 16.2 %collective-permute-start.3 = (bf16[2,3,160,128]{3,2,1,0:T(8,128)(2,1)S(1)}, bf16[2,3,160,128]{3,2,1,0:T(8,128)(2,1)S(1)}, u32[]{:S(2)}, u32[]{:S(2)}) collective-permute-start(bf16[2,3,160,128]{3,2,1,0:T(8,128)(2,1)S(1)} %dynamic-slice_bitcast_fusion), channel_id=1, source_target_pairs={{0,128},{16,400},{64,192},{80,464},{128,256},{144,16},{192,320},{2... | collective-permute-start | bytes 737288 | tf_op jit(solution)/shard_map/ppermute | solution.py:371
  42.2 22.6 %collective-permute-start.8 = (bf16[12,16,1536]{2,1,0:T(8,128)(2,1)S(1)}, bf16[12,16,1536]{2,1,0:T(8,128)(2,1)S(1)}, u32[]{:S(2)}, u32[]{:S(2)}) collective-permute-start(bf16[12,16,1536]{2,1,0:T(8,128)(2,1)S(1)} %get-tuple-element.44.w0_ref), channel_id=1, source_target_pairs={{0,128},{16,400},{64,192},{80,464},{128,256},{144,16},{192,320},{2... | collective-permute-start | bytes 1769480 | tf_op jit(solution)/shard_map/ppermute | solution.py:371
  50.5 3.4 %collective-permute-start.5 = (bf16[2,512,128]{2,1,0:T(8,128)(2,1)S(1)}, bf16[2,512,128]{2,1,0:T(8,128)(2,1)S(1)}, u32[]{:S(2)}, u32[]{:S(2)}) collective-permute-start(bf16[2,512,128]{2,1,0:T(8,128)(2,1)S(1)} %get-tuple-element.41), channel_id=1, source_target_pairs={{0,16},{16,0},{1,17},{17,1},{2,18},{18,2},{3,19},{19,3},{4,20},{20... | collective-permute-start | bytes 786440 | tf_op jit(solution)/shard_map/ppermute | solution.py:395
  54.5 14.9 %collective-permute-start.6 = (bf16[512,128]{1,0:T(8,128)(2,1)S(1)}, bf16[512,128]{1,0:T(8,128)(2,1)S(1)}, u32[]{:S(2)}, u32[]{:S(2)}) collective-permute-start(bf16[512,128]{1,0:T(8,128)(2,1)S(1)} %get-tuple-element.43), channel_id=1, source_target_pairs={{0,32},{32,0},{1,33},{33,1},{2,34},{34,2},{3,35},{35,3},{4,36},{36... | collective-permute-start | bytes 393224 | tf_op jit(solution)/shard_map/ppermute | solution.py:396
  60.0 28.1 %collective-permute-start.7 = (bf16[12,16,1536]{2,1,0:T(8,128)(2,1)S(1)}, bf16[12,16,1536]{2,1,0:T(8,128)(2,1)S(1)}, u32[]{:S(2)}, u32[]{:S(2)}) collective-permute-start(bf16[12,16,1536]{2,1,0:T(8,128)(2,1)S(1)} %get-tuple-element.44.w0_ref), channel_id=1, source_target_pairs={{0,64},{16,464},{64,128},{80,16},{128,192},{144,80},{192,256},{208... | collective-permute-start | bytes 1769480 | tf_op jit(solution)/shard_map/ppermute | solution.py:371
  64.9 23.2 %collective-permute-start.10 = (bf16[6,16,1536]{2,1,0:T(8,128)(2,1)S(1)}, bf16[6,16,1536]{2,1,0:T(8,128)(2,1)S(1)}, u32[]{:S(2)}, u32[]{:S(2)}) collective-permute-start(bf16[6,16,1536]{2,1,0:T(8,128)(2,1)S(1)} %slice.4), channel_id=1, source_target_pairs={{0,128},{16,400},{64,192},{80,464},{128,256},{144,16},{192,320},{2... | collective-permute-start | bytes 884744 | tf_op jit(solution)/shard_map/ppermute | solution.py:371
  67.2 20.9 %collective-permute-start.9 = (bf16[12,16,1536]{2,1,0:T(8,128)(2,1)S(1)}, bf16[12,16,1536]{2,1,0:T(8,128)(2,1)S(1)}, u32[]{:S(2)}, u32[]{:S(2)}) collective-permute-start(bf16[12,16,1536]{2,1,0:T(8,128)(2,1)S(1)} %collective-permute-done.8.w2_ref), channel_id=1, source_target_pairs={{0,64},{16,464},{64,128},{80,16},{128,192},{144,80},{192,256},{208... | collective-permute-start | bytes 1769480 | tf_op jit(solution)/shard_map/ppermute | solution.py:371
  89.9 3.8 %collective-permute-start.11 = (bf16[160,1536]{1,0:T(8,128)(2,1)S(1)}, bf16[160,1536]{1,0:T(8,128)(2,1)S(1)}, u32[]{:S(2)}, u32[]{:S(2)}) collective-permute-start(bf16[160,1536]{1,0:T(8,128)(2,1)S(1)} %get-tuple-element.46), channel_id=1, source_target_pairs={{0,16},{16,0},{1,17},{17,1},{2,18},{18,2},{3,19},{19,3},{4,20},{20... | collective-permute-start | bytes 1474568 | tf_op jit(solution)/shard_map/ppermute | solution.py:404
  94.5 4.1 %copy-start = (f32[1536]{0:T(1024)S(1)}, f32[1536]{0:T(1024)}, u32[]{:S(2)}) copy-start(f32[1536]{0:T(1024)} %param.9) | copy-start | bytes 18436
  94.5 12.7 %all-to-all-start = ((bf16[4,40,1536]{2,1,0:T(8,128)(2,1)}), bf16[4,40,1536]{2,1,0:T(8,128)(2,1)S(1)}, u32[]{:S(2)}, u32[]{:S(2)}) async-start(bf16[4,40,1536]{2,1,0:T(8,128)(2,1)} %bitcast.14), calls=%async_computation | async-start | bytes 983040 | tf_op jit(solution)/shard_map/all_to_all | solution.py:407

commit v6 on v5

--- a/solution.py
+++ b/solution.py
@@ -207,9 +207,7 @@
         in_specs=[SMEM] + [VMEM] * 6,
         out_specs=(VMEM, VMEM),
         compiler_params=PARAMS,
-        cost_estimate=pl.CostEstimate(
-            flops=16 * rows * keys * size * heads, bytes_accessed=4 << 20, transcendentals=4 * rows * keys * heads
-        ),
+        cost_estimate=pl.CostEstimate(flops=1 << 31, bytes_accessed=1 << 18, transcendentals=0),
         name="attend_far",
     )(idx, query, b3, b4, *state)
 
@@ -240,26 +238,27 @@
         out_ref[at + 16 : at + 32] = low[:, 128:]
 
 
-def merge_core_kernel(rows, heads, a_ref, b_ref, keep_ref, send_ref):
-    merge_two(rows, heads, a_ref[1], b_ref[1], send_ref, False)
-    merge_two(rows, heads, a_ref[0], b_ref[0], keep_ref, False)
+def merge_core_kernel(rows, heads, idx_ref, a_ref, b_ref, keep_ref, send_ref):
+    other = 1 - idx_ref[2]
+    merge_two(rows, heads, a_ref[1], b_ref[other, 1], send_ref, False)
+    merge_two(rows, heads, a_ref[0], b_ref[other, 0], keep_ref, False)
 
 
 def merge_far_kernel(rows, heads, a_ref, b_ref, out_ref):
     merge_two(rows, heads, a_ref[...], b_ref[...], out_ref, True)
 
 
-def merge_core(keep, other, heads):
+def merge_core(idx, keep, both, heads):
     _, lines, size = keep.shape
     out = jax.ShapeDtypeStruct((lines, size), jnp.bfloat16)
     return pl.pallas_call(
         functools.partial(merge_core_kernel, (lines - 32) // heads, heads),
         out_shape=(out, out),
-        in_specs=[VMEM, VMEM],
+        in_specs=[SMEM, VMEM, VMEM],
         out_specs=(VMEM, VMEM),
         compiler_params=PARAMS,
         name="merge_core",
-    )(keep, other)
+    )(idx, keep, both)
 
 
 def merge_far(keep, other, heads):
@@ -324,19 +323,19 @@
     )(idx, attended, *weights)
 
 
-def join_kernel(keep_ref, other_ref, out_ref):
-    out_ref[...] = (keep_ref[...] + other_ref[...].astype(jnp.float32)).astype(jnp.bfloat16)
-
-
-def join(keep, other):
+def join_kernel(idx_ref, keep_ref, both_ref, out_ref):
+    out_ref[...] = (keep_ref[...] + both_ref[1 - idx_ref[2]].astype(jnp.float32)).astype(jnp.bfloat16)
+
+
+def join(idx, keep, both):
     return pl.pallas_call(
         join_kernel,
-        out_shape=jax.ShapeDtypeStruct(other.shape, jnp.bfloat16),
-        in_specs=[VMEM, VMEM],
+        out_shape=jax.ShapeDtypeStruct(both.shape[1:], jnp.bfloat16),
+        in_specs=[SMEM, VMEM, VMEM],
         out_specs=VMEM,
         compiler_params=PARAMS,
         name="join",
-    )(keep, other)
+    )(idx, keep, both)
 
 
 def finish_kernel(pieces_ref, bias_ref, out_ref):
@@ -392,7 +391,7 @@
     w2 = onward(weight, 2)
     w1 = onward(weight, 1)
     keep, send = attend_far(idx, query, b3, b4, state, ring)
-    keep, send = merge_core(keep, lax.ppermute(send, "c", swap), heads)
+    keep, send = merge_core(idx, keep, lax.all_gather(send, "c", axis=0), heads)
     other = lax.ppermute(send, "zh", swap)
     w3 = onward(w2, 1)
     w4 = onward(w2[: w2.shape[0] // 2], 2)
@@ -401,7 +400,7 @@
     attended = lax.all_gather(attended, "col", axis=0, tiled=True)
     attended = lax.all_gather(attended, "c", axis=0)
     keep, send = project(idx, attended, (weight, w1, w2, w3, w4), ring)
-    joined = join(keep, lax.ppermute(send, "c", swap))
+    joined = join(idx, keep, lax.all_gather(send, "c", axis=0))
     parts = lax.axis_size("row")
     pieces = joined.reshape(parts, rows // parts, joined.shape[1])
     pieces = lax.all_to_all(pieces, "row", 0, 0, tiled=True)

time: 109 us -> 107 us (0.982)
  blocking collectives: 32.1 us -> 36.8 us
  starting transfers between devices: 47.1 us -> 42.9 us
  waiting for transfers between devices: 12.9 us -> 9.95 us
    all_gather x0 -> x2, blocking collectives: none -> 4.7 us  [the longest x1 2.52 us: on_device(): joined = join(idx, keep, lax.all_gather(send, 'c', axis=0))]
    ppermute x2 -> x0, starting transfers between devices: 4.2 us -> none  [the longest x1 2.28 us: on_device(): joined = join(keep, lax.ppermute(send, 'c', swap))]
    ppermute x2 -> x0, waiting for transfers between devices: 2.97 us -> none  [the longest x1 1.5 us: on_device(): keep, send = merge_core(keep, lax.ppermute(send, 'c', swap), heads)]
  transfers between devices with their start and end apart: 13 -> 11, of which waited for: 4 -> 2; matrix products, arithmetic and copies ran while one was open for 0% -> 0% of each run, Pallas kernels for 10% -> 11%
where the time goes in v6:
time: 107 us; the launch traced here: 106 us
  starting transfers between devices  42.9 us (40%)
  blocking collectives  36.8 us (34%)
  Pallas kernels  15.5 us (14%)
  waiting for transfers between devices  9.95 us (9%)
    ppermute x8, starting transfers between devices, onward(): return lax.ppermute(block, ('y', 'c'), pairs)  24.1 us
    all_gather x1, blocking collectives, on_device(): attended = lax.all_gather(attended, 'col', axis=0, tiled=True)  13.3 us
    ppermute x1, starting transfers between devices, on_device(): qw_far = lax.ppermute(qw, 'zh', swap)  9.21 us
    all_gather x1, blocking collectives, on_device(): chip = lax.all_gather(own, 'c', axis=0)  8.66 us
    all_to_all x1, waiting for transfers between devices, on_device(): pieces = lax.all_to_all(pieces, 'row', 0, 0, tiled=True)  8.55 us
    ppermute x1, starting transfers between devices, on_device(): other = lax.ppermute(send, 'zh', swap)  5.5 us
    all_gather x1, blocking collectives, on_device(): attended = lax.all_gather(attended, 'c', axis=0)  4.96 us
    pallas_call x1, Pallas kernels, attend_near(): pl.pallas_call(functools.partial(near_kernel, rows, heads, ring, scale2),...  4.35 us
  transfers between devices with their start and end apart: 11, of which 2 were waited for; matrix products, arithmetic and copies ran while one was open for 0% of the time, Pallas kernels for 11%

profile of v6, /device:TPU:1, one launch (start us, length us, event | category | flops | bytes accessed | tf_op | source)
XLA Modules:
  0.0 106.5 jit_solution(17156720444585482548)
XLA Ops:
  0.0 1.0 pad_maximum_fusion.own_ref
  1.0 8.7 %all-gather = bf16[4,3,160,128]{3,2,1,0:T(8,128)(2,1)S(1)} all-gather(bf16[2,3,160,128]{3,2,1,0:T(8,128)(2,1)S(1)} %pad_maximum_fusion.own_ref), channel_id=2, replica_groups=mesh['y'=8,'zh'=2,'c'=2,'row'=4,'col'=4] {'c'}, dimensions={0}, use_global_device_ids=true | all-gather | bytes 737280 | tf_op jit(solution)/shard_map/all_gather | solution.py:375
  9.7 1.9 %collective-permute-start = (bf16[2,2,3,160,128]{4,3,2,1,0:T(8,128)(2,1)S(1)}, bf16[2,2,3,160,128]{4,3,2,1,0:T(8,128)(2,1)S(1)}, u32[]{:S(2)}, u32[]{:S(2)}) collective-permute-start(bf16[2,2,3,160,128]{4,3,2,1,0:T(8,128)(2,1)S(1)} %bitcast.26), channel_id=1, source_target_pairs={{0,128},{16,400},{64,192},{80,464},{128,256},{144,16},{192,320},{2... | collective-permute-start | bytes 1474568 | tf_op jit(solution)/shard_map/ppermute | solution.py:370
  11.6 1.7 %pack.1 = bf16[1056,128]{1,0:T(8,128)(2,1)} custom-call(bf16[3,160,128]{2,1,0:T(8,128)(2,1)} %bitcast.28, bf16[12,4,1536]{2,1,0:T(4,128)(2,1)} %w_ref), custom_call_target="tpu_custom_call" | custom-call | tf_op jit(solution)/shard_map/pack/pallas_call | solution.py:76
  13.3 9.2 %collective-permute-start.1 = (bf16[1056,128]{1,0:T(8,128)(2,1)}, bf16[1056,128]{1,0:T(8,128)(2,1)S(1)}, u32[]{:S(2)}, u32[]{:S(2)}) collective-permute-start(bf16[1056,128]{1,0:T(8,128)(2,1)} %pack.1), channel_id=1, source_target_pairs={{0,32},{32,0},{1,33},{33,1},{2,34},{34,2},{3,35},{35,3},{4,36},{36... | collective-permute-start | bytes 811016 | tf_op jit(solution)/shard_map/ppermute | solution.py:381
  22.5 3.0 %collective-permute-start.4 = (bf16[2,2,3,160,128]{4,3,2,1,0:T(8,128)(2,1)S(1)}, bf16[2,2,3,160,128]{4,3,2,1,0:T(8,128)(2,1)S(1)}, u32[]{:S(2)}, u32[]{:S(2)}) collective-permute-start(bf16[2,2,3,160,128]{4,3,2,1,0:T(8,128)(2,1)S(1)} %bitcast.27), channel_id=1, source_target_pairs={{0,64},{16,464},{64,128},{80,16},{128,192},{144,80},{192,256},{208... | collective-permute-start | bytes 1474568 | tf_op jit(solution)/shard_map/ppermute | solution.py:370
  25.5 2.4 %all-gather.1 = bf16[2112,128]{1,0:T(8,128)(2,1)S(1)} all-gather(bf16[1056,128]{1,0:T(8,128)(2,1)} %pack.1), channel_id=3, replica_groups=mesh['y'=8,'zh'=2,'c'=2,'row'=4,'col'=4] {'c'}, dimensions={0}, use_global_device_ids=true | all-gather | bytes 811008 | tf_op jit(solution)/shard_map/all_gather | solution.py:382
  27.9 0.0 collective-permute-done.b2_ref
  27.9 3.0 %collective-permute-start.2 = (bf16[2,2,3,160,128]{4,3,2,1,0:T(8,128)(2,1)S(1)}, bf16[2,2,3,160,128]{4,3,2,1,0:T(8,128)(2,1)S(1)}, u32[]{:S(2)}, u32[]{:S(2)}) collective-permute-start(bf16[2,2,3,160,128]{4,3,2,1,0:T(8,128)(2,1)S(1)} %collective-permute-done.b2_ref), channel_id=1, source_target_pairs={{0,64},{16,464},{64,128},{80,16},{128,192},{144,80},{192,256},{208... | collective-permute-start | bytes 1474568 | tf_op jit(solution)/shard_map/ppermute | solution.py:370
  30.9 0.1 pad_add_fusion.idx_ref
  31.0 2.0 %collective-permute-start.3 = (bf16[2,3,160,128]{3,2,1,0:T(8,128)(2,1)S(1)}, bf16[2,3,160,128]{3,2,1,0:T(8,128)(2,1)S(1)}, u32[]{:S(2)}, u32[]{:S(2)}) collective-permute-start(bf16[2,3,160,128]{3,2,1,0:T(8,128)(2,1)S(1)} %dynamic-slice_bitcast_fusion), channel_id=1, source_target_pairs={{0,128},{16,400},{64,192},{80,464},{128,256},{144,16},{192,320},{2... | collective-permute-start | bytes 737288 | tf_op jit(solution)/shard_map/ppermute | solution.py:370
  32.9 1.4 %collective-permute-done.1 = bf16[1056,128]{1,0:T(8,128)(2,1)S(1)} collective-permute-done((bf16[1056,128]{1,0:T(8,128)(2,1)}, bf16[1056,128]{1,0:T(8,128)(2,1)S(1)}, u32[]{:S(2)}, u32[]{:S(2)}) %collective-permute-start.1) | collective-permute-done | bytes 270368 | tf_op jit(solution)/shard_map/ppermute | solution.py:381
  34.3 2.7 %all-gather.2 = bf16[2112,128]{1,0:T(8,128)(2,1)S(1)} all-gather(bf16[1056,128]{1,0:T(8,128)(2,1)S(1)} %collective-permute-done.1), channel_id=4, replica_groups=mesh['y'=8,'zh'=2,'c'=2,'row'=4,'col'=4] {'c'}, dimensions={0}, use_global_device_ids=true | all-gather | bytes 811008 | tf_op jit(solution)/shard_map/all_gather | solution.py:383
  37.0 0.8 unpack.1
  37.8 0.0 collective-permute-done.4.b1_ref
  37.9 4.3 %attend_near.1 = (f32[3,1,640]{2,1,0:T(1,128)S(1)}, f32[3,1,640]{2,1,0:T(1,128)S(1)}, f32[3,128,640]{2,1,0:T(8,128)S(1)}) custom-call(s32[3]{0:T(128)S(1)} %pad_add_fusion.idx_ref, bf16[3,640,128]{2,1,0:T(8,128)(2,1)S(1)} %get-tuple-element.30.q_ref, bf16[2,3,160,128]{3,2,1,0:T(8,128)(2,1)S(1)} %pad_maximum_fusion.own_ref, ...), custom_call_target="tpu_custom_call" | custom-call | flops 268435456 | bytes 262144 | tf_op jit(solution)/shard_map/attend_near/pallas_call | solution.py:188
  42.2 5.0 %collective-permute-start.7 = (bf16[12,16,1536]{2,1,0:T(8,128)(2,1)S(1)}, bf16[12,16,1536]{2,1,0:T(8,128)(2,1)S(1)}, u32[]{:S(2)}, u32[]{:S(2)}) collective-permute-start(bf16[12,16,1536]{2,1,0:T(8,128)(2,1)S(1)} %get-tuple-element.44.w0_ref), channel_id=1, source_target_pairs={{0,128},{16,400},{64,192},{80,464},{128,256},{144,16},{192,320},{2... | collective-permute-start | bytes 1769480 | tf_op jit(solution)/shard_map/ppermute | solution.py:370
  47.2 0.0 collective-permute-done.3.b4_ref
  47.2 0.0 collective-permute-done.2.b3_ref
  47.2 3.3 %attend_far.1 = (bf16[2,512,128]{2,1,0:T(8,128)(2,1)S(1)}, bf16[2,512,128]{2,1,0:T(8,128)(2,1)S(1)}) custom-call(s32[3]{0:T(128)S(1)} %pad_add_fusion.idx_ref, bf16[3,640,128]{2,1,0:T(8,128)(2,1)S(1)} %get-tuple-element.30.q_ref, bf16[2,2,3,160,128]{4,3,2,1,0:T(8,128)(2,1)S(1)} %collective-permute-done.2.b3_ref, ...), custom_call_target="tpu_custom_call" | custom-call | flops 2147483648 | bytes 262144 | tf_op jit(solution)/shard_map/attend_far/pallas_call | solution.py:204
  50.5 2.2 %all-gather.3 = bf16[4,512,128]{2,1,0:T(8,128)(2,1)S(1)} all-gather(bf16[2,512,128]{2,1,0:T(8,128)(2,1)S(1)} %get-tuple-element.41), channel_id=5, replica_groups=mesh['y'=8,'zh'=2,'c'=2,'row'=4,'col'=4] {'c'}, dimensions={0}, use_global_device_ids=true | all-gather | bytes 786432 | tf_op jit(solution)/shard_map/all_gather | solution.py:394
  52.7 1.1 %merge_core.1 = (bf16[512,128]{1,0:T(8,128)(2,1)S(1)}, bf16[512,128]{1,0:T(8,128)(2,1)S(1)}) custom-call(s32[3]{0:T(128)S(1)} %pad_add_fusion.idx_ref, bf16[2,512,128]{2,1,0:T(8,128)(2,1)S(1)} %get-tuple-element.40.a_ref, bf16[2,2,512,128]{3,2,1,0:T(8,128)(2,1)S(1)} %bitcast.24), custom_call_target="tpu_custom_call" | custom-call | tf_op jit(solution)/shard_map/merge_core/pallas_call | solution.py:254
  53.8 5.5 %collective-permute-start.5 = (bf16[512,128]{1,0:T(8,128)(2,1)S(1)}, bf16[512,128]{1,0:T(8,128)(2,1)S(1)}, u32[]{:S(2)}, u32[]{:S(2)}) collective-permute-start(bf16[512,128]{1,0:T(8,128)(2,1)S(1)} %get-tuple-element.43), channel_id=1, source_target_pairs={{0,32},{32,0},{1,33},{33,1},{2,34},{34,2},{3,35},{35,3},{4,36},{36... | collective-permute-start | bytes 393224 | tf_op jit(solution)/shard_map/ppermute | solution.py:395
  59.3 4.9 %collective-permute-start.6 = (bf16[12,16,1536]{2,1,0:T(8,128)(2,1)S(1)}, bf16[12,16,1536]{2,1,0:T(8,128)(2,1)S(1)}, u32[]{:S(2)}, u32[]{:S(2)}) collective-permute-start(bf16[12,16,1536]{2,1,0:T(8,128)(2,1)S(1)} %get-tuple-element.44.w0_ref), channel_id=1, source_target_pairs={{0,64},{16,464},{64,128},{80,16},{128,192},{144,80},{192,256},{208... | collective-permute-start | bytes 1769480 | tf_op jit(solution)/shard_map/ppermute | solution.py:370
  64.2 0.0 collective-permute-done.7.w2_ref
  64.2 2.3 %collective-permute-start.9 = (bf16[6,16,1536]{2,1,0:T(8,128)(2,1)S(1)}, bf16[6,16,1536]{2,1,0:T(8,128)(2,1)S(1)}, u32[]{:S(2)}, u32[]{:S(2)}) collective-permute-start(bf16[6,16,1536]{2,1,0:T(8,128)(2,1)S(1)} %slice.4), channel_id=1, source_target_pairs={{0,128},{16,400},{64,192},{80,464},{128,256},{144,16},{192,320},{2... | collective-permute-start | bytes 884744 | tf_op jit(solution)/shard_map/ppermute | solution.py:370
  66.5 2.1 %collective-permute-start.8 = (bf16[12,16,1536]{2,1,0:T(8,128)(2,1)S(1)}, bf16[12,16,1536]{2,1,0:T(8,128)(2,1)S(1)}, u32[]{:S(2)}, u32[]{:S(2)}) collective-permute-start(bf16[12,16,1536]{2,1,0:T(8,128)(2,1)S(1)} %collective-permute-done.7.w2_ref), channel_id=1, source_target_pairs={{0,64},{16,464},{64,128},{80,16},{128,192},{144,80},{192,256},{208... | collective-permute-start | bytes 1769480 | tf_op jit(solution)/shard_map/ppermute | solution.py:370
  68.7 0.0 collective-permute-done.5.b_ref
  68.7 0.4 merge_far.1
  69.1 13.3 %all_gather.47 = bf16[12,160,128]{2,1,0:T(8,128)(2,1)S(1)} all-gather(bf16[3,160,128]{2,1,0:T(8,128)(2,1)S(1)} %bitcast.25), channel_id=1, replica_groups=mesh['y'=8,'zh'=2,'c'=2,'row'=4,'col'=4] {'col'}, dimensions={0}, use_global_device_ids=true | all-gather | bytes 614400 | tf_op jit(solution)/shard_map/all_gather | solution.py:400
  82.4 5.0 %all-gather.4 = bf16[24,160,128]{2,1,0:T(8,128)(2,1)S(1)} all-gather(bf16[12,160,128]{2,1,0:T(8,128)(2,1)S(1)} %all_gather.47), channel_id=6, replica_groups=mesh['y'=8,'zh'=2,'c'=2,'row'=4,'col'=4] {'c'}, dimensions={0}, use_global_device_ids=true | all-gather | bytes 1474560 | tf_op jit(solution)/shard_map/all_gather | solution.py:401
  87.4 0.0 collective-permute-done.6.w1_ref
  87.4 0.0 collective-permute-done.9.w4_ref
  87.4 0.0 collective-permute-done.8.w3_ref
  87.4 1.8 %project.1 = (f32[160,1536]{1,0:T(8,128)S(1)}, bf16[160,1536]{1,0:T(8,128)(2,1)S(1)}) custom-call(s32[3]{0:T(128)S(1)} %pad_add_fusion.idx_ref, bf16[2,12,160,128]{3,2,1,0:T(8,128)(2,1)S(1)} %bitcast.21, bf16[12,16,1536]{2,1,0:T(8,128)(2,1)S(1)} %get-tuple-element.44.w0_ref, bf16[12,16,1536]{2,1,0:T(8,128)(2,1)S(1)} %collective-permute-done.6.w1_ref, ...), custom_call_target="tpu_custom_call" | custom-call | tf_op jit(solution)/shard_map/project/pallas_call | solution.py:316
  89.1 2.5 %all-gather.5 = bf16[320,1536]{1,0:T(8,128)(2,1)S(1)} all-gather(bf16[160,1536]{1,0:T(8,128)(2,1)S(1)} %get-tuple-element.46), channel_id=7, replica_groups=mesh['y'=8,'zh'=2,'c'=2,'row'=4,'col'=4] {'c'}, dimensions={0}, use_global_device_ids=true | all-gather | bytes 1474560 | tf_op jit(solution)/shard_map/all_gather | solution.py:403
  91.7 1.4 %join.1 = bf16[160,1536]{1,0:T(8,128)(2,1)} custom-call(s32[3]{0:T(128)S(1)} %pad_add_fusion.idx_ref, f32[160,1536]{1,0:T(8,128)S(1)} %get-tuple-element.45.keep_ref, bf16[2,160,1536]{2,1,0:T(8,128)(2,1)S(1)} %bitcast.20), custom_call_target="tpu_custom_call" | custom-call | tf_op jit(solution)/shard_map/join/pallas_call | solution.py:331
  93.1 0.0 copy-start
  93.1 4.1 %all-to-all-start = ((bf16[4,40,1536]{2,1,0:T(8,128)(2,1)}), bf16[4,40,1536]{2,1,0:T(8,128)(2,1)S(1)}, u32[]{:S(2)}, u32[]{:S(2)}) async-start(bf16[4,40,1536]{2,1,0:T(8,128)(2,1)} %bitcast.16), calls=%async_computation | async-start | bytes 983040 | tf_op jit(solution)/shard_map/all_to_all | solution.py:406
  97.2 0.0 copy-done
  97.2 8.5 %all-to-all-done.pieces_ref = bf16[4,40,1536]{2,1,0:T(8,128)(2,1)S(1)} async-done(((bf16[4,40,1536]{2,1,0:T(8,128)(2,1)}), bf16[4,40,1536]{2,1,0:T(8,128)(2,1)S(1)}, u32[]{:S(2)}, u32[]{:S(2)}) %all-to-all-start) | async-done | bytes 491552 | tf_op jit(solution)/shard_map/all_to_all | solution.py:406
  105.8 0.7 finish.1
  (3 shorter events, 0.0 us)
Async XLA Ops:
  9.7 18.2 %collective-permute-start = (bf16[2,2,3,160,128]{4,3,2,1,0:T(8,128)(2,1)S(1)}, bf16[2,2,3,160,128]{4,3,2,1,0:T(8,128)(2,1)S(1)}, u32[]{:S(2)}, u32[]{:S(2)}) collective-permute-start(bf16[2,2,3,160,128]{4,3,2,1,0:T(8,128)(2,1)S(1)} %bitcast.26), channel_id=1, source_target_pairs={{0,128},{16,400},{64,192},{80,464},{128,256},{144,16},{192,320},{2... | collective-permute-start | bytes 1474568 | tf_op jit(solution)/shard_map/ppermute | solution.py:370
  13.3 21.0 %collective-permute-start.1 = (bf16[1056,128]{1,0:T(8,128)(2,1)}, bf16[1056,128]{1,0:T(8,128)(2,1)S(1)}, u32[]{:S(2)}, u32[]{:S(2)}) collective-permute-start(bf16[1056,128]{1,0:T(8,128)(2,1)} %pack.1), channel_id=1, source_target_pairs={{0,32},{32,0},{1,33},{33,1},{2,34},{34,2},{3,35},{35,3},{4,36},{36... | collective-permute-start | bytes 811016 | tf_op jit(solution)/shard_map/ppermute | solution.py:381
  22.5 15.3 %collective-permute-start.4 = (bf16[2,2,3,160,128]{4,3,2,1,0:T(8,128)(2,1)S(1)}, bf16[2,2,3,160,128]{4,3,2,1,0:T(8,128)(2,1)S(1)}, u32[]{:S(2)}, u32[]{:S(2)}) collective-permute-start(bf16[2,2,3,160,128]{4,3,2,1,0:T(8,128)(2,1)S(1)} %bitcast.27), channel_id=1, source_target_pairs={{0,64},{16,464},{64,128},{80,16},{128,192},{144,80},{192,256},{208... | collective-permute-start | bytes 1474568 | tf_op jit(solution)/shard_map/ppermute | solution.py:370
  27.9 19.3 %collective-permute-start.2 = (bf16[2,2,3,160,128]{4,3,2,1,0:T(8,128)(2,1)S(1)}, bf16[2,2,3,160,128]{4,3,2,1,0:T(8,128)(2,1)S(1)}, u32[]{:S(2)}, u32[]{:S(2)}) collective-permute-start(bf16[2,2,3,160,128]{4,3,2,1,0:T(8,128)(2,1)S(1)} %collective-permute-done.b2_ref), channel_id=1, source_target_pairs={{0,64},{16,464},{64,128},{80,16},{128,192},{144,80},{192,256},{208... | collective-permute-start | bytes 1474568 | tf_op jit(solution)/shard_map/ppermute | solution.py:370
  31.0 16.2 %collective-permute-start.3 = (bf16[2,3,160,128]{3,2,1,0:T(8,128)(2,1)S(1)}, bf16[2,3,160,128]{3,2,1,0:T(8,128)(2,1)S(1)}, u32[]{:S(2)}, u32[]{:S(2)}) collective-permute-start(bf16[2,3,160,128]{3,2,1,0:T(8,128)(2,1)S(1)} %dynamic-slice_bitcast_fusion), channel_id=1, source_target_pairs={{0,128},{16,400},{64,192},{80,464},{128,256},{144,16},{192,320},{2... | collective-permute-start | bytes 737288 | tf_op jit(solution)/shard_map/ppermute | solution.py:370
  42.2 22.0 %collective-permute-start.7 = (bf16[12,16,1536]{2,1,0:T(8,128)(2,1)S(1)}, bf16[12,16,1536]{2,1,0:T(8,128)(2,1)S(1)}, u32[]{:S(2)}, u32[]{:S(2)}) collective-permute-start(bf16[12,16,1536]{2,1,0:T(8,128)(2,1)S(1)} %get-tuple-element.44.w0_ref), channel_id=1, source_target_pairs={{0,128},{16,400},{64,192},{80,464},{128,256},{144,16},{192,320},{2... | collective-permute-start | bytes 1769480 | tf_op jit(solution)/shard_map/ppermute | solution.py:370
  53.8 14.9 %collective-permute-start.5 = (bf16[512,128]{1,0:T(8,128)(2,1)S(1)}, bf16[512,128]{1,0:T(8,128)(2,1)S(1)}, u32[]{:S(2)}, u32[]{:S(2)}) collective-permute-start(bf16[512,128]{1,0:T(8,128)(2,1)S(1)} %get-tuple-element.43), channel_id=1, source_target_pairs={{0,32},{32,0},{1,33},{33,1},{2,34},{34,2},{3,35},{35,3},{4,36},{36... | collective-permute-start | bytes 393224 | tf_op jit(solution)/shard_map/ppermute | solution.py:395
  59.3 28.1 %collective-permute-start.6 = (bf16[12,16,1536]{2,1,0:T(8,128)(2,1)S(1)}, bf16[12,16,1536]{2,1,0:T(8,128)(2,1)S(1)}, u32[]{:S(2)}, u32[]{:S(2)}) collective-permute-start(bf16[12,16,1536]{2,1,0:T(8,128)(2,1)S(1)} %get-tuple-element.44.w0_ref), channel_id=1, source_target_pairs={{0,64},{16,464},{64,128},{80,16},{128,192},{144,80},{192,256},{208... | collective-permute-start | bytes 1769480 | tf_op jit(solution)/shard_map/ppermute | solution.py:370
  64.2 23.2 %collective-permute-start.9 = (bf16[6,16,1536]{2,1,0:T(8,128)(2,1)S(1)}, bf16[6,16,1536]{2,1,0:T(8,128)(2,1)S(1)}, u32[]{:S(2)}, u32[]{:S(2)}) collective-permute-start(bf16[6,16,1536]{2,1,0:T(8,128)(2,1)S(1)} %slice.4), channel_id=1, source_target_pairs={{0,128},{16,400},{64,192},{80,464},{128,256},{144,16},{192,320},{2... | collective-permute-start | bytes 884744 | tf_op jit(solution)/shard_map/ppermute | solution.py:370
  66.5 20.9 %collective-permute-start.8 = (bf16[12,16,1536]{2,1,0:T(8,128)(2,1)S(1)}, bf16[12,16,1536]{2,1,0:T(8,128)(2,1)S(1)}, u32[]{:S(2)}, u32[]{:S(2)}) collective-permute-start(bf16[12,16,1536]{2,1,0:T(8,128)(2,1)S(1)} %collective-permute-done.7.w2_ref), channel_id=1, source_target_pairs={{0,64},{16,464},{64,128},{80,16},{128,192},{144,80},{192,256},{208... | collective-permute-start | bytes 1769480 | tf_op jit(solution)/shard_map/ppermute | solution.py:370
  93.1 4.1 %copy-start = (f32[1536]{0:T(1024)S(1)}, f32[1536]{0:T(1024)}, u32[]{:S(2)}) copy-start(f32[1536]{0:T(1024)} %param.9) | copy-start | bytes 18436
  93.1 12.7 %all-to-all-start = ((bf16[4,40,1536]{2,1,0:T(8,128)(2,1)}), bf16[4,40,1536]{2,1,0:T(8,128)(2,1)S(1)}, u32[]{:S(2)}, u32[]{:S(2)}) async-start(bf16[4,40,1536]{2,1,0:T(8,128)(2,1)} %bitcast.16), calls=%async_computation | async-start | bytes 983040 | tf_op jit(solution)/shard_map/all_to_all | solution.py:406

commit v7 on v6

--- a/solution.py
+++ b/solution.py
@@ -302,12 +302,12 @@
             rights += [(ref, h + side) for ref in (w4_ref if opposite else w0_ref, w1_ref, w2_ref, w3_ref)]
         lefts.append(left.astype(jnp.bfloat16))
     left = jnp.concatenate(lefts, axis=1)
-    for at in range(0, w0_ref.shape[2], 256):
-        right = jnp.concatenate([ref[h, :, at : at + 256] for ref, h in rights], axis=0)
+    for at in range(0, w0_ref.shape[2], 512):
+        right = jnp.concatenate([ref[h, :, at : at + 512] for ref, h in rights], axis=0)
         total = jnp.dot(left, right, preferred_element_type=jnp.float32)
         first, second = total[:rows], total[rows:]
-        keep_ref[:, at : at + 256] = jnp.where(c == 0, first, second)
-        send_ref[:, at : at + 256] = jnp.where(c == 0, second, first).astype(jnp.bfloat16)
+        keep_ref[:, at : at + 512] = jnp.where(c == 0, first, second).astype(jnp.bfloat16)
+        send_ref[:, at : at + 512] = jnp.where(c == 0, second, first).astype(jnp.bfloat16)
 
 
 def project(idx, attended, weights, ring):
@@ -315,7 +315,7 @@
     shape = (rows, weights[0].shape[2])
     return pl.pallas_call(
         functools.partial(project_kernel, ring),
-        out_shape=(jax.ShapeDtypeStruct(shape, jnp.float32), jax.ShapeDtypeStruct(shape, jnp.bfloat16)),
+        out_shape=(jax.ShapeDtypeStruct(shape, jnp.bfloat16), jax.ShapeDtypeStruct(shape, jnp.bfloat16)),
         in_specs=[SMEM] + [VMEM] * (1 + len(weights)),
         out_specs=(VMEM, VMEM),
         compiler_params=PARAMS,
@@ -324,7 +324,7 @@
 
 
 def join_kernel(idx_ref, keep_ref, both_ref, out_ref):
-    out_ref[...] = (keep_ref[...] + both_ref[1 - idx_ref[2]].astype(jnp.float32)).astype(jnp.bfloat16)
+    out_ref[...] = (keep_ref[...].astype(jnp.float32) + both_ref[1 - idx_ref[2]].astype(jnp.float32)).astype(jnp.bfloat16)
 
 
 def join(idx, keep, both):

time: 107 us -> 107 us (level)
  no operation moved by 1% of the time
where the time goes in v7:
time: 107 us
  starting transfers between devices  42.9 us (40%)
  blocking collectives  36.8 us (34%)
  Pallas kernels  15.6 us (15%)
  waiting for transfers between devices  9.95 us (9%)
    ppermute x8, starting transfers between devices, onward(): return lax.ppermute(block, ('y', 'c'), pairs)  24.1 us
    all_gather x1, blocking collectives, on_device(): attended = lax.all_gather(attended, 'col', axis=0, tiled=True)  13.3 us
    ppermute x1, starting transfers between devices, on_device(): qw_far = lax.ppermute(qw, 'zh', swap)  9.21 us
    all_gather x1, blocking collectives, on_device(): chip = lax.all_gather(own, 'c', axis=0)  8.66 us
    all_to_all x1, waiting for transfers between devices, on_device(): pieces = lax.all_to_all(pieces, 'row', 0, 0, tiled=True)  8.55 us
    ppermute x1, starting transfers between devices, on_device(): other = lax.ppermute(send, 'zh', swap)  5.5 us
    all_gather x1, blocking collectives, on_device(): attended = lax.all_gather(attended, 'c', axis=0)  4.96 us
    pallas_call x1, Pallas kernels, attend_near(): pl.pallas_call(functools.partial(near_kernel, rows, heads, ring, scale2),...  4.35 us
  transfers between devices with their start and end apart: 11, of which 2 were waited for; matrix products, arithmetic and copies ran while one was open for 0% of the time, Pallas kernels for 11%

profile of v7, /device:TPU:1, one launch (start us, length us, event | category | flops | bytes accessed | tf_op | source)
XLA Modules:
  0.0 106.5 jit_solution(18041632373228437421)
XLA Ops:
  0.0 1.0 pad_maximum_fusion.own_ref
  1.0 8.7 %all-gather = bf16[4,3,160,128]{3,2,1,0:T(8,128)(2,1)S(1)} all-gather(bf16[2,3,160,128]{3,2,1,0:T(8,128)(2,1)S(1)} %pad_maximum_fusion.own_ref), channel_id=2, replica_groups=mesh['y'=8,'zh'=2,'c'=2,'row'=4,'col'=4] {'c'}, dimensions={0}, use_global_device_ids=true | all-gather | bytes 737280 | tf_op jit(solution)/shard_map/all_gather | solution.py:375
  9.7 1.9 %collective-permute-start = (bf16[2,2,3,160,128]{4,3,2,1,0:T(8,128)(2,1)S(1)}, bf16[2,2,3,160,128]{4,3,2,1,0:T(8,128)(2,1)S(1)}, u32[]{:S(2)}, u32[]{:S(2)}) collective-permute-start(bf16[2,2,3,160,128]{4,3,2,1,0:T(8,128)(2,1)S(1)} %bitcast.26), channel_id=1, source_target_pairs={{0,128},{16,400},{64,192},{80,464},{128,256},{144,16},{192,320},{2... | collective-permute-start | bytes 1474568 | tf_op jit(solution)/shard_map/ppermute | solution.py:370
  11.6 1.7 %pack.1 = bf16[1056,128]{1,0:T(8,128)(2,1)} custom-call(bf16[3,160,128]{2,1,0:T(8,128)(2,1)} %bitcast.28, bf16[12,4,1536]{2,1,0:T(4,128)(2,1)} %w_ref), custom_call_target="tpu_custom_call" | custom-call | tf_op jit(solution)/shard_map/pack/pallas_call | solution.py:76
  13.3 9.2 %collective-permute-start.1 = (bf16[1056,128]{1,0:T(8,128)(2,1)}, bf16[1056,128]{1,0:T(8,128)(2,1)S(1)}, u32[]{:S(2)}, u32[]{:S(2)}) collective-permute-start(bf16[1056,128]{1,0:T(8,128)(2,1)} %pack.1), channel_id=1, source_target_pairs={{0,32},{32,0},{1,33},{33,1},{2,34},{34,2},{3,35},{35,3},{4,36},{36... | collective-permute-start | bytes 811016 | tf_op jit(solution)/shard_map/ppermute | solution.py:381
  22.5 3.0 %collective-permute-start.4 = (bf16[2,2,3,160,128]{4,3,2,1,0:T(8,128)(2,1)S(1)}, bf16[2,2,3,160,128]{4,3,2,1,0:T(8,128)(2,1)S(1)}, u32[]{:S(2)}, u32[]{:S(2)}) collective-permute-start(bf16[2,2,3,160,128]{4,3,2,1,0:T(8,128)(2,1)S(1)} %bitcast.27), channel_id=1, source_target_pairs={{0,64},{16,464},{64,128},{80,16},{128,192},{144,80},{192,256},{208... | collective-permute-start | bytes 1474568 | tf_op jit(solution)/shard_map/ppermute | solution.py:370
  25.5 2.4 %all-gather.1 = bf16[2112,128]{1,0:T(8,128)(2,1)S(1)} all-gather(bf16[1056,128]{1,0:T(8,128)(2,1)} %pack.1), channel_id=3, replica_groups=mesh['y'=8,'zh'=2,'c'=2,'row'=4,'col'=4] {'c'}, dimensions={0}, use_global_device_ids=true | all-gather | bytes 811008 | tf_op jit(solution)/shard_map/all_gather | solution.py:382
  27.9 0.0 collective-permute-done.b2_ref
  27.9 3.0 %collective-permute-start.2 = (bf16[2,2,3,160,128]{4,3,2,1,0:T(8,128)(2,1)S(1)}, bf16[2,2,3,160,128]{4,3,2,1,0:T(8,128)(2,1)S(1)}, u32[]{:S(2)}, u32[]{:S(2)}) collective-permute-start(bf16[2,2,3,160,128]{4,3,2,1,0:T(8,128)(2,1)S(1)} %collective-permute-done.b2_ref), channel_id=1, source_target_pairs={{0,64},{16,464},{64,128},{80,16},{128,192},{144,80},{192,256},{208... | collective-permute-start | bytes 1474568 | tf_op jit(solution)/shard_map/ppermute | solution.py:370
  30.9 0.1 pad_add_fusion.idx_ref
  31.0 2.0 %collective-permute-start.3 = (bf16[2,3,160,128]{3,2,1,0:T(8,128)(2,1)S(1)}, bf16[2,3,160,128]{3,2,1,0:T(8,128)(2,1)S(1)}, u32[]{:S(2)}, u32[]{:S(2)}) collective-permute-start(bf16[2,3,160,128]{3,2,1,0:T(8,128)(2,1)S(1)} %dynamic-slice_bitcast_fusion), channel_id=1, source_target_pairs={{0,128},{16,400},{64,192},{80,464},{128,256},{144,16},{192,320},{2... | collective-permute-start | bytes 737288 | tf_op jit(solution)/shard_map/ppermute | solution.py:370
  32.9 1.4 %collective-permute-done.1 = bf16[1056,128]{1,0:T(8,128)(2,1)S(1)} collective-permute-done((bf16[1056,128]{1,0:T(8,128)(2,1)}, bf16[1056,128]{1,0:T(8,128)(2,1)S(1)}, u32[]{:S(2)}, u32[]{:S(2)}) %collective-permute-start.1) | collective-permute-done | bytes 270368 | tf_op jit(solution)/shard_map/ppermute | solution.py:381
  34.3 2.7 %all-gather.2 = bf16[2112,128]{1,0:T(8,128)(2,1)S(1)} all-gather(bf16[1056,128]{1,0:T(8,128)(2,1)S(1)} %collective-permute-done.1), channel_id=4, replica_groups=mesh['y'=8,'zh'=2,'c'=2,'row'=4,'col'=4] {'c'}, dimensions={0}, use_global_device_ids=true | all-gather | bytes 811008 | tf_op jit(solution)/shard_map/all_gather | solution.py:383
  37.0 0.8 unpack.1
  37.8 0.0 collective-permute-done.4.b1_ref
  37.9 4.3 %attend_near.1 = (f32[3,1,640]{2,1,0:T(1,128)S(1)}, f32[3,1,640]{2,1,0:T(1,128)S(1)}, f32[3,128,640]{2,1,0:T(8,128)S(1)}) custom-call(s32[3]{0:T(128)S(1)} %pad_add_fusion.idx_ref, bf16[3,640,128]{2,1,0:T(8,128)(2,1)S(1)} %get-tuple-element.30.q_ref, bf16[2,3,160,128]{3,2,1,0:T(8,128)(2,1)S(1)} %pad_maximum_fusion.own_ref, ...), custom_call_target="tpu_custom_call" | custom-call | flops 268435456 | bytes 262144 | tf_op jit(solution)/shard_map/attend_near/pallas_call | solution.py:188
  42.2 5.0 %collective-permute-start.7 = (bf16[12,16,1536]{2,1,0:T(8,128)(2,1)S(1)}, bf16[12,16,1536]{2,1,0:T(8,128)(2,1)S(1)}, u32[]{:S(2)}, u32[]{:S(2)}) collective-permute-start(bf16[12,16,1536]{2,1,0:T(8,128)(2,1)S(1)} %get-tuple-element.44.w0_ref), channel_id=1, source_target_pairs={{0,128},{16,400},{64,192},{80,464},{128,256},{144,16},{192,320},{2... | collective-permute-start | bytes 1769480 | tf_op jit(solution)/shard_map/ppermute | solution.py:370
  47.2 0.0 collective-permute-done.3.b4_ref
  47.2 0.0 collective-permute-done.2.b3_ref
  47.2 3.3 %attend_far.1 = (bf16[2,512,128]{2,1,0:T(8,128)(2,1)S(1)}, bf16[2,512,128]{2,1,0:T(8,128)(2,1)S(1)}) custom-call(s32[3]{0:T(128)S(1)} %pad_add_fusion.idx_ref, bf16[3,640,128]{2,1,0:T(8,128)(2,1)S(1)} %get-tuple-element.30.q_ref, bf16[2,2,3,160,128]{4,3,2,1,0:T(8,128)(2,1)S(1)} %collective-permute-done.2.b3_ref, ...), custom_call_target="tpu_custom_call" | custom-call | flops 2147483648 | bytes 262144 | tf_op jit(solution)/shard_map/attend_far/pallas_call | solution.py:204
  50.5 2.2 %all-gather.3 = bf16[4,512,128]{2,1,0:T(8,128)(2,1)S(1)} all-gather(bf16[2,512,128]{2,1,0:T(8,128)(2,1)S(1)} %get-tuple-element.41), channel_id=5, replica_groups=mesh['y'=8,'zh'=2,'c'=2,'row'=4,'col'=4] {'c'}, dimensions={0}, use_global_device_ids=true | all-gather | bytes 786432 | tf_op jit(solution)/shard_map/all_gather | solution.py:394
  52.7 1.1 %merge_core.1 = (bf16[512,128]{1,0:T(8,128)(2,1)S(1)}, bf16[512,128]{1,0:T(8,128)(2,1)S(1)}) custom-call(s32[3]{0:T(128)S(1)} %pad_add_fusion.idx_ref, bf16[2,512,128]{2,1,0:T(8,128)(2,1)S(1)} %get-tuple-element.40.a_ref, bf16[2,2,512,128]{3,2,1,0:T(8,128)(2,1)S(1)} %bitcast.24), custom_call_target="tpu_custom_call" | custom-call | tf_op jit(solution)/shard_map/merge_core/pallas_call | solution.py:254
  53.8 5.5 %collective-permute-start.5 = (bf16[512,128]{1,0:T(8,128)(2,1)S(1)}, bf16[512,128]{1,0:T(8,128)(2,1)S(1)}, u32[]{:S(2)}, u32[]{:S(2)}) collective-permute-start(bf16[512,128]{1,0:T(8,128)(2,1)S(1)} %get-tuple-element.43), channel_id=1, source_target_pairs={{0,32},{32,0},{1,33},{33,1},{2,34},{34,2},{3,35},{35,3},{4,36},{36... | collective-permute-start | bytes 393224 | tf_op jit(solution)/shard_map/ppermute | solution.py:395
  59.3 4.9 %collective-permute-start.6 = (bf16[12,16,1536]{2,1,0:T(8,128)(2,1)S(1)}, bf16[12,16,1536]{2,1,0:T(8,128)(2,1)S(1)}, u32[]{:S(2)}, u32[]{:S(2)}) collective-permute-start(bf16[12,16,1536]{2,1,0:T(8,128)(2,1)S(1)} %get-tuple-element.44.w0_ref), channel_id=1, source_target_pairs={{0,64},{16,464},{64,128},{80,16},{128,192},{144,80},{192,256},{208... | collective-permute-start | bytes 1769480 | tf_op jit(solution)/shard_map/ppermute | solution.py:370
  64.2 0.0 collective-permute-done.7.w2_ref
  64.2 2.3 %collective-permute-start.9 = (bf16[6,16,1536]{2,1,0:T(8,128)(2,1)S(1)}, bf16[6,16,1536]{2,1,0:T(8,128)(2,1)S(1)}, u32[]{:S(2)}, u32[]{:S(2)}) collective-permute-start(bf16[6,16,1536]{2,1,0:T(8,128)(2,1)S(1)} %slice.4), channel_id=1, source_target_pairs={{0,128},{16,400},{64,192},{80,464},{128,256},{144,16},{192,320},{2... | collective-permute-start | bytes 884744 | tf_op jit(solution)/shard_map/ppermute | solution.py:370
  66.5 2.1 %collective-permute-start.8 = (bf16[12,16,1536]{2,1,0:T(8,128)(2,1)S(1)}, bf16[12,16,1536]{2,1,0:T(8,128)(2,1)S(1)}, u32[]{:S(2)}, u32[]{:S(2)}) collective-permute-start(bf16[12,16,1536]{2,1,0:T(8,128)(2,1)S(1)} %collective-permute-done.7.w2_ref), channel_id=1, source_target_pairs={{0,64},{16,464},{64,128},{80,16},{128,192},{144,80},{192,256},{208... | collective-permute-start | bytes 1769480 | tf_op jit(solution)/shard_map/ppermute | solution.py:370
  68.7 0.0 collective-permute-done.5.b_ref
  68.7 0.4 merge_far.1
  69.1 13.3 %all_gather.47 = bf16[12,160,128]{2,1,0:T(8,128)(2,1)S(1)} all-gather(bf16[3,160,128]{2,1,0:T(8,128)(2,1)S(1)} %bitcast.25), channel_id=1, replica_groups=mesh['y'=8,'zh'=2,'c'=2,'row'=4,'col'=4] {'col'}, dimensions={0}, use_global_device_ids=true | all-gather | bytes 614400 | tf_op jit(solution)/shard_map/all_gather | solution.py:400
  82.4 5.0 %all-gather.4 = bf16[24,160,128]{2,1,0:T(8,128)(2,1)S(1)} all-gather(bf16[12,160,128]{2,1,0:T(8,128)(2,1)S(1)} %all_gather.47), channel_id=6, replica_groups=mesh['y'=8,'zh'=2,'c'=2,'row'=4,'col'=4] {'c'}, dimensions={0}, use_global_device_ids=true | all-gather | bytes 1474560 | tf_op jit(solution)/shard_map/all_gather | solution.py:401
  87.4 0.0 collective-permute-done.6.w1_ref
  87.4 0.0 collective-permute-done.9.w4_ref
  87.4 0.0 collective-permute-done.8.w3_ref
  87.4 1.8 %project.1 = (bf16[160,1536]{1,0:T(8,128)(2,1)S(1)}, bf16[160,1536]{1,0:T(8,128)(2,1)S(1)}) custom-call(s32[3]{0:T(128)S(1)} %pad_add_fusion.idx_ref, bf16[2,12,160,128]{3,2,1,0:T(8,128)(2,1)S(1)} %bitcast.21, bf16[12,16,1536]{2,1,0:T(8,128)(2,1)S(1)} %get-tuple-element.44.w0_ref, bf16[12,16,1536]{2,1,0:T(8,128)(2,1)S(1)} %collective-permute-done.6.w1_ref, ...), custom_call_target="tpu_custom_call" | custom-call | tf_op jit(solution)/shard_map/project/pallas_call | solution.py:316
  89.1 2.5 %all-gather.5 = bf16[320,1536]{1,0:T(8,128)(2,1)S(1)} all-gather(bf16[160,1536]{1,0:T(8,128)(2,1)S(1)} %get-tuple-element.46), channel_id=7, replica_groups=mesh['y'=8,'zh'=2,'c'=2,'row'=4,'col'=4] {'c'}, dimensions={0}, use_global_device_ids=true | all-gather | bytes 1474560 | tf_op jit(solution)/shard_map/all_gather | solution.py:403
  91.7 1.4 %join.1 = bf16[160,1536]{1,0:T(8,128)(2,1)} custom-call(s32[3]{0:T(128)S(1)} %pad_add_fusion.idx_ref, bf16[160,1536]{1,0:T(8,128)(2,1)S(1)} %get-tuple-element.45.keep_ref, bf16[2,160,1536]{2,1,0:T(8,128)(2,1)S(1)} %bitcast.20), custom_call_target="tpu_custom_call" | custom-call | tf_op jit(solution)/shard_map/join/pallas_call | solution.py:331
  93.1 0.0 copy-start
  93.1 4.1 %all-to-all-start = ((bf16[4,40,1536]{2,1,0:T(8,128)(2,1)}), bf16[4,40,1536]{2,1,0:T(8,128)(2,1)S(1)}, u32[]{:S(2)}, u32[]{:S(2)}) async-start(bf16[4,40,1536]{2,1,0:T(8,128)(2,1)} %bitcast.16), calls=%async_computation | async-start | bytes 983040 | tf_op jit(solution)/shard_map/all_to_all | solution.py:406
  97.2 0.0 copy-done
  97.3 8.5 %all-to-all-done.pieces_ref = bf16[4,40,1536]{2,1,0:T(8,128)(2,1)S(1)} async-done(((bf16[4,40,1536]{2,1,0:T(8,128)(2,1)}), bf16[4,40,1536]{2,1,0:T(8,128)(2,1)S(1)}, u32[]{:S(2)}, u32[]{:S(2)}) %all-to-all-start) | async-done | bytes 491552 | tf_op jit(solution)/shard_map/all_to_all | solution.py:406
  105.8 0.7 finish.1
  (3 shorter events, 0.0 us)
Async XLA Ops:
  9.7 18.2 %collective-permute-start = (bf16[2,2,3,160,128]{4,3,2,1,0:T(8,128)(2,1)S(1)}, bf16[2,2,3,160,128]{4,3,2,1,0:T(8,128)(2,1)S(1)}, u32[]{:S(2)}, u32[]{:S(2)}) collective-permute-start(bf16[2,2,3,160,128]{4,3,2,1,0:T(8,128)(2,1)S(1)} %bitcast.26), channel_id=1, source_target_pairs={{0,128},{16,400},{64,192},{80,464},{128,256},{144,16},{192,320},{2... | collective-permute-start | bytes 1474568 | tf_op jit(solution)/shard_map/ppermute | solution.py:370
  13.3 21.0 %collective-permute-start.1 = (bf16[1056,128]{1,0:T(8,128)(2,1)}, bf16[1056,128]{1,0:T(8,128)(2,1)S(1)}, u32[]{:S(2)}, u32[]{:S(2)}) collective-permute-start(bf16[1056,128]{1,0:T(8,128)(2,1)} %pack.1), channel_id=1, source_target_pairs={{0,32},{32,0},{1,33},{33,1},{2,34},{34,2},{3,35},{35,3},{4,36},{36... | collective-permute-start | bytes 811016 | tf_op jit(solution)/shard_map/ppermute | solution.py:381
  22.5 15.3 %collective-permute-start.4 = (bf16[2,2,3,160,128]{4,3,2,1,0:T(8,128)(2,1)S(1)}, bf16[2,2,3,160,128]{4,3,2,1,0:T(8,128)(2,1)S(1)}, u32[]{:S(2)}, u32[]{:S(2)}) collective-permute-start(bf16[2,2,3,160,128]{4,3,2,1,0:T(8,128)(2,1)S(1)} %bitcast.27), channel_id=1, source_target_pairs={{0,64},{16,464},{64,128},{80,16},{128,192},{144,80},{192,256},{208... | collective-permute-start | bytes 1474568 | tf_op jit(solution)/shard_map/ppermute | solution.py:370
  27.9 19.3 %collective-permute-start.2 = (bf16[2,2,3,160,128]{4,3,2,1,0:T(8,128)(2,1)S(1)}, bf16[2,2,3,160,128]{4,3,2,1,0:T(8,128)(2,1)S(1)}, u32[]{:S(2)}, u32[]{:S(2)}) collective-permute-start(bf16[2,2,3,160,128]{4,3,2,1,0:T(8,128)(2,1)S(1)} %collective-permute-done.b2_ref), channel_id=1, source_target_pairs={{0,64},{16,464},{64,128},{80,16},{128,192},{144,80},{192,256},{208... | collective-permute-start | bytes 1474568 | tf_op jit(solution)/shard_map/ppermute | solution.py:370
  31.0 16.2 %collective-permute-start.3 = (bf16[2,3,160,128]{3,2,1,0:T(8,128)(2,1)S(1)}, bf16[2,3,160,128]{3,2,1,0:T(8,128)(2,1)S(1)}, u32[]{:S(2)}, u32[]{:S(2)}) collective-permute-start(bf16[2,3,160,128]{3,2,1,0:T(8,128)(2,1)S(1)} %dynamic-slice_bitcast_fusion), channel_id=1, source_target_pairs={{0,128},{16,400},{64,192},{80,464},{128,256},{144,16},{192,320},{2... | collective-permute-start | bytes 737288 | tf_op jit(solution)/shard_map/ppermute | solution.py:370
  42.2 22.0 %collective-permute-start.7 = (bf16[12,16,1536]{2,1,0:T(8,128)(2,1)S(1)}, bf16[12,16,1536]{2,1,0:T(8,128)(2,1)S(1)}, u32[]{:S(2)}, u32[]{:S(2)}) collective-permute-start(bf16[12,16,1536]{2,1,0:T(8,128)(2,1)S(1)} %get-tuple-element.44.w0_ref), channel_id=1, source_target_pairs={{0,128},{16,400},{64,192},{80,464},{128,256},{144,16},{192,320},{2... | collective-permute-start | bytes 1769480 | tf_op jit(solution)/shard_map/ppermute | solution.py:370
  53.8 14.9 %collective-permute-start.5 = (bf16[512,128]{1,0:T(8,128)(2,1)S(1)}, bf16[512,128]{1,0:T(8,128)(2,1)S(1)}, u32[]{:S(2)}, u32[]{:S(2)}) collective-permute-start(bf16[512,128]{1,0:T(8,128)(2,1)S(1)} %get-tuple-element.43), channel_id=1, source_target_pairs={{0,32},{32,0},{1,33},{33,1},{2,34},{34,2},{3,35},{35,3},{4,36},{36... | collective-permute-start | bytes 393224 | tf_op jit(solution)/shard_map/ppermute | solution.py:395
  59.3 28.1 %collective-permute-start.6 = (bf16[12,16,1536]{2,1,0:T(8,128)(2,1)S(1)}, bf16[12,16,1536]{2,1,0:T(8,128)(2,1)S(1)}, u32[]{:S(2)}, u32[]{:S(2)}) collective-permute-start(bf16[12,16,1536]{2,1,0:T(8,128)(2,1)S(1)} %get-tuple-element.44.w0_ref), channel_id=1, source_target_pairs={{0,64},{16,464},{64,128},{80,16},{128,192},{144,80},{192,256},{208... | collective-permute-start | bytes 1769480 | tf_op jit(solution)/shard_map/ppermute | solution.py:370
  64.2 23.2 %collective-permute-start.9 = (bf16[6,16,1536]{2,1,0:T(8,128)(2,1)S(1)}, bf16[6,16,1536]{2,1,0:T(8,128)(2,1)S(1)}, u32[]{:S(2)}, u32[]{:S(2)}) collective-permute-start(bf16[6,16,1536]{2,1,0:T(8,128)(2,1)S(1)} %slice.4), channel_id=1, source_target_pairs={{0,128},{16,400},{64,192},{80,464},{128,256},{144,16},{192,320},{2... | collective-permute-start | bytes 884744 | tf_op jit(solution)/shard_map/ppermute | solution.py:370
  66.5 20.9 %collective-permute-start.8 = (bf16[12,16,1536]{2,1,0:T(8,128)(2,1)S(1)}, bf16[12,16,1536]{2,1,0:T(8,128)(2,1)S(1)}, u32[]{:S(2)}, u32[]{:S(2)}) collective-permute-start(bf16[12,16,1536]{2,1,0:T(8,128)(2,1)S(1)} %collective-permute-done.7.w2_ref), channel_id=1, source_target_pairs={{0,64},{16,464},{64,128},{80,16},{128,192},{144,80},{192,256},{208... | collective-permute-start | bytes 1769480 | tf_op jit(solution)/shard_map/ppermute | solution.py:370
  93.1 4.1 %copy-start = (f32[1536]{0:T(1024)S(1)}, f32[1536]{0:T(1024)}, u32[]{:S(2)}) copy-start(f32[1536]{0:T(1024)} %param.9) | copy-start | bytes 18436
  93.1 12.7 %all-to-all-start = ((bf16[4,40,1536]{2,1,0:T(8,128)(2,1)}), bf16[4,40,1536]{2,1,0:T(8,128)(2,1)S(1)}, u32[]{:S(2)}, u32[]{:S(2)}) async-start(bf16[4,40,1536]{2,1,0:T(8,128)(2,1)} %bitcast.16), calls=%async_computation | async-start | bytes 983040 | tf_op jit(solution)/shard_map/all_to_all | solution.py:406

commit v8 on v6

--- a/solution.py
+++ b/solution.py
@@ -323,16 +323,23 @@
     )(idx, attended, *weights)
 
 
-def join_kernel(idx_ref, keep_ref, both_ref, out_ref):
-    out_ref[...] = (keep_ref[...] + both_ref[1 - idx_ref[2]].astype(jnp.float32)).astype(jnp.bfloat16)
+def join_kernel(idx_ref, keep_ref, other_ref, out_ref):
+    out_ref[...] = (keep_ref[...] + other_ref[0].astype(jnp.float32)).astype(jnp.bfloat16)
 
 
 def join(idx, keep, both):
+    _, rows, wide = both.shape
+    half = wide // 2
+    mine = pl.BlockSpec((rows, half), lambda i, idx_ref: (0, i))
     return pl.pallas_call(
         join_kernel,
-        out_shape=jax.ShapeDtypeStruct(both.shape[1:], jnp.bfloat16),
-        in_specs=[SMEM, VMEM, VMEM],
-        out_specs=VMEM,
+        out_shape=jax.ShapeDtypeStruct((rows, wide), jnp.bfloat16),
+        grid_spec=pltpu.PrefetchScalarGridSpec(
+            num_scalar_prefetch=1,
+            grid=(2,),
+            in_specs=[mine, pl.BlockSpec((1, rows, half), lambda i, idx_ref: (1 - idx_ref[2], 0, i))],
+            out_specs=mine,
+        ),
         compiler_params=PARAMS,
         name="join",
     )(idx, keep, both)

time: 107 us -> 107 us (level)
  no operation moved by 1% of the time
where the time goes in v8:
time: 107 us
  starting transfers between devices  42.9 us (40%)
  blocking collectives  36.8 us (34%)
  Pallas kernels  15.7 us (15%)
  waiting for transfers between devices  9.95 us (9%)
    ppermute x8, starting transfers between devices, onward(): return lax.ppermute(block, ('y', 'c'), pairs)  24.1 us
    all_gather x1, blocking collectives, on_device(): attended = lax.all_gather(attended, 'col', axis=0, tiled=True)  13.3 us
    ppermute x1, starting transfers between devices, on_device(): qw_far = lax.ppermute(qw, 'zh', swap)  9.21 us
    all_gather x1, blocking collectives, on_device(): chip = lax.all_gather(own, 'c', axis=0)  8.66 us
    all_to_all x1, waiting for transfers between devices, on_device(): pieces = lax.all_to_all(pieces, 'row', 0, 0, tiled=True)  8.55 us
    ppermute x1, starting transfers between devices, on_device(): other = lax.ppermute(send, 'zh', swap)  5.5 us
    all_gather x1, blocking collectives, on_device(): attended = lax.all_gather(attended, 'c', axis=0)  4.96 us
    pallas_call x1, Pallas kernels, attend_near(): pl.pallas_call(functools.partial(near_kernel, rows, heads, ring, scale2),...  4.35 us
  transfers between devices with their start and end apart: 11, of which 2 were waited for; matrix products, arithmetic and copies ran while one was open for 0% of the time, Pallas kernels for 11%

profile of v8, /device:TPU:1, one launch (start us, length us, event | category | flops | bytes accessed | tf_op | source)
XLA Modules:
  0.0 106.6 jit_solution(12485912215888070711)
XLA Ops:
  0.0 1.0 pad_maximum_fusion.own_ref
  1.0 8.7 %all-gather = bf16[4,3,160,128]{3,2,1,0:T(8,128)(2,1)S(1)} all-gather(bf16[2,3,160,128]{3,2,1,0:T(8,128)(2,1)S(1)} %pad_maximum_fusion.own_ref), channel_id=2, replica_groups=mesh['y'=8,'zh'=2,'c'=2,'row'=4,'col'=4] {'c'}, dimensions={0}, use_global_device_ids=true | all-gather | bytes 737280 | tf_op jit(solution)/shard_map/all_gather | solution.py:382
  9.7 1.9 %collective-permute-start = (bf16[2,2,3,160,128]{4,3,2,1,0:T(8,128)(2,1)S(1)}, bf16[2,2,3,160,128]{4,3,2,1,0:T(8,128)(2,1)S(1)}, u32[]{:S(2)}, u32[]{:S(2)}) collective-permute-start(bf16[2,2,3,160,128]{4,3,2,1,0:T(8,128)(2,1)S(1)} %bitcast.26), channel_id=1, source_target_pairs={{0,128},{16,400},{64,192},{80,464},{128,256},{144,16},{192,320},{2... | collective-permute-start | bytes 1474568 | tf_op jit(solution)/shard_map/ppermute | solution.py:377
  11.6 1.7 %pack.1 = bf16[1056,128]{1,0:T(8,128)(2,1)} custom-call(bf16[3,160,128]{2,1,0:T(8,128)(2,1)} %bitcast.28, bf16[12,4,1536]{2,1,0:T(4,128)(2,1)} %w_ref), custom_call_target="tpu_custom_call" | custom-call | tf_op jit(solution)/shard_map/pack/pallas_call | solution.py:76
  13.3 9.2 %collective-permute-start.1 = (bf16[1056,128]{1,0:T(8,128)(2,1)}, bf16[1056,128]{1,0:T(8,128)(2,1)S(1)}, u32[]{:S(2)}, u32[]{:S(2)}) collective-permute-start(bf16[1056,128]{1,0:T(8,128)(2,1)} %pack.1), channel_id=1, source_target_pairs={{0,32},{32,0},{1,33},{33,1},{2,34},{34,2},{3,35},{35,3},{4,36},{36... | collective-permute-start | bytes 811016 | tf_op jit(solution)/shard_map/ppermute | solution.py:388
  22.5 3.0 %collective-permute-start.4 = (bf16[2,2,3,160,128]{4,3,2,1,0:T(8,128)(2,1)S(1)}, bf16[2,2,3,160,128]{4,3,2,1,0:T(8,128)(2,1)S(1)}, u32[]{:S(2)}, u32[]{:S(2)}) collective-permute-start(bf16[2,2,3,160,128]{4,3,2,1,0:T(8,128)(2,1)S(1)} %bitcast.27), channel_id=1, source_target_pairs={{0,64},{16,464},{64,128},{80,16},{128,192},{144,80},{192,256},{208... | collective-permute-start | bytes 1474568 | tf_op jit(solution)/shard_map/ppermute | solution.py:377
  25.5 2.4 %all-gather.1 = bf16[2112,128]{1,0:T(8,128)(2,1)S(1)} all-gather(bf16[1056,128]{1,0:T(8,128)(2,1)} %pack.1), channel_id=3, replica_groups=mesh['y'=8,'zh'=2,'c'=2,'row'=4,'col'=4] {'c'}, dimensions={0}, use_global_device_ids=true | all-gather | bytes 811008 | tf_op jit(solution)/shard_map/all_gather | solution.py:389
  27.9 0.0 collective-permute-done.b2_ref
  27.9 3.0 %collective-permute-start.2 = (bf16[2,2,3,160,128]{4,3,2,1,0:T(8,128)(2,1)S(1)}, bf16[2,2,3,160,128]{4,3,2,1,0:T(8,128)(2,1)S(1)}, u32[]{:S(2)}, u32[]{:S(2)}) collective-permute-start(bf16[2,2,3,160,128]{4,3,2,1,0:T(8,128)(2,1)S(1)} %collective-permute-done.b2_ref), channel_id=1, source_target_pairs={{0,64},{16,464},{64,128},{80,16},{128,192},{144,80},{192,256},{208... | collective-permute-start | bytes 1474568 | tf_op jit(solution)/shard_map/ppermute | solution.py:377
  30.9 0.1 pad_add_fusion.idx_ref
  31.0 2.0 %collective-permute-start.3 = (bf16[2,3,160,128]{3,2,1,0:T(8,128)(2,1)S(1)}, bf16[2,3,160,128]{3,2,1,0:T(8,128)(2,1)S(1)}, u32[]{:S(2)}, u32[]{:S(2)}) collective-permute-start(bf16[2,3,160,128]{3,2,1,0:T(8,128)(2,1)S(1)} %dynamic-slice_bitcast_fusion), channel_id=1, source_target_pairs={{0,128},{16,400},{64,192},{80,464},{128,256},{144,16},{192,320},{2... | collective-permute-start | bytes 737288 | tf_op jit(solution)/shard_map/ppermute | solution.py:377
  32.9 1.4 %collective-permute-done.1 = bf16[1056,128]{1,0:T(8,128)(2,1)S(1)} collective-permute-done((bf16[1056,128]{1,0:T(8,128)(2,1)}, bf16[1056,128]{1,0:T(8,128)(2,1)S(1)}, u32[]{:S(2)}, u32[]{:S(2)}) %collective-permute-start.1) | collective-permute-done | bytes 270368 | tf_op jit(solution)/shard_map/ppermute | solution.py:388
  34.3 2.7 %all-gather.2 = bf16[2112,128]{1,0:T(8,128)(2,1)S(1)} all-gather(bf16[1056,128]{1,0:T(8,128)(2,1)S(1)} %collective-permute-done.1), channel_id=4, replica_groups=mesh['y'=8,'zh'=2,'c'=2,'row'=4,'col'=4] {'c'}, dimensions={0}, use_global_device_ids=true | all-gather | bytes 811008 | tf_op jit(solution)/shard_map/all_gather | solution.py:390
  37.0 0.8 unpack.1
  37.8 0.0 collective-permute-done.4.b1_ref
  37.9 4.3 %attend_near.1 = (f32[3,1,640]{2,1,0:T(1,128)S(1)}, f32[3,1,640]{2,1,0:T(1,128)S(1)}, f32[3,128,640]{2,1,0:T(8,128)S(1)}) custom-call(s32[3]{0:T(128)S(1)} %pad_add_fusion.idx_ref, bf16[3,640,128]{2,1,0:T(8,128)(2,1)S(1)} %get-tuple-element.30.q_ref, bf16[2,3,160,128]{3,2,1,0:T(8,128)(2,1)S(1)} %pad_maximum_fusion.own_ref, ...), custom_call_target="tpu_custom_call" | custom-call | flops 268435456 | bytes 262144 | tf_op jit(solution)/shard_map/attend_near/pallas_call | solution.py:188
  42.2 5.0 %collective-permute-start.7 = (bf16[12,16,1536]{2,1,0:T(8,128)(2,1)S(1)}, bf16[12,16,1536]{2,1,0:T(8,128)(2,1)S(1)}, u32[]{:S(2)}, u32[]{:S(2)}) collective-permute-start(bf16[12,16,1536]{2,1,0:T(8,128)(2,1)S(1)} %get-tuple-element.44.w0_ref), channel_id=1, source_target_pairs={{0,128},{16,400},{64,192},{80,464},{128,256},{144,16},{192,320},{2... | collective-permute-start | bytes 1769480 | tf_op jit(solution)/shard_map/ppermute | solution.py:377
  47.2 0.0 collective-permute-done.3.b4_ref
  47.2 0.0 collective-permute-done.2.b3_ref
  47.2 3.3 %attend_far.1 = (bf16[2,512,128]{2,1,0:T(8,128)(2,1)S(1)}, bf16[2,512,128]{2,1,0:T(8,128)(2,1)S(1)}) custom-call(s32[3]{0:T(128)S(1)} %pad_add_fusion.idx_ref, bf16[3,640,128]{2,1,0:T(8,128)(2,1)S(1)} %get-tuple-element.30.q_ref, bf16[2,2,3,160,128]{4,3,2,1,0:T(8,128)(2,1)S(1)} %collective-permute-done.2.b3_ref, ...), custom_call_target="tpu_custom_call" | custom-call | flops 2147483648 | bytes 262144 | tf_op jit(solution)/shard_map/attend_far/pallas_call | solution.py:204
  50.5 2.2 %all-gather.3 = bf16[4,512,128]{2,1,0:T(8,128)(2,1)S(1)} all-gather(bf16[2,512,128]{2,1,0:T(8,128)(2,1)S(1)} %get-tuple-element.41), channel_id=5, replica_groups=mesh['y'=8,'zh'=2,'c'=2,'row'=4,'col'=4] {'c'}, dimensions={0}, use_global_device_ids=true | all-gather | bytes 786432 | tf_op jit(solution)/shard_map/all_gather | solution.py:401
  52.7 1.1 %merge_core.1 = (bf16[512,128]{1,0:T(8,128)(2,1)S(1)}, bf16[512,128]{1,0:T(8,128)(2,1)S(1)}) custom-call(s32[3]{0:T(128)S(1)} %pad_add_fusion.idx_ref, bf16[2,512,128]{2,1,0:T(8,128)(2,1)S(1)} %get-tuple-element.40.a_ref, bf16[2,2,512,128]{3,2,1,0:T(8,128)(2,1)S(1)} %bitcast.24), custom_call_target="tpu_custom_call" | custom-call | tf_op jit(solution)/shard_map/merge_core/pallas_call | solution.py:254
  53.8 5.5 %collective-permute-start.5 = (bf16[512,128]{1,0:T(8,128)(2,1)S(1)}, bf16[512,128]{1,0:T(8,128)(2,1)S(1)}, u32[]{:S(2)}, u32[]{:S(2)}) collective-permute-start(bf16[512,128]{1,0:T(8,128)(2,1)S(1)} %get-tuple-element.43), channel_id=1, source_target_pairs={{0,32},{32,0},{1,33},{33,1},{2,34},{34,2},{3,35},{35,3},{4,36},{36... | collective-permute-start | bytes 393224 | tf_op jit(solution)/shard_map/ppermute | solution.py:402
  59.3 4.9 %collective-permute-start.6 = (bf16[12,16,1536]{2,1,0:T(8,128)(2,1)S(1)}, bf16[12,16,1536]{2,1,0:T(8,128)(2,1)S(1)}, u32[]{:S(2)}, u32[]{:S(2)}) collective-permute-start(bf16[12,16,1536]{2,1,0:T(8,128)(2,1)S(1)} %get-tuple-element.44.w0_ref), channel_id=1, source_target_pairs={{0,64},{16,464},{64,128},{80,16},{128,192},{144,80},{192,256},{208... | collective-permute-start | bytes 1769480 | tf_op jit(solution)/shard_map/ppermute | solution.py:377
  64.2 0.0 collective-permute-done.7.w2_ref
  64.2 2.3 %collective-permute-start.9 = (bf16[6,16,1536]{2,1,0:T(8,128)(2,1)S(1)}, bf16[6,16,1536]{2,1,0:T(8,128)(2,1)S(1)}, u32[]{:S(2)}, u32[]{:S(2)}) collective-permute-start(bf16[6,16,1536]{2,1,0:T(8,128)(2,1)S(1)} %slice.4), channel_id=1, source_target_pairs={{0,128},{16,400},{64,192},{80,464},{128,256},{144,16},{192,320},{2... | collective-permute-start | bytes 884744 | tf_op jit(solution)/shard_map/ppermute | solution.py:377
  66.5 2.1 %collective-permute-start.8 = (bf16[12,16,1536]{2,1,0:T(8,128)(2,1)S(1)}, bf16[12,16,1536]{2,1,0:T(8,128)(2,1)S(1)}, u32[]{:S(2)}, u32[]{:S(2)}) collective-permute-start(bf16[12,16,1536]{2,1,0:T(8,128)(2,1)S(1)} %collective-permute-done.7.w2_ref), channel_id=1, source_target_pairs={{0,64},{16,464},{64,128},{80,16},{128,192},{144,80},{192,256},{208... | collective-permute-start | bytes 1769480 | tf_op jit(solution)/shard_map/ppermute | solution.py:377
  68.7 0.0 collective-permute-done.5.b_ref
  68.7 0.4 merge_far.1
  69.1 13.3 %all_gather.47 = bf16[12,160,128]{2,1,0:T(8,128)(2,1)S(1)} all-gather(bf16[3,160,128]{2,1,0:T(8,128)(2,1)S(1)} %bitcast.25), channel_id=1, replica_groups=mesh['y'=8,'zh'=2,'c'=2,'row'=4,'col'=4] {'col'}, dimensions={0}, use_global_device_ids=true | all-gather | bytes 614400 | tf_op jit(solution)/shard_map/all_gather | solution.py:407
  82.4 5.0 %all-gather.4 = bf16[24,160,128]{2,1,0:T(8,128)(2,1)S(1)} all-gather(bf16[12,160,128]{2,1,0:T(8,128)(2,1)S(1)} %all_gather.47), channel_id=6, replica_groups=mesh['y'=8,'zh'=2,'c'=2,'row'=4,'col'=4] {'c'}, dimensions={0}, use_global_device_ids=true | all-gather | bytes 1474560 | tf_op jit(solution)/shard_map/all_gather | solution.py:408
  87.4 0.0 collective-permute-done.6.w1_ref
  87.4 0.0 collective-permute-done.9.w4_ref
  87.4 0.0 collective-permute-done.8.w3_ref
  87.4 1.8 %project.1 = (f32[160,1536]{1,0:T(8,128)S(1)}, bf16[160,1536]{1,0:T(8,128)(2,1)S(1)}) custom-call(s32[3]{0:T(128)S(1)} %pad_add_fusion.idx_ref, bf16[2,12,160,128]{3,2,1,0:T(8,128)(2,1)S(1)} %bitcast.21, bf16[12,16,1536]{2,1,0:T(8,128)(2,1)S(1)} %get-tuple-element.44.w0_ref, bf16[12,16,1536]{2,1,0:T(8,128)(2,1)S(1)} %collective-permute-done.6.w1_ref, ...), custom_call_target="tpu_custom_call" | custom-call | tf_op jit(solution)/shard_map/project/pallas_call | solution.py:316
  89.1 2.5 %all-gather.5 = bf16[320,1536]{1,0:T(8,128)(2,1)S(1)} all-gather(bf16[160,1536]{1,0:T(8,128)(2,1)S(1)} %get-tuple-element.46), channel_id=7, replica_groups=mesh['y'=8,'zh'=2,'c'=2,'row'=4,'col'=4] {'c'}, dimensions={0}, use_global_device_ids=true | all-gather | bytes 1474560 | tf_op jit(solution)/shard_map/all_gather | solution.py:410
  91.7 1.5 %join.1 = bf16[160,1536]{1,0:T(8,128)(2,1)} custom-call(s32[3]{0:T(128)S(1)} %pad_add_fusion.idx_ref, f32[160,1536]{1,0:T(8,128)S(1)} %get-tuple-element.45.keep_ref, bf16[2,160,1536]{2,1,0:T(8,128)(2,1)S(1)} %bitcast.20), custom_call_target="tpu_custom_call" | custom-call | tf_op jit(solution)/shard_map/join/pallas_call | solution.py:334
  93.2 0.0 copy-start
  93.2 4.1 %all-to-all-start = ((bf16[4,40,1536]{2,1,0:T(8,128)(2,1)}), bf16[4,40,1536]{2,1,0:T(8,128)(2,1)S(1)}, u32[]{:S(2)}, u32[]{:S(2)}) async-start(bf16[4,40,1536]{2,1,0:T(8,128)(2,1)} %bitcast.16), calls=%async_computation | async-start | bytes 983040 | tf_op jit(solution)/shard_map/all_to_all | solution.py:413
  97.3 0.0 copy-done
  97.4 8.5 %all-to-all-done.pieces_ref = bf16[4,40,1536]{2,1,0:T(8,128)(2,1)S(1)} async-done(((bf16[4,40,1536]{2,1,0:T(8,128)(2,1)}), bf16[4,40,1536]{2,1,0:T(8,128)(2,1)S(1)}, u32[]{:S(2)}, u32[]{:S(2)}) %all-to-all-start) | async-done | bytes 491552 | tf_op jit(solution)/shard_map/all_to_all | solution.py:413
  105.9 0.7 finish.1
  (3 shorter events, 0.0 us)
Async XLA Ops:
  9.7 18.2 %collective-permute-start = (bf16[2,2,3,160,128]{4,3,2,1,0:T(8,128)(2,1)S(1)}, bf16[2,2,3,160,128]{4,3,2,1,0:T(8,128)(2,1)S(1)}, u32[]{:S(2)}, u32[]{:S(2)}) collective-permute-start(bf16[2,2,3,160,128]{4,3,2,1,0:T(8,128)(2,1)S(1)} %bitcast.26), channel_id=1, source_target_pairs={{0,128},{16,400},{64,192},{80,464},{128,256},{144,16},{192,320},{2... | collective-permute-start | bytes 1474568 | tf_op jit(solution)/shard_map/ppermute | solution.py:377
  13.3 21.0 %collective-permute-start.1 = (bf16[1056,128]{1,0:T(8,128)(2,1)}, bf16[1056,128]{1,0:T(8,128)(2,1)S(1)}, u32[]{:S(2)}, u32[]{:S(2)}) collective-permute-start(bf16[1056,128]{1,0:T(8,128)(2,1)} %pack.1), channel_id=1, source_target_pairs={{0,32},{32,0},{1,33},{33,1},{2,34},{34,2},{3,35},{35,3},{4,36},{36... | collective-permute-start | bytes 811016 | tf_op jit(solution)/shard_map/ppermute | solution.py:388
  22.5 15.3 %collective-permute-start.4 = (bf16[2,2,3,160,128]{4,3,2,1,0:T(8,128)(2,1)S(1)}, bf16[2,2,3,160,128]{4,3,2,1,0:T(8,128)(2,1)S(1)}, u32[]{:S(2)}, u32[]{:S(2)}) collective-permute-start(bf16[2,2,3,160,128]{4,3,2,1,0:T(8,128)(2,1)S(1)} %bitcast.27), channel_id=1, source_target_pairs={{0,64},{16,464},{64,128},{80,16},{128,192},{144,80},{192,256},{208... | collective-permute-start | bytes 1474568 | tf_op jit(solution)/shard_map/ppermute | solution.py:377
  27.9 19.3 %collective-permute-start.2 = (bf16[2,2,3,160,128]{4,3,2,1,0:T(8,128)(2,1)S(1)}, bf16[2,2,3,160,128]{4,3,2,1,0:T(8,128)(2,1)S(1)}, u32[]{:S(2)}, u32[]{:S(2)}) collective-permute-start(bf16[2,2,3,160,128]{4,3,2,1,0:T(8,128)(2,1)S(1)} %collective-permute-done.b2_ref), channel_id=1, source_target_pairs={{0,64},{16,464},{64,128},{80,16},{128,192},{144,80},{192,256},{208... | collective-permute-start | bytes 1474568 | tf_op jit(solution)/shard_map/ppermute | solution.py:377
  31.0 16.2 %collective-permute-start.3 = (bf16[2,3,160,128]{3,2,1,0:T(8,128)(2,1)S(1)}, bf16[2,3,160,128]{3,2,1,0:T(8,128)(2,1)S(1)}, u32[]{:S(2)}, u32[]{:S(2)}) collective-permute-start(bf16[2,3,160,128]{3,2,1,0:T(8,128)(2,1)S(1)} %dynamic-slice_bitcast_fusion), channel_id=1, source_target_pairs={{0,128},{16,400},{64,192},{80,464},{128,256},{144,16},{192,320},{2... | collective-permute-start | bytes 737288 | tf_op jit(solution)/shard_map/ppermute | solution.py:377
  42.2 22.0 %collective-permute-start.7 = (bf16[12,16,1536]{2,1,0:T(8,128)(2,1)S(1)}, bf16[12,16,1536]{2,1,0:T(8,128)(2,1)S(1)}, u32[]{:S(2)}, u32[]{:S(2)}) collective-permute-start(bf16[12,16,1536]{2,1,0:T(8,128)(2,1)S(1)} %get-tuple-element.44.w0_ref), channel_id=1, source_target_pairs={{0,128},{16,400},{64,192},{80,464},{128,256},{144,16},{192,320},{2... | collective-permute-start | bytes 1769480 | tf_op jit(solution)/shard_map/ppermute | solution.py:377
  53.8 14.9 %collective-permute-start.5 = (bf16[512,128]{1,0:T(8,128)(2,1)S(1)}, bf16[512,128]{1,0:T(8,128)(2,1)S(1)}, u32[]{:S(2)}, u32[]{:S(2)}) collective-permute-start(bf16[512,128]{1,0:T(8,128)(2,1)S(1)} %get-tuple-element.43), channel_id=1, source_target_pairs={{0,32},{32,0},{1,33},{33,1},{2,34},{34,2},{3,35},{35,3},{4,36},{36... | collective-permute-start | bytes 393224 | tf_op jit(solution)/shard_map/ppermute | solution.py:402
  59.3 28.1 %collective-permute-start.6 = (bf16[12,16,1536]{2,1,0:T(8,128)(2,1)S(1)}, bf16[12,16,1536]{2,1,0:T(8,128)(2,1)S(1)}, u32[]{:S(2)}, u32[]{:S(2)}) collective-permute-start(bf16[12,16,1536]{2,1,0:T(8,128)(2,1)S(1)} %get-tuple-element.44.w0_ref), channel_id=1, source_target_pairs={{0,64},{16,464},{64,128},{80,16},{128,192},{144,80},{192,256},{208... | collective-permute-start | bytes 1769480 | tf_op jit(solution)/shard_map/ppermute | solution.py:377
  64.2 23.2 %collective-permute-start.9 = (bf16[6,16,1536]{2,1,0:T(8,128)(2,1)S(1)}, bf16[6,16,1536]{2,1,0:T(8,128)(2,1)S(1)}, u32[]{:S(2)}, u32[]{:S(2)}) collective-permute-start(bf16[6,16,1536]{2,1,0:T(8,128)(2,1)S(1)} %slice.4), channel_id=1, source_target_pairs={{0,128},{16,400},{64,192},{80,464},{128,256},{144,16},{192,320},{2... | collective-permute-start | bytes 884744 | tf_op jit(solution)/shard_map/ppermute | solution.py:377
  66.5 20.9 %collective-permute-start.8 = (bf16[12,16,1536]{2,1,0:T(8,128)(2,1)S(1)}, bf16[12,16,1536]{2,1,0:T(8,128)(2,1)S(1)}, u32[]{:S(2)}, u32[]{:S(2)}) collective-permute-start(bf16[12,16,1536]{2,1,0:T(8,128)(2,1)S(1)} %collective-permute-done.7.w2_ref), channel_id=1, source_target_pairs={{0,64},{16,464},{64,128},{80,16},{128,192},{144,80},{192,256},{208... | collective-permute-start | bytes 1769480 | tf_op jit(solution)/shard_map/ppermute | solution.py:377
  93.2 4.1 %copy-start = (f32[1536]{0:T(1024)S(1)}, f32[1536]{0:T(1024)}, u32[]{:S(2)}) copy-start(f32[1536]{0:T(1024)} %param.9) | copy-start | bytes 18436
  93.2 12.7 %all-to-all-start = ((bf16[4,40,1536]{2,1,0:T(8,128)(2,1)}), bf16[4,40,1536]{2,1,0:T(8,128)(2,1)S(1)}, u32[]{:S(2)}, u32[]{:S(2)}) async-start(bf16[4,40,1536]{2,1,0:T(8,128)(2,1)} %bitcast.16), calls=%async_computation | async-start | bytes 983040 | tf_op jit(solution)/shard_map/all_to_all | solution.py:413
